TPU v7x, 1024 devices: a whole 4x8x16 slice. The times are simulated.
1024 devices in a mesh: dp: 128 (over z_lo, y, x), seq: 8 (over z_hi, core).
Axes of the slice: x: 4, y: 8, z: 16 (z_hi: 4, z_lo: 4; z = z_hi * 4 + z_lo), core: 2. Of those that a mesh axis runs over, the one named last changes fastest.
Arguments:
- qkv_input: bfloat16 [128, 1024, 7680], P('dp', 'seq'), may hold values from -24 to 24
- conv_weight: float32 [4, 7680], replicated, may hold values from -3 to 3
- out_cotangent: bfloat16 [128, 1024, 2560], P('dp', 'seq'), may hold values from -6 to 6
Outputs:
- input_grad: bfloat16 [128, 1024, 2560], P('dp', 'seq')
- weight_grad: float32 [4, 2560], P(None, 'dp')
All inputs are finite; a program needn't handle non-finite values.
Results may differ from a plain program's by a relative error of at most 0.019.
Values may be sent and summed in bfloat16 or wider, within the bound.
No kernel may reach another device: no remote copies, remote signals or barrier semaphores. Data moves between devices by JAX's collectives and lax.ppermute only.
A program may use at most 64 MiB of HBM per device.

v0:
```python
import jax
import jax.numpy as jnp
from jax import lax
from jax.sharding import PartitionSpec as P

HEAD = 128
BLOCK = 128


def shifted(array, axis, by):
    peers = lax.axis_size(axis)
    pairs = [(i, i + by) for i in range(peers) if 0 <= i + by < peers]
    return lax.ppermute(array, axis, pairs)


def carried_in(array, axis, combine, identity, reverse):
    peers, place = (lax.axis_size(axis), lax.axis_index(axis))
    everything = lax.all_gather(array.astype(jnp.bfloat16), axis)
    start = jnp.broadcast_to(jnp.asarray(identity, array.dtype), array.shape)

    def lap(k, before):
        at = peers - 1 - k if reverse else k
        reached = at > place if reverse else at < place
        new = combine(before, everything[at].astype(array.dtype))
        return jnp.where(reached, new, before)

    return lax.fori_loop(0, peers, lap, start)


def combine_sum(earlier_part, later_part):
    return earlier_part + later_part


def convolve_range(padded, conv_weight, lower, upper, length):
    taps = conv_weight.shape[0]
    total = conv_weight[0, lower:upper] * padded[taps - 1 : taps - 1 + length, lower:upper].astype(
        jnp.float32
    )
    for offset in range(1, taps):
        total = total + conv_weight[offset, lower:upper] * padded[
            taps - 1 - offset : taps - 1 - offset + length, lower:upper
        ].astype(jnp.float32)
    return total.astype(jnp.bfloat16)


def per_device(qkv_input, conv_weight, out_cotangent):
    sequence = qkv_input[0]
    length = sequence.shape[0]
    width_all = sequence.shape[1]
    channels = width_all // 3
    half = channels // 2
    half_heads = half // HEAD
    conv_taps = conv_weight.shape[0]
    incoming = shifted(sequence[length - (conv_taps - 1) :], "seq", 1)
    padded = jnp.concatenate([incoming, sequence], 0)
    blocks = length // BLOCK
    shape_four = (blocks, BLOCK, half_heads, HEAD)
    query_a = convolve_range(padded, conv_weight, 0, half, length).reshape(shape_four)
    rest = convolve_range(padded, conv_weight, 3 * half, 6 * half, length)
    key_b = rest[:, 0:half].reshape(shape_four)
    value_a = rest[:, half : 2 * half].reshape(shape_four)
    value_b = rest[:, 2 * half : 3 * half].reshape(shape_four)
    probe = out_cotangent[0]
    probe_a = probe[:, 0:half].reshape(shape_four)
    probe_b = probe[:, half : 2 * half].reshape(shape_four)
    states = jnp.einsum("bshd,bshe->bhde", key_b, value_b, preferred_element_type=jnp.float32)
    adjoints = jnp.einsum("bshd,bshe->bhde", query_a, probe_a, preferred_element_type=jnp.float32)
    local_states = jnp.sum(states, 0)
    local_adjoints = jnp.sum(adjoints, 0)
    zero_state = jnp.zeros_like(local_states)
    states_before = carried_in(local_states, "seq", combine_sum, zero_state, False)
    adjoints_after = carried_in(local_adjoints, "seq", combine_sum, zero_state, True)
    nothing = jnp.zeros_like(states)
    block_before = states_before[None] + jnp.concatenate([nothing, jnp.cumsum(states, 0)[:-1]], 0)
    block_after = adjoints_after[None] + jnp.concatenate(
        [jnp.cumsum(adjoints[::-1], 0)[::-1][1:], nothing], 0
    )
    before_half = block_before.astype(jnp.bfloat16)
    after_half = block_after.astype(jnp.bfloat16)
    causal = jnp.tril(jnp.ones((BLOCK, BLOCK), jnp.bool_))
    scores_b = jnp.where(
        causal,
        jnp.einsum("bthd,bshd->bhts", probe_b, value_b, preferred_element_type=jnp.float32) / HEAD,
        0.0,
    ).astype(jnp.bfloat16)
    scores_a = jnp.where(
        causal,
        jnp.einsum("bthd,bshd->bhts", probe_a, value_a, preferred_element_type=jnp.float32) / HEAD,
        0.0,
    ).astype(jnp.bfloat16)
    query_grad = (
        jnp.einsum("bhts,bshd->bthd", scores_b, key_b, preferred_element_type=jnp.float32)
        + jnp.einsum("bthe,bhde->bthd", probe_b, before_half, preferred_element_type=jnp.float32)
        / HEAD
    )
    key_grad = (
        jnp.einsum("bhts,bthd->bshd", scores_a, query_a, preferred_element_type=jnp.float32)
        + jnp.einsum("bshe,bhde->bshd", value_a, after_half, preferred_element_type=jnp.float32)
        / HEAD
    )
    kept_grads = jnp.concatenate(
        [query_grad.reshape(length, half), key_grad.reshape(length, half)], 1
    )
    arriving = shifted(kept_grads[: conv_taps - 1], "seq", -1)
    extended = jnp.concatenate([kept_grads, arriving], 0)
    kept_weight = conv_weight[:, half : 3 * half]
    input_grad = kept_weight[0] * extended[0:length]
    for offset in range(1, conv_taps):
        input_grad = input_grad + kept_weight[offset] * extended[offset : offset + length]
    weight_terms = jnp.stack(
        [
            jnp.sum(
                kept_grads
                * padded[
                    conv_taps - 1 - offset : conv_taps - 1 - offset + length, half : 3 * half
                ].astype(jnp.float32),
                0,
            )
            for offset in range(conv_taps)
        ],
        0,
    )
    seq_total = lax.psum(weight_terms.astype(jnp.bfloat16), "seq").astype(jnp.float32)
    shares = lax.psum_scatter(seq_total, "dp", scatter_dimension=1, tiled=True)
    return (input_grad.astype(jnp.bfloat16)[None], shares / lax.axis_size("dp"))


def solution(mesh):
    in_specs = (P("dp", "seq", None), P(), P("dp", "seq", None))
    out_specs = (P("dp", "seq", None), P(None, "dp"))
    return jax.shard_map(
        per_device, mesh=mesh, in_specs=in_specs, out_specs=out_specs, check_vma=False
    )
```

profile of v0, /device:TPU:256, one launch (start us, length us, event | category | flops | bytes accessed | tf_op | source)
XLA Modules:
  0.0 989.9 jit_solution(9747735599715455412)
XLA Ops:
  7.2 0.0 all-gather.5.cloned.1.call-start
  7.2 0.9 slice_bitcast_fusion
  8.2 1.9 collective-permute-start
  10.1 1.3 slice_reduce_fusion.3
  11.3 2.8 copy.22
  14.2 3.4 collective-permute-done
  17.6 1.8 copy.23
  19.4 6.1 add_convert_fusion
  25.5 0.0 copy-start.5
  25.5 0.8 fusion.32
  26.3 0.7 copy-done.4
  27.0 1.1 convolution_convert_fusion.1
  28.1 0.0 all-gather.5.cloned.1.call-update
  28.1 0.0 all-gather.7.cloned.1.call-start
  28.2 2.2 copy.24
  30.4 0.0 copy-done.5
  30.4 0.1 slice_reduce_fusion.11
  30.4 1.9 fusion.33
  32.3 0.0 copy-done.3
  32.3 2.5 add_convert_fusion.1
  34.8 0.0 copy-start.1
  34.8 0.0 copy-done.2
  34.8 1.1 convolution_convert_fusion
  35.9 0.0 all-gather.7.cloned.1.call-update
  36.0 0.0 copy-done.1
  36.0 70.5 %all-gather.5.cloned.1.call-done = bf16[80,128,128]{2,1,0:T(8,128)(2,1)} async-done(((bf16[10,128,128]{2,1,0:T(8,128)(2,1)}), bf16[80,128,128]{2,1,0:T(8,128)(2,1)}) %all-gather.5.cloned.1.call-update) | async-done | bytes 2621456 | tf_op jit(solution)/shard_map/all_gather | solution.py:18
  106.5 10.8 %while.30 = (s32[]{:T(128)}, f32[10,128,128]{2,1,0:T(8,128)S(1)}, s32[]{:T(128)}, bf16[8,10,128,128]{3,2,1,0:T(8,128)(2,1)}, s32[]{:T(128)}, /*index=5*/s32[]{:T(128)}) while((s32[]{:T(128)}, f32[10,128,128]{2,1,0:T(8,128)S(1)}, s32[]{:T(128)}, bf16[8,10,128,128]{3,2,1,0:T(8,128)(2,1)}, s32[]{:T(128)}, /*index=5*/s32[]{:T(128)}) %tuple.100), condition=%wide.region_1.0_spmd.clone, body=%wide.region_0.0_spmd.clone.sunk | while | flops 655364 | bytes 1638493 | solution.py:27
  106.5 1.3 add_select_fusion.4
  107.8 1.3 add_select_fusion.4
  109.2 1.3 add_select_fusion.4
  110.5 1.3 add_select_fusion.4
  111.9 1.3 add_select_fusion.4
  113.2 1.3 add_select_fusion.4
  114.5 1.3 add_select_fusion.4
  115.9 1.3 add_select_fusion.4
  117.2 63.3 %all-gather.7.cloned.1.call-done = bf16[80,128,128]{2,1,0:T(8,128)(2,1)} async-done(((bf16[10,128,128]{2,1,0:T(8,128)(2,1)}), bf16[80,128,128]{2,1,0:T(8,128)(2,1)}) %all-gather.7.cloned.1.call-update) | async-done | bytes 2621456 | tf_op jit(solution)/shard_map/all_gather | solution.py:18
  180.5 10.8 %while.31 = (s32[]{:T(128)}, f32[10,128,128]{2,1,0:T(8,128)S(1)}, s32[]{:T(128)}, bf16[8,10,128,128]{3,2,1,0:T(8,128)(2,1)}, s32[]{:T(128)}, /*index=5*/s32[]{:T(128)}, s32[]{:T(128)}, s32[]{:T(128)}) while((s32[]{:T(128)}, f32[10,128,128]{2,1,0:T(8,128)S(1)}, s32[]{:T(128)}, bf16[8,10,128,128]{3,2,1,0:T(8,128)(2,1)}, s32[]{:T(128)}, ...), condition=%wide.region_3.4_spmd.clone, body=%wide.region_2.3_spmd.clone.sunk | while | flops 655368 | bytes 1638555 | solution.py:27
  180.5 1.3 add_select_fusion.5
  181.8 1.3 add_select_fusion.5
  183.2 1.3 add_select_fusion.5
  184.5 1.3 add_select_fusion.5
  185.9 1.3 add_select_fusion.5
  187.3 1.3 add_select_fusion.5
  188.6 1.3 add_select_fusion.5
  190.0 1.3 add_select_fusion.5
  191.3 2.0 convolution_multiply_fusion.2
  193.3 1.8 convolution_add_fusion.1
  195.2 2.1 convolution_multiply_fusion
  197.2 1.9 convolution_add_fusion
  199.2 1.2 fusion
  200.3 1.7 copy.35
  202.0 4.5 collective-permute-start.1
  206.5 0.1 slice_reduce_fusion.7
  206.6 1.3 dynamic-slice
  208.5 0.0 collective-permute-done.1
  208.6 1.5 copy.36
  210.1 1.6 pad_maximum_fusion
  211.7 0.3 copy-done
  212.0 6.6 multiply_reduce_fusion.2
  218.6 0.1 pad_maximum_fusion.3
  218.7 39.5 %psum.7 = bf16[4,2560]{1,0:T(4,128)(2,1)S(1)} all-reduce(bf16[4,2560]{1,0:T(4,128)(2,1)S(1)} %pad_maximum_fusion.3), channel_id=1, replica_groups=mesh['dp'=128,'seq'=8] {'seq'}, use_global_device_ids=true, to_apply=%region_8.9 | all-reduce | flops 10240 | bytes 40960 | tf_op jit(solution)/shard_map/psum | solution.py:123
  258.1 722.1 %all-reduce = f32[4,2560]{1,0:T(4,128)S(1)} all-reduce(bf16[4,2560]{1,0:T(4,128)(2,1)S(1)} %psum.7), channel_id=4, replica_groups=mesh['dp'=128,'seq'=8] {'dp'}, use_global_device_ids=true, to_apply=%region_9.10.clone | all-reduce | flops 10240 | bytes 61440
  980.2 2.2 copy.37
  982.4 0.7 dynamic-slice_multiply_fusion
  (11 shorter events, 0.1 us)
Async XLA Ops:
  7.2 99.3 %all-gather.5.cloned.1.call-start = ((), (), s32[]{:S(2)}) async-start(), calls=%async_computation | async-start | bytes 2949120 | tf_op jit(solution)/shard_map/all_gather | solution.py:18
  8.2 9.4 collective-permute-start
  25.5 4.9 copy-start.5
  26.3 0.7 copy-start.4
  26.3 6.0 copy-start.3
  28.1 152.3 %all-gather.7.cloned.1.call-start = ((), (), s32[]{:S(2)}) async-start(), calls=%async_computation.1 | async-start | bytes 2949120 | tf_op jit(solution)/shard_map/all_gather | solution.py:18
  32.3 2.5 copy-start.2
  34.8 1.1 copy-start.1
  202.0 6.5 collective-permute-start.1
  210.1 1.9 copy-start
Sparse Core Ops, SparseCore 0:
  28.3 78.1 all-gather.4
  109.7 70.6 all-gather.6
where the time goes:
time: 991 us; the launch traced here: 990 us
  blocking collectives  762 us (77%)
  waiting for transfers between devices  137 us (14%)
  other arithmetic  39.9 us (4%)
  local copies, waits for them, and re-layouts  19.5 us (2%)
  between operations  14.9 us (2%)
  matrix products  10.1 us (1%)
    unnamed x1, blocking collectives  722 us
    all_gather x2, waiting for transfers between devices, carried_in(): everything = lax.all_gather(array.astype(jnp.bfloat16), axis)  134 us
    psum x1, blocking collectives, per_device(): lax.psum(weight_terms.astype(jnp.bfloat16), 'seq').astype(jnp.float32)  39.5 us
    select_n x16, other arithmetic, lap(): return jnp.where(reached, new, before)  21.2 us
  transfers between devices with their start and end apart: 4, of which 3 were waited for; matrix products, arithmetic and copies ran while one was open for 2% of the time, Pallas kernels for 0%

commit v1 on v0

v1 whole, which is shorter than its diff:
```python
import jax
import jax.numpy as jnp
from jax import lax
from jax.experimental import pallas as pl
from jax.experimental.pallas import tpu as pltpu
from jax.sharding import Mesh
from jax.sharding import PartitionSpec as P

HEAD = 128
TAPS = 4
ROWS = 128
PAIR = 2 * ROWS
EXT = PAIR + 16
PRE = 8
F32 = jnp.float32
BF16 = jnp.bfloat16
QA, QB, KA, KB, VA, VB, GA, GB = range(8)
VMEM = pl.BlockSpec(memory_space=pltpu.VMEM)
SMEM = pl.BlockSpec(memory_space=pltpu.SMEM)


def call(kernel, shapes, scratch, scalars, *arrays):
    return pl.pallas_call(
        kernel,
        out_shape=[jax.ShapeDtypeStruct(s, t) for s, t in shapes],
        in_specs=[SMEM] + [VMEM] * len(arrays),
        out_specs=[VMEM] * len(shapes),
        scratch_shapes=scratch,
        compiler_params=pltpu.CompilerParams(vmem_limit_bytes=32 * 1024 * 1024),
    )(scalars, *arrays)


def nt(a, b):
    return lax.dot_general(a, b, (((1,), (1,)), ((), ())), preferred_element_type=F32)


def tn(a, b):
    return lax.dot_general(a, b, (((0,), (0,)), ((), ())), preferred_element_type=F32)


def nn(a, b):
    return lax.dot_general(a, b, (((1,), (0,)), ((), ())), preferred_element_type=F32)


def own_columns(x_ref, g_ref, group, half, width):
    ref, at = (x_ref, group) if group < GA else (g_ref, group - GA)
    return ref, pl.ds(pl.multiple_of((2 * at + half) * width, HEAD), width)


def pack_kernel(scalars, x_ref, g_ref, send_ref, same_ref, cross_ref):
    core = scalars[0]
    width = same_ref.shape[1]
    edge = pl.ds(pl.multiple_of(core * (ROWS - 16), 16), 16)
    for half, out_ref in ((core, same_ref), (1 - core, cross_ref)):
        pieces = []
        for group in range(8):
            ref, lanes = own_columns(x_ref, g_ref, group, half, width)
            rows = ref[edge, lanes].astype(F32)
            pieces.append(jnp.where(core == 1, rows[12:16], rows[0:4]))
        out_ref[...] = jnp.concatenate(pieces, 0).astype(BF16)
    for group in range(8):
        ref, lanes = own_columns(x_ref, g_ref, group, 1 - core, width)
        send_ref[:, group * width : (group + 1) * width] = ref[:, lanes]


def edges(core, same_ref, cross_ref):
    same, cross = same_ref[...].astype(F32), cross_ref[...].astype(F32)
    return jnp.where(core == 1, same, cross), jnp.where(core == 1, cross, same)


def gather_rows(core, x_ref, g_ref, received_ref, group, head, padded_ref):
    width = received_ref.shape[1] // 8
    half_at = core * width + head * HEAD
    ref, at = (x_ref, group) if group < GA else (g_ref, group - GA)
    lanes = pl.ds(pl.multiple_of(2 * at * width + half_at, HEAD), HEAD)
    own = ref[:, lanes].astype(F32)
    other = received_ref[:, group * width + head * HEAD : group * width + (head + 1) * HEAD]
    padded_ref[pl.ds(pl.multiple_of(PRE + core * ROWS, 8), ROWS), :] = own
    padded_ref[pl.ds(pl.multiple_of(PRE + (1 - core) * ROWS, 8), ROWS), :] = other.astype(F32)


def fill_edges(before, after, group, head, padded_ref):
    lanes = slice(head * HEAD, (head + 1) * HEAD)
    none = jnp.zeros((4, HEAD), F32)
    rows = slice(4 * group, 4 * group + 4)
    padded_ref[0:PRE, :] = jnp.concatenate([none, before[rows, lanes]], 0)
    padded_ref[PRE + PAIR : PRE + PAIR + 8, :] = jnp.concatenate([after[rows, lanes], none], 0)


def convolve(padded_ref, w_ref, core, width, group, head, out_ref):
    lanes = pl.ds(pl.multiple_of((2 * group + core) * width + head * HEAD, HEAD), HEAD)
    taps = w_ref[:, lanes]
    at = slice(head * HEAD, (head + 1) * HEAD)
    for first, count in ((0, ROWS), (ROWS, ROWS), (PAIR, 8)):
        start = PRE + first
        total = taps[0:1] * padded_ref[start : start + count, :]
        for j in range(1, TAPS):
            total = total + taps[j : j + 1] * padded_ref[start - j : start - j + count, :]
        if first == PAIR:
            total = jnp.concatenate([total, jnp.zeros((8, HEAD), F32)], 0)
            count = 16
        out_ref[first : first + count, at] = total.astype(BF16)


def copy_rows(padded_ref, head, out_ref):
    at = slice(head * HEAD, (head + 1) * HEAD)
    out_ref[0:PAIR, at] = padded_ref[PRE : PRE + PAIR, :].astype(BF16)
    tail = padded_ref[PRE + PAIR : PRE + PAIR + 8, :]
    out_ref[PAIR:EXT, at] = jnp.concatenate([tail, jnp.zeros((8, HEAD), F32)], 0).astype(BF16)


def states_kernel(
    scalars, x_ref, g_ref, received_ref, same_ref, cross_ref, w_ref,
    up_ref, down_ref, far_ref, qa_ref, kb_ref, vb_ref, ga_ref, *padded_refs,
):
    core, chip = scalars[0], scalars[1]
    width = received_ref.shape[1] // 8
    before, after = edges(core, same_ref, cross_ref)
    turn = 0
    for head in range(width // HEAD):
        for group, out_ref in ((KB, kb_ref), (VB, vb_ref), (QA, qa_ref), (GA, ga_ref)):
            padded_ref = padded_refs[turn % len(padded_refs)]
            turn += 1
            gather_rows(core, x_ref, g_ref, received_ref, group, head, padded_ref)
            fill_edges(before, after, group, head, padded_ref)
            if group == GA:
                copy_rows(padded_ref, head, out_ref)
            else:
                convolve(padded_ref, w_ref, core, width, group, head, out_ref)
        at = slice(head * HEAD, (head + 1) * HEAD)
        state = tn(kb_ref[0:PAIR, at], vb_ref[0:PAIR, at]).astype(BF16)
        adjoint = tn(qa_ref[0:PAIR, at], ga_ref[0:PAIR, at]).astype(BF16)
        up_ref[head] = jnp.where(chip == 3, adjoint, state)
        down_ref[head] = jnp.where(chip == 0, state, adjoint)
        far_ref[head] = jnp.where(chip < 2, state, adjoint)


def inside_kernel(
    scalars, x_ref, g_ref, received_ref, same_ref, cross_ref, w_ref,
    qa_ref, kb_ref, vb_ref, ga_ref,
    kept_ref, va_ref, gb_ref, raw_ref, *padded_refs,
):
    core = scalars[0]
    width = received_ref.shape[1] // 8
    before, after = edges(core, same_ref, cross_ref)
    row = lax.broadcasted_iota(jnp.int32, (EXT, EXT), 0)
    column = lax.broadcasted_iota(jnp.int32, (EXT, EXT), 1)
    causal = jnp.where(column <= row, 1.0 / HEAD, 0.0)
    reverse = jnp.where(
        (column >= row) & (column < PAIR),
        1.0 / HEAD,
        jnp.where((column >= PAIR) & (column < row), -1.0 / HEAD, 0.0),
    )
    turn = 0
    for head in range(width // HEAD):
        at = slice(head * HEAD, (head + 1) * HEAD)
        for group in (VA, GB, QB, KA):
            padded_ref = padded_refs[turn % len(padded_refs)]
            turn += 1
            gather_rows(core, x_ref, g_ref, received_ref, group, head, padded_ref)
            fill_edges(before, after, group, head, padded_ref)
            if group == VA:
                convolve(padded_ref, w_ref, core, width, group, head, va_ref)
            elif group == GB:
                copy_rows(padded_ref, head, gb_ref)
            else:
                to = slice((group - QB) * width + head * HEAD, (group - QB) * width + (head + 1) * HEAD)
                raw_ref[:, to] = padded_ref[...]
        scores = (nt(gb_ref[:, at], vb_ref[:, at]) * causal).astype(BF16)
        kept_ref[:, at] = nn(scores, kb_ref[:, at])
        scores = (nt(va_ref[:, at], ga_ref[:, at]) * reverse).astype(BF16)
        kept_ref[:, width + head * HEAD : width + (head + 1) * HEAD] = nn(scores, qa_ref[:, at])


def gradients_kernel(
    scalars, kept_ref, va_ref, gb_ref, raw_ref, up_ref, down_ref, far_ref, w_ref,
    own_ref, send_ref, terms_ref, total_ref, grad_ref,
):
    core, chip = scalars[0], scalars[1]
    width = va_ref.shape[1]
    for head in range(width // HEAD):
        up, down, far = (r[head].astype(F32) for r in (up_ref, down_ref, far_ref))
        none = jnp.zeros_like(up)
        earlier = (
            jnp.where(chip >= 1, up, none) + jnp.where(chip >= 2, far, none)
            + jnp.where(chip == 3, down, none)
        ).astype(BF16)
        later = (
            jnp.where(chip <= 2, down, none) + jnp.where(chip <= 1, far, none)
            + jnp.where(chip == 0, up, none)
        ).astype(BF16)
        at = slice(head * HEAD, (head + 1) * HEAD)
        for part, left_ref, right in ((0, gb_ref, earlier), (1, va_ref, later)):
            to = slice(part * width + head * HEAD, part * width + (head + 1) * HEAD)
            total_ref[:, :] = kept_ref[:, to] + nt(left_ref[:, at], right) * (1.0 / HEAD)
            group = QB + part
            lanes = pl.ds(pl.multiple_of((2 * group + core) * width + head * HEAD, HEAD), HEAD)
            taps = w_ref[:, lanes]
            sums = [jnp.zeros((8, HEAD), F32)] * TAPS
            for first in range(0, PAIR, 64):
                grad = taps[0:1] * total_ref[first : first + 64, :]
                for j in range(1, TAPS):
                    grad = grad + taps[j : j + 1] * total_ref[first + j : first + j + 64, :]
                grad_ref[first : first + 64, to] = grad.astype(BF16)
                kept = total_ref[first : first + 64, :]
                for j in range(TAPS):
                    start = PRE + first - j
                    term = kept * raw_ref[start : start + 64, to]
                    sums[j] = sums[j] + jnp.sum(term.reshape(8, 8, HEAD), 0)
            terms_ref[:, to] = jnp.concatenate(
                [jnp.sum(s, 0, keepdims=True) for s in sums], 0
            )
    own_ref[...] = grad_ref[pl.ds(pl.multiple_of(core * ROWS, ROWS), ROWS), :]
    send_ref[...] = grad_ref[pl.ds(pl.multiple_of((1 - core) * ROWS, ROWS), ROWS), :]


def per_device(qkv_input, conv_weight, out_cotangent):
    x, g = qkv_input[0], out_cotangent[0]
    half = g.shape[1] // 2
    width = half // 2
    heads = width // HEAD
    chips = lax.axis_size("zh")
    core, chip, low = lax.axis_index("core"), lax.axis_index("zh"), lax.axis_index("zl")
    scalars = jnp.stack([core, chip]).astype(jnp.int32)
    swap = [(0, 1), (1, 0)]
    line = (("zh", "core"))

    def place(c, k):
        return 2 * c + k

    to_same = [(place(c, 1), place(c + 1, 1)) for c in range(chips - 1)]
    to_same += [(place(c + 1, 0), place(c, 0)) for c in range(chips - 1)]
    to_cross = [(place(c, 1), place(c + 1, 0)) for c in range(chips - 1)]
    to_cross += [(place(c + 1, 0), place(c, 1)) for c in range(chips - 1)]

    send, same, cross = call(
        pack_kernel,
        [((ROWS, 8 * width), BF16), ((32, width), BF16), ((32, width), BF16)],
        [], scalars, x, g,
    )
    received = lax.ppermute(send, "core", swap)
    same = lax.ppermute(same, line, to_same)
    cross = lax.ppermute(cross, line, to_cross)

    block = ((heads, HEAD, HEAD), BF16)
    long = ((EXT, width), BF16)
    padded = [pltpu.VMEM((PRE + PAIR + 8, HEAD), F32)] * 4
    up, down, far, qa, kb, vb, ga = call(
        states_kernel, [block] * 3 + [long] * 4, padded,
        scalars, x, g, received, same, cross, conv_weight,
    )
    far = lax.ppermute(far, "zh", [(c, (c + 2) % chips) for c in range(chips)])
    up = lax.ppermute(up, "zh", [(c, (c + 1) % chips) for c in range(chips)])
    down = lax.ppermute(down, "zh", [(c, (c - 1) % chips) for c in range(chips)])

    kept, va, gb, raw = call(
        inside_kernel,
        [((EXT, half), F32), long, long, ((PRE + PAIR + 8, half), F32)], padded,
        scalars, x, g, received, same, cross, conv_weight, qa, kb, vb, ga,
    )
    own, sent, terms = call(
        gradients_kernel,
        [((ROWS, half), BF16), ((ROWS, half), BF16), ((TAPS, half), F32)],
        [pltpu.VMEM((EXT, HEAD), F32), pltpu.VMEM((PAIR, half), BF16)],
        scalars, kept, va, gb, raw, up, down, far, conv_weight,
    )
    other = lax.ppermute(sent, "core", swap)

    spread = lax.axis_size("yx")
    few = width // spread
    rows = terms.reshape(TAPS, 2, spread, few).transpose(2, 1, 0, 3).reshape(spread, 2 * TAPS * few)
    summed = jnp.sum(lax.all_to_all(rows, "yx", 0, 0, tiled=True), 0).reshape(2, TAPS * few)
    along = 2 * chips
    rows = jnp.repeat(summed, 2 * along, axis=0)
    rows = lax.all_to_all(rows, ("zl", "zh", "core"), 0, 0, tiled=True)
    fitting = (jnp.arange(4 * along) % 2 == low % 2)[:, None]
    share = jnp.sum(jnp.where(fitting, rows, 0.0), 0).reshape(TAPS, few)
    shares = share / (lax.axis_size("zl") * spread)

    first, second = jnp.where(core == 0, own, other), jnp.where(core == 0, other, own)
    grad = jnp.concatenate(
        [first[:, :width], second[:, :width], first[:, width:], second[:, width:]], 1
    )
    return grad[None], shares


def solution(mesh):
    dp, seq = mesh.shape["dp"], mesh.shape["seq"]
    fine = Mesh(mesh.devices.reshape(4, dp // 4, seq // 2, 2), ("zl", "yx", "zh", "core"))
    rows = P(("zl", "yx"), ("zh", "core"), None)
    return jax.shard_map(
        per_device, mesh=fine, in_specs=(rows, P(), rows),
        out_specs=(rows, P(None, ("zl", "yx"))), check_vma=False,
    )
```

time: 991 us -> 121 us (0.12)
  the two profiles are of different devices: /device:TPU:256 before, /device:TPU:1 now
where the time goes in v1:
time: 121 us; the launch traced here: 120 us
  starting transfers between devices  67.4 us (56%)
  waiting for transfers between devices  38.3 us (32%)
  Pallas kernels  7.31 us (6%)
  local copies, waits for them, and re-layouts  5.08 us (4%)
    ppermute x1, starting transfers between devices, per_device(): received = lax.ppermute(send, 'core', swap)  16.1 us
    all_to_all x1, starting transfers between devices, per_device(): rows = lax.all_to_all(rows, ('zl', 'zh', 'core'), 0, 0, tiled=True)  15.7 us
    ppermute x1, waiting for transfers between devices, per_device(): far = lax.ppermute(far, 'zh', [(c, (c + 2) % chips) for c in range(chips)])  11.5 us
    ppermute x1, starting transfers between devices, per_device(): far = lax.ppermute(far, 'zh', [(c, (c + 2) % chips) for c in range(chips)])  10.2 us
    all_to_all x1, waiting for transfers between devices, per_device(): rows = lax.all_to_all(rows, ('zl', 'zh', 'core'), 0, 0, tiled=True)  9.42 us
    all_to_all x1, waiting for transfers between devices, per_device(): lax.all_to_all(rows, 'yx', 0, 0, tiled=True)  8.68 us
    ppermute x1, starting transfers between devices, per_device(): cross = lax.ppermute(cross, line, to_cross)  8.08 us
    pallas_call x4, Pallas kernels, call(): pl.pallas_call(kernel, out_shape=[jax.ShapeDtypeStruct(s, t) for s, t in...  7.31 us
  transfers between devices with their start and end apart: 9, of which 5 were waited for; matrix products, arithmetic and copies ran while one was open for 1% of the time, Pallas kernels for 2%

profile of v1, /device:TPU:1, one launch (start us, length us, event | category | flops | bytes accessed | tf_op | source)
XLA Modules:
  0.0 120.1 jit_solution(5257644098265039581)
XLA Ops:
  0.6 0.1 pad_add_fusion.scalars
  0.7 0.0 copy-start
  0.7 1.5 %copy-done = bf16[1,128,7680]{2,1,0:T(8,128)(2,1)S(1)} copy-done((bf16[1,128,7680]{2,1,0:T(8,128)(2,1)S(1)}, bf16[1,128,7680]{2,1,0:T(8,128)(2,1)}, u32[]{:S(2)}) %copy-start) | copy-done | bytes 1966104
  2.3 0.0 copy-start.1
  2.3 1.1 copy-done.1
  3.3 0.0 copy-start.2
  3.3 0.7 shard_map.50
  4.0 16.1 %collective-permute-start = (bf16[128,5120]{1,0:T(8,128)(2,1)S(1)}, bf16[128,5120]{1,0:T(8,128)(2,1)S(1)}, u32[]{:S(2)}, u32[]{:S(2)}) collective-permute-start(bf16[128,5120]{1,0:T(8,128)(2,1)S(1)} %get-tuple-element.19), channel_id=1, source_target_pairs={{0,1},{1,0},{2,3},{3,2},{4,5},{5,4},{6,7},{7,6},{8,9},{9,8},{10,11... | collective-permute-start | bytes 3932168 | tf_op jit(solution)/shard_map/ppermute | solution.py:241
  20.1 1.3 %collective-permute-start.1 = (bf16[32,640]{1,0:T(8,128)(2,1)S(1)}, bf16[32,640]{1,0:T(8,128)(2,1)S(1)}, u32[]{:S(2)}, u32[]{:S(2)}) collective-permute-start(bf16[32,640]{1,0:T(8,128)(2,1)S(1)} %get-tuple-element.20), channel_id=1, source_target_pairs={{1,3},{3,5},{5,7},{2,0},{4,2},{6,4},{9,11},{11,13},{13,15},{10,8},... | collective-permute-start | bytes 122888 | tf_op jit(solution)/shard_map/ppermute | solution.py:242
  21.4 8.1 %collective-permute-start.2 = (bf16[32,640]{1,0:T(8,128)(2,1)S(1)}, bf16[32,640]{1,0:T(8,128)(2,1)S(1)}, u32[]{:S(2)}, u32[]{:S(2)}) collective-permute-start(bf16[32,640]{1,0:T(8,128)(2,1)S(1)} %get-tuple-element.21), channel_id=1, source_target_pairs={{1,2},{3,4},{5,6},{2,1},{4,3},{6,5},{9,10},{11,12},{13,14},{10,9},... | collective-permute-start | bytes 122888 | tf_op jit(solution)/shard_map/ppermute | solution.py:243
  29.5 0.0 collective-permute-done.1.same_ref
  29.5 1.9 %collective-permute-done.2.cross_ref = bf16[32,640]{1,0:T(8,128)(2,1)S(1)} collective-permute-done((bf16[32,640]{1,0:T(8,128)(2,1)S(1)}, bf16[32,640]{1,0:T(8,128)(2,1)S(1)}, u32[]{:S(2)}, u32[]{:S(2)}) %collective-permute-start.2) | collective-permute-done | bytes 40992 | tf_op jit(solution)/shard_map/ppermute | solution.py:243
  31.4 0.0 collective-permute-done.received_ref
  31.4 0.0 copy-done.2
  31.4 1.8 %shard_map.51 = (bf16[5,128,128]{2,1,0:T(8,128)(2,1)S(1)}, bf16[5,128,128]{2,1,0:T(8,128)(2,1)S(1)}, bf16[5,128,128]{2,1,0:T(8,128)(2,1)S(1)}, bf16[272,640]{1,0...) custom-call(s32[2]{0:T(128)S(1)} %pad_add_fusion.scalars, ...), custom_call_target="tpu_custom_call" | custom-call | tf_op jit(solution)/shard_map/pallas_call | solution.py:23
  33.2 6.9 %collective-permute-start.3 = (bf16[5,128,128]{2,1,0:T(8,128)(2,1)S(1)}, bf16[5,128,128]{2,1,0:T(8,128)(2,1)S(1)}, u32[]{:S(2)}, u32[]{:S(2)}) collective-permute-start(bf16[5,128,128]{2,1,0:T(8,128)(2,1)S(1)} %get-tuple-element.30), channel_id=1, source_target_pairs={{0,2},{2,4},{4,6},{6,0},{1,3},{3,5},{5,7},{7,1},{8,10},{10,12},{12... | collective-permute-start | bytes 491528 | tf_op jit(solution)/shard_map/ppermute | solution.py:253
  40.1 2.3 %collective-permute-start.4 = (bf16[5,128,128]{2,1,0:T(8,128)(2,1)S(1)}, bf16[5,128,128]{2,1,0:T(8,128)(2,1)S(1)}, u32[]{:S(2)}, u32[]{:S(2)}) collective-permute-start(bf16[5,128,128]{2,1,0:T(8,128)(2,1)S(1)} %get-tuple-element.31), channel_id=1, source_target_pairs={{0,6},{2,0},{4,2},{6,4},{1,7},{3,1},{5,3},{7,5},{8,14},{10,8},{12,... | collective-permute-start | bytes 491528 | tf_op jit(solution)/shard_map/ppermute | solution.py:254
  42.4 10.2 %collective-permute-start.5 = (bf16[5,128,128]{2,1,0:T(8,128)(2,1)S(1)}, bf16[5,128,128]{2,1,0:T(8,128)(2,1)S(1)}, u32[]{:S(2)}, u32[]{:S(2)}) collective-permute-start(bf16[5,128,128]{2,1,0:T(8,128)(2,1)S(1)} %get-tuple-element.32), channel_id=1, source_target_pairs={{0,4},{2,6},{4,0},{6,2},{1,5},{3,7},{5,1},{7,3},{8,12},{10,14},{12... | collective-permute-start | bytes 491528 | tf_op jit(solution)/shard_map/ppermute | solution.py:252
  52.7 2.5 %shard_map.52 = (f32[272,1280]{1,0:T(8,128)S(1)}, bf16[272,640]{1,0:T(8,128)(2,1)S(1)}, bf16[272,640]{1,0:T(8,128)(2,1)S(1)}, f32[272,1280]{1,0:T(8,128)S(1)}) custom-call(s32[2]{0:T(128)S(1)} %pad_add_fusion.scalars, bf16[128,7680]{1,0:T(8,128)(2,1)S(1)} %bitcast.11, bf16[128,2560]{1,0:T(8,128)(2,1)S(1)} %bitcast.14, ...), custom_call_target="tpu_custom_call" | custom-call | tf_op jit(solution)/shard_map/pallas_call | solution.py:23
  55.2 0.0 collective-permute-done.3.up_ref
  55.2 6.9 %collective-permute-done.4.down_ref = bf16[5,128,128]{2,1,0:T(8,128)(2,1)S(1)} collective-permute-done((bf16[5,128,128]{2,1,0:T(8,128)(2,1)S(1)}, bf16[5,128,128]{2,1,0:T(8,128)(2,1)S(1)}, u32[]{:S(2)}, u32[]{:S(2)}) %collective-permute-start.4) | collective-permute-done | bytes 163872 | tf_op jit(solution)/shard_map/ppermute | solution.py:254
  62.1 11.5 %collective-permute-done.5.far_ref = bf16[5,128,128]{2,1,0:T(8,128)(2,1)S(1)} collective-permute-done((bf16[5,128,128]{2,1,0:T(8,128)(2,1)S(1)}, bf16[5,128,128]{2,1,0:T(8,128)(2,1)S(1)}, u32[]{:S(2)}, u32[]{:S(2)}) %collective-permute-start.5) | collective-permute-done | bytes 163872 | tf_op jit(solution)/shard_map/ppermute | solution.py:252
  73.5 2.3 %shard_map.53 = (bf16[128,1280]{1,0:T(8,128)(2,1)S(1)}, bf16[128,1280]{1,0:T(8,128)(2,1)S(1)}, f32[4,1280]{1,0:T(4,128)S(1)}) custom-call(s32[2]{0:T(128)S(1)} %pad_add_fusion.scalars, f32[272,1280]{1,0:T(8,128)S(1)} %get-tuple-element.26.kept_ref, bf16[272,640]{1,0:T(8,128)(2,1)S(1)} %get-tuple-element.27.va_ref, ...), custom_call_target="tpu_custom_call" | custom-call | tf_op jit(solution)/shard_map/pallas_call | solution.py:23
  75.8 0.2 reshape.31
  76.0 0.1 copy.6
  76.1 0.8 all_to_all.19
  76.8 4.8 %all-to-all-start = ((f32[32,1,160]{2,1,0:T(1,128)}), f32[32,1,160]{2,1,0:T(1,128)S(1)}, u32[]{:S(2)}, u32[]{:S(2)}) async-start(f32[32,1,160]{2,1,0:T(1,128)} %all_to_all.19), calls=%async_computation | async-start | bytes 65536 | tf_op jit(solution)/shard_map/all_to_all | solution.py:272
  81.6 8.7 %all-to-all-done = f32[32,1,160]{2,1,0:T(1,128)S(1)} async-done(((f32[32,1,160]{2,1,0:T(1,128)}), f32[32,1,160]{2,1,0:T(1,128)S(1)}, u32[]{:S(2)}, u32[]{:S(2)}) %all-to-all-start) | async-done | bytes 20512 | tf_op jit(solution)/shard_map/all_to_all | solution.py:272
  90.3 0.1 reduce_sum.18
  90.4 0.1 reshape.32
  90.5 0.6 broadcast_in_dim.21
  91.1 15.7 %all-to-all-start.1 = ((f32[32,1,80]{2,1,0:T(1,128)}), f32[32,1,80]{2,1,0:T(1,128)S(1)}, u32[]{:S(2)}, u32[]{:S(2)}) async-start(f32[32,1,80]{2,1,0:T(1,128)} %bitcast.6), calls=%async_computation.1 | async-start | bytes 32768 | tf_op jit(solution)/shard_map/all_to_all | solution.py:275
  106.8 2.1 %collective-permute-start.6 = (bf16[128,1280]{1,0:T(8,128)(2,1)S(1)}, bf16[128,1280]{1,0:T(8,128)(2,1)S(1)}, u32[]{:S(2)}, u32[]{:S(2)}) collective-permute-start(bf16[128,1280]{1,0:T(8,128)(2,1)S(1)} %get-tuple-element.34), channel_id=1, source_target_pairs={{0,1},{1,0},{2,3},{3,2},{4,5},{5,4},{6,7},{7,6},{8,9},{9,8},{10,11... | collective-permute-start | bytes 983048 | tf_op jit(solution)/shard_map/ppermute | solution.py:267
  108.9 9.4 %all-to-all-done.1 = f32[32,1,80]{2,1,0:T(1,128)S(1)} async-done(((f32[32,1,80]{2,1,0:T(1,128)}), f32[32,1,80]{2,1,0:T(1,128)S(1)}, u32[]{:S(2)}, u32[]{:S(2)}) %all-to-all-start.1) | async-done | bytes 10272 | tf_op jit(solution)/shard_map/all_to_all | solution.py:275
  118.3 0.1 select_reduce_fusion
  118.4 0.7 div.10
  119.1 0.0 collective-permute-done.6
  119.1 0.1 broadcast_select_fusion.1
  119.2 0.1 fusion.1
  119.3 0.9 maximum_bitcast_fusion
  (2 shorter events, 0.0 us)
Async XLA Ops:
  0.7 1.5 %copy-start = (bf16[1,128,7680]{2,1,0:T(8,128)(2,1)S(1)}, bf16[1,128,7680]{2,1,0:T(8,128)(2,1)}, u32[]{:S(2)}) copy-start(bf16[1,128,7680]{2,1,0:T(8,128)(2,1)} %param.3) | copy-start | bytes 5898244
  2.3 1.1 copy-start.1
  3.3 28.0 %copy-start.2 = (f32[4,7680]{1,0:T(4,128)S(1)}, f32[4,7680]{1,0:T(4,128)}, u32[]{:S(2)}) copy-start(f32[4,7680]{1,0:T(4,128)} %w_ref.5) | copy-start | bytes 368644
  4.0 27.4 %collective-permute-start = (bf16[128,5120]{1,0:T(8,128)(2,1)S(1)}, bf16[128,5120]{1,0:T(8,128)(2,1)S(1)}, u32[]{:S(2)}, u32[]{:S(2)}) collective-permute-start(bf16[128,5120]{1,0:T(8,128)(2,1)S(1)} %get-tuple-element.19), channel_id=1, source_target_pairs={{0,1},{1,0},{2,3},{3,2},{4,5},{5,4},{6,7},{7,6},{8,9},{9,8},{10,11... | collective-permute-start | bytes 3932168 | tf_op jit(solution)/shard_map/ppermute | solution.py:241
  20.1 9.4 %collective-permute-start.1 = (bf16[32,640]{1,0:T(8,128)(2,1)S(1)}, bf16[32,640]{1,0:T(8,128)(2,1)S(1)}, u32[]{:S(2)}, u32[]{:S(2)}) collective-permute-start(bf16[32,640]{1,0:T(8,128)(2,1)S(1)} %get-tuple-element.20), channel_id=1, source_target_pairs={{1,3},{3,5},{5,7},{2,0},{4,2},{6,4},{9,11},{11,13},{13,15},{10,8},... | collective-permute-start | bytes 122888 | tf_op jit(solution)/shard_map/ppermute | solution.py:242
  21.4 10.0 %collective-permute-start.2 = (bf16[32,640]{1,0:T(8,128)(2,1)S(1)}, bf16[32,640]{1,0:T(8,128)(2,1)S(1)}, u32[]{:S(2)}, u32[]{:S(2)}) collective-permute-start(bf16[32,640]{1,0:T(8,128)(2,1)S(1)} %get-tuple-element.21), channel_id=1, source_target_pairs={{1,2},{3,4},{5,6},{2,1},{4,3},{6,5},{9,10},{11,12},{13,14},{10,9},... | collective-permute-start | bytes 122888 | tf_op jit(solution)/shard_map/ppermute | solution.py:243
  33.2 21.9 %collective-permute-start.3 = (bf16[5,128,128]{2,1,0:T(8,128)(2,1)S(1)}, bf16[5,128,128]{2,1,0:T(8,128)(2,1)S(1)}, u32[]{:S(2)}, u32[]{:S(2)}) collective-permute-start(bf16[5,128,128]{2,1,0:T(8,128)(2,1)S(1)} %get-tuple-element.30), channel_id=1, source_target_pairs={{0,2},{2,4},{4,6},{6,0},{1,3},{3,5},{5,7},{7,1},{8,10},{10,12},{12... | collective-permute-start | bytes 491528 | tf_op jit(solution)/shard_map/ppermute | solution.py:253
  40.1 21.9 %collective-permute-start.4 = (bf16[5,128,128]{2,1,0:T(8,128)(2,1)S(1)}, bf16[5,128,128]{2,1,0:T(8,128)(2,1)S(1)}, u32[]{:S(2)}, u32[]{:S(2)}) collective-permute-start(bf16[5,128,128]{2,1,0:T(8,128)(2,1)S(1)} %get-tuple-element.31), channel_id=1, source_target_pairs={{0,6},{2,0},{4,2},{6,4},{1,7},{3,1},{5,3},{7,5},{8,14},{10,8},{12,... | collective-permute-start | bytes 491528 | tf_op jit(solution)/shard_map/ppermute | solution.py:254
  42.4 31.1 %collective-permute-start.5 = (bf16[5,128,128]{2,1,0:T(8,128)(2,1)S(1)}, bf16[5,128,128]{2,1,0:T(8,128)(2,1)S(1)}, u32[]{:S(2)}, u32[]{:S(2)}) collective-permute-start(bf16[5,128,128]{2,1,0:T(8,128)(2,1)S(1)} %get-tuple-element.32), channel_id=1, source_target_pairs={{0,4},{2,6},{4,0},{6,2},{1,5},{3,7},{5,1},{7,3},{8,12},{10,14},{12... | collective-permute-start | bytes 491528 | tf_op jit(solution)/shard_map/ppermute | solution.py:252
  76.8 13.5 %all-to-all-start = ((f32[32,1,160]{2,1,0:T(1,128)}), f32[32,1,160]{2,1,0:T(1,128)S(1)}, u32[]{:S(2)}, u32[]{:S(2)}) async-start(f32[32,1,160]{2,1,0:T(1,128)} %all_to_all.19), calls=%async_computation | async-start | bytes 65536 | tf_op jit(solution)/shard_map/all_to_all | solution.py:272
  91.1 27.3 %all-to-all-start.1 = ((f32[32,1,80]{2,1,0:T(1,128)}), f32[32,1,80]{2,1,0:T(1,128)S(1)}, u32[]{:S(2)}, u32[]{:S(2)}) async-start(f32[32,1,80]{2,1,0:T(1,128)} %bitcast.6), calls=%async_computation.1 | async-start | bytes 32768 | tf_op jit(solution)/shard_map/all_to_all | solution.py:275
  106.8 12.3 %collective-permute-start.6 = (bf16[128,1280]{1,0:T(8,128)(2,1)S(1)}, bf16[128,1280]{1,0:T(8,128)(2,1)S(1)}, u32[]{:S(2)}, u32[]{:S(2)}) collective-permute-start(bf16[128,1280]{1,0:T(8,128)(2,1)S(1)} %get-tuple-element.34), channel_id=1, source_target_pairs={{0,1},{1,0},{2,3},{3,2},{4,5},{5,4},{6,7},{7,6},{8,9},{9,8},{10,11... | collective-permute-start | bytes 983048 | tf_op jit(solution)/shard_map/ppermute | solution.py:267

commit v2 on v0

v2 whole, which is shorter than its diff:
```python
import jax
import jax.numpy as jnp
from jax import lax
from jax.experimental import pallas as pl
from jax.experimental.pallas import tpu as pltpu
from jax.sharding import Mesh
from jax.sharding import PartitionSpec as P

HEAD = 128
TAPS = 4
ROWS = 128
PAIR = 2 * ROWS
EXT = PAIR + 16
PRE = 8
LONG = PRE + PAIR + 8
EDGE = 8
F32 = jnp.float32
BF16 = jnp.bfloat16
LEFT, A, B, RAW = range(4)
VMEM = pl.BlockSpec(memory_space=pltpu.VMEM)
SMEM = pl.BlockSpec(memory_space=pltpu.SMEM)


def call(kernel, shapes, scratch, scalars, *arrays, space=VMEM, limit=32):
    return pl.pallas_call(
        kernel,
        out_shape=[jax.ShapeDtypeStruct(s, t) for s, t in shapes],
        in_specs=[SMEM] + [space] * len(arrays),
        out_specs=[VMEM] * len(shapes),
        scratch_shapes=scratch,
        compiler_params=pltpu.CompilerParams(vmem_limit_bytes=limit * 1024 * 1024),
    )(scalars, *arrays)


def nt(a, b):
    return lax.dot_general(a, b, (((1,), (1,)), ((), ())), preferred_element_type=F32)


def tn(a, b):
    return lax.dot_general(a, b, (((0,), (0,)), ((), ())), preferred_element_type=F32)


def nn(a, b):
    return lax.dot_general(a, b, (((1,), (0,)), ((), ())), preferred_element_type=F32)


def lanes(group, head, width):
    return slice(group * width + head * HEAD, group * width + (head + 1) * HEAD)


def pack_kernel(scalars, x_ref, g_ref, keep_ref, send_ref, sems):
    core = scalars[0]
    width = keep_ref.shape[1] // 4
    of_core = (
        ((x_ref, 3), (g_ref, 1), (x_ref, 5), (x_ref, 1)),
        ((x_ref, 0), (x_ref, 4), (g_ref, 0), (x_ref, 2)),
    )

    def fill(mine):
        copies = []

        def copy(source_ref, group, out_ref, slot):
            lanes_in = slice(group * width, (group + 1) * width)
            lanes_out = slice(slot * width, (slot + 1) * width)
            copies.append(
                pltpu.make_async_copy(
                    source_ref.at[:, lanes_in], out_ref.at[:, lanes_out], sems.at[len(copies)]
                )
            )

        for slot, (source_ref, group) in enumerate(of_core[1 - mine]):
            copy(source_ref, group, send_ref, slot)
        for slot, (source_ref, group) in enumerate(of_core[mine]):
            copy(source_ref, group, keep_ref, slot)
        for each in copies:
            each.start()
        for each in copies:
            each.wait()

    @pl.when(core == 0)
    def _():
        fill(0)

    @pl.when(core == 1)
    def _():
        fill(1)


def taps_kernel(scalars, w_ref, taps_ref):
    width = taps_ref.shape[1] // 4
    row = lax.broadcasted_iota(jnp.int32, (TAPS, width), 0)
    unit = jnp.where(row == 0, 1.0, 0.0).astype(F32)
    for core, groups in enumerate(((3, None, 5, 1), (0, 4, None, 2))):

        @pl.when(scalars[0] == core)
        def _():
            for slot, group in enumerate(groups):
                part = unit if group is None else w_ref[:, group * width : (group + 1) * width]
                taps_ref[:, slot * width : (slot + 1) * width] = part


def gather_rows(core, keep_ref, received_ref, at, padded_ref):
    own = pl.ds(pl.multiple_of(PRE + core * ROWS, 8), ROWS)
    other = pl.ds(pl.multiple_of(PRE + (1 - core) * ROWS, 8), ROWS)
    padded_ref[own, :] = keep_ref[:, at].astype(F32)
    padded_ref[other, :] = received_ref[:, at].astype(F32)


def convolved(padded_ref, taps, start, count):
    total = taps[0:1] * padded_ref[start : start + count, :]
    for j in range(1, TAPS):
        total = total + taps[j : j + 1] * padded_ref[start - j : start - j + count, :]
    return total


def states_kernel(scalars, keep_ref, received_ref, taps_ref, message_ref, wrap_ref, *scratch):
    core, chip = scalars[0], scalars[1]
    width = keep_ref.shape[1] // 4
    padded_refs, value_refs = scratch[:4], scratch[4:]
    for ref in padded_refs:
        ref[0:PRE, :] = jnp.zeros((PRE, HEAD), F32)
    row = lax.broadcasted_iota(jnp.int32, (ROWS, HEAD), 0)
    kept_rows = (row >= TAPS - 1) | (chip == 0)
    first_rows = jnp.where(chip == 0, 0.0, 1.0)
    for head in range(width // HEAD):
        firsts, lasts = [], []
        for turn, group in enumerate((LEFT, B)):
            padded_ref = padded_refs[(2 * head + turn) % 4]
            value_ref = value_refs[(2 * head + turn) % 4]
            at = lanes(group, head, width)
            gather_rows(core, keep_ref, received_ref, at, padded_ref)
            taps = taps_ref[:, at]
            for first in (0, ROWS):
                total = convolved(padded_ref, taps, PRE + first, ROWS)
                if group == LEFT and first == 0:
                    total = jnp.where(kept_rows, total, 0.0)
                value_ref[first : first + ROWS, :] = total.astype(BF16)
            front = padded_ref[PRE : PRE + 4, :]
            firsts.append(front * first_rows if group == LEFT else front)
            lasts.append(padded_ref[PRE + PAIR - 4 : PRE + PAIR, :])
        left, right = value_refs[(2 * head) % 4], value_refs[(2 * head + 1) % 4]
        state = tn(left[...], right[...]).astype(BF16)
        firsts, lasts = jnp.concatenate(firsts, 0), jnp.concatenate(lasts, 0)
        for ref in (message_ref, wrap_ref):
            ref[head, 0:HEAD, :] = state
        message_ref[head, HEAD:, :] = jnp.concatenate([firsts, lasts], 0).astype(BF16)
        wrap_ref[head, HEAD:, :] = jnp.where(core == 0, lasts, firsts).astype(BF16)


def edge_rows_kernel(scalars, keep_ref, send_ref, message_ref, same_ref, cross_ref):
    core = scalars[0]
    width = keep_ref.shape[1] // 4
    edge = pl.ds(pl.multiple_of(core * (ROWS - 16), 16), 16)
    for ref, out_ref, later in ((keep_ref, same_ref, A), (send_ref, cross_ref, B)):
        for slot, (first, last) in enumerate(((LEFT, LEFT), (A, later), (B, RAW))):
            zero = ref[edge, first * width : (first + 1) * width].astype(F32)[0:4]
            one = ref[edge, last * width : (last + 1) * width].astype(F32)[12:16]
            rows = jnp.where(core == 1, one, zero).astype(BF16)
            out_ref[:, slot * width : (slot + 1) * width] = rows


def inside_kernel(
    scalars, keep_ref, received_ref, same_ref, cross_ref, taps_ref,
    kept_ref, a_ref, raw_ref, left_tail_ref, b_tail_ref, *scratch,
):
    core = scalars[0]
    width = keep_ref.shape[1] // 4
    padded_refs, value_refs = scratch[:4], scratch[4:]
    same, cross = same_ref[...].astype(F32), cross_ref[...].astype(F32)
    before, after = jnp.where(core == 1, same, cross), jnp.where(core == 1, cross, same)
    row = lax.broadcasted_iota(jnp.int32, (EXT, EXT), 0)
    column = lax.broadcasted_iota(jnp.int32, (EXT, EXT), 1)
    causal = jnp.where(column <= row, 1.0 / HEAD, 0.0)
    reverse = jnp.where(
        (column >= row) & (column < PAIR),
        1.0 / HEAD,
        jnp.where((column >= PAIR) & (column < row), -1.0 / HEAD, 0.0),
    )
    mask = jnp.where(core == 0, causal, reverse)
    none = jnp.zeros((4, HEAD), F32)
    tail_row = lax.broadcasted_iota(jnp.int32, (16, HEAD), 0)
    tail_used = (tail_row < TAPS - 1) & (core == 1)
    turn = 0
    for head in range(width // HEAD):
        to = lanes(0, head, width)
        values = []
        for group in (LEFT, A, B, RAW):
            padded_ref = padded_refs[turn % 4]
            value_ref = value_refs[turn % 4]
            turn += 1
            at = lanes(group, head, width)
            gather_rows(core, keep_ref, received_ref, at, padded_ref)
            front = before[:, lanes((0, 1, 1, 2)[group], head, width)]
            back = after[:, lanes((0, 1, 2, 2)[group], head, width)]
            padded_ref[0:PRE, :] = jnp.concatenate([none, front], 0)
            padded_ref[PRE + PAIR : LONG, :] = jnp.concatenate([back, none], 0)
            if group == RAW:
                raw_ref[:, to] = padded_ref[...]
                continue
            taps = taps_ref[:, at]
            for first in (0, ROWS):
                total = convolved(padded_ref, taps, PRE + first, ROWS)
                value_ref[first : first + ROWS, :] = total.astype(BF16)
            tail = convolved(padded_ref, taps, PRE + PAIR, 8)
            tail = jnp.concatenate([tail, jnp.zeros((8, HEAD), F32)], 0)
            value_ref[PAIR:EXT, :] = tail.astype(BF16)
            if group != A:
                tail_ref = left_tail_ref if group == LEFT else b_tail_ref
                tail_ref[:, to] = jnp.where(tail_used, tail, 0.0).astype(BF16)
            values.append(value_ref)
        left, a, b = (ref[...] for ref in values)
        a_ref[:, to] = a
        scores = (nt(a, b) * mask).astype(BF16)
        kept_ref[:, to] = nn(scores, left)


def kept_kernel(
    scalars, inside_ref, a_ref, raw_ref, left_tail_ref, b_tail_ref, near_ref, far_ref, wrap_ref,
    taps_ref, kept_ref, terms_ref, edge_ref,
):
    core = scalars[0]
    width = a_ref.shape[1]
    row = lax.broadcasted_iota(jnp.int32, (8, HEAD), 0)
    nothing = jnp.zeros((8, HEAD), F32)
    for head in range(width // HEAD):
        to = lanes(0, head, width)
        near, far, wrap = (r[head, HEAD:, :].astype(F32) for r in (near_ref, far_ref, wrap_ref))
        near = jnp.where(core == 0, near[0:EDGE], near[EDGE : 2 * EDGE])
        first, last = far[0:EDGE], far[EDGE : 2 * EDGE]
        rows = []
        seams = []
        for zero, one in (((last, near), (near, first)), ((wrap, first), (last, wrap))):
            seams.append([jnp.where(core == 0, *pair) for pair in zip(zero, one)])
        for group, at in ((LEFT, slice(0, 4)), (B, slice(4, 8))):
            taps = taps_ref[:, lanes(group, head, width)]
            for turn, seam in enumerate(seams):
                part = edge_ref.at[2 * (group // 2) + turn]
                part[0:8, :] = jnp.concatenate([seam[0][at], seam[1][at]], 0)
                part[8:16, :] = nothing
                total = convolved(part, taps, 4, 8)
                rows.append(jnp.where(row < TAPS - 1, total, 0.0))
        left = jnp.concatenate(rows[0:2], 0).astype(BF16)
        right = jnp.concatenate(rows[2:4], 0).astype(BF16)
        state = (
            near_ref[head, 0:HEAD, :].astype(F32) + far_ref[head, 0:HEAD, :].astype(F32)
            + wrap_ref[head, 0:HEAD, :].astype(F32)
            + tn(left, right) + tn(left_tail_ref[:, to], b_tail_ref[:, to])
        ).astype(BF16)
        kept_ref[:, to] = inside_ref[:, to] + nt(a_ref[:, to], state) * (1.0 / HEAD)
        sums = [jnp.zeros((8, HEAD), F32)] * TAPS
        for first in range(0, PAIR, 64):
            kept = kept_ref[first : first + 64, to]
            for j in range(TAPS):
                start = PRE + first - j
                term = kept * raw_ref[start : start + 64, to]
                sums[j] = sums[j] + jnp.sum(term.reshape(8, 8, HEAD), 0)
        terms_ref[:, to] = jnp.concatenate([jnp.sum(s, 0, keepdims=True) for s in sums], 0)


def input_kernel(scalars, kept_ref, taps_ref, own_ref, send_ref, grad_ref):
    core = scalars[0]
    width = own_ref.shape[1]
    for head in range(width // HEAD):
        to = lanes(0, head, width)
        taps = taps_ref[:, lanes(RAW, head, width)]
        for first in range(0, PAIR, 64):
            grad = taps[0:1] * kept_ref[first : first + 64, to]
            for j in range(1, TAPS):
                grad = grad + taps[j : j + 1] * kept_ref[first + j : first + j + 64, to]
            grad_ref[first : first + 64, to] = grad.astype(BF16)
    own_ref[...] = grad_ref[pl.ds(pl.multiple_of(core * ROWS, ROWS), ROWS), :]
    send_ref[...] = grad_ref[pl.ds(pl.multiple_of((1 - core) * ROWS, ROWS), ROWS), :]


def per_device(qkv_input, conv_weight, out_cotangent):
    x, g = qkv_input[0], out_cotangent[0]
    width = g.shape[1] // 2
    heads = width // HEAD
    chips = lax.axis_size("zh")
    core, chip, low = lax.axis_index("core"), lax.axis_index("zh"), lax.axis_index("zl")
    scalars = jnp.stack([core, chip]).astype(jnp.int32)
    swap = [(0, 1), (1, 0)]
    line = ("zh", "core")

    def hops(by):
        later = [(2 * c, 2 * (c + by)) for c in range(chips - by)]
        return later + [(2 * (c + by) + 1, 2 * c + 1) for c in range(chips - by)]

    pairs = range(chips - 1)
    to_same = [(2 * c + 1, 2 * c + 3) for c in pairs] + [(2 * c + 2, 2 * c) for c in pairs]
    to_cross = [(2 * c + 1, 2 * c + 2) for c in pairs] + [(2 * c + 2, 2 * c + 1) for c in pairs]

    keep, send = call(
        pack_kernel, [((ROWS, 4 * width), BF16)] * 2, [pltpu.SemaphoreType.DMA((8,))],
        scalars, x, g, space=pl.BlockSpec(memory_space=pl.ANY), limit=8,
    )
    (taps,) = call(taps_kernel, [((TAPS, 4 * width), F32)], [], scalars, conv_weight)
    received = lax.ppermute(send, "core", swap)
    padded = [pltpu.VMEM((LONG, HEAD), F32)] * 4
    message, wrap = call(
        states_kernel,
        [((heads, HEAD + size, HEAD), BF16) for size in (2 * EDGE, EDGE)],
        padded + [pltpu.VMEM((PAIR, HEAD), BF16)] * 4,
        scalars, keep, received, taps,
    )
    same, cross = call(
        edge_rows_kernel, [((4, 3 * width), BF16)] * 2, [], scalars, keep, send, message
    )
    near = lax.ppermute(message, line, hops(1))
    far = lax.ppermute(message, line, hops(2))
    wrap = lax.ppermute(wrap, line, hops(3))
    same = lax.ppermute(same, line, to_same)
    cross = lax.ppermute(cross, line, to_cross)
    inside, a, raw, left_tail, b_tail = call(
        inside_kernel,
        [((EXT, width), F32), ((EXT, width), BF16), ((LONG, width), F32)]
        + [((16, width), BF16)] * 2,
        padded + [pltpu.VMEM((EXT, HEAD), BF16)] * 4,
        scalars, keep, received, same, cross, taps,
    )
    kept, terms = call(
        kept_kernel, [((EXT, width), F32), ((TAPS, width), F32)],
        [pltpu.VMEM((4, 16, HEAD), F32)],
        scalars, inside, a, raw, left_tail, b_tail, near, far, wrap, taps,
    )

    spread = lax.axis_size("yx")
    few = width // 2 // spread
    rows = terms.reshape(TAPS, 2, spread, few).transpose(2, 1, 0, 3).reshape(spread, 2 * TAPS * few)
    summed = jnp.sum(lax.all_to_all(rows, "yx", 0, 0, tiled=True), 0).reshape(2, TAPS * few)
    rows = jnp.broadcast_to(summed[None, None, :, None], (2, 2, 2, chips, TAPS * few))
    rows = lax.all_to_all(
        rows.reshape(8 * chips, TAPS * few), ("core", "zl", "zh"), 0, 0, tiled=True
    )
    fitting = (jnp.arange(8 * chips) // (4 * chips) == low // 2)[:, None]
    share = jnp.sum(jnp.where(fitting, rows, 0.0), 0).reshape(TAPS, few)
    shares = share / (lax.axis_size("zl") * spread)

    own, sent = call(
        input_kernel, [((ROWS, width), BF16)] * 2, [pltpu.VMEM((PAIR, width), BF16)],
        scalars, kept, taps,
    )
    other = lax.ppermute(sent, "core", swap)
    first, second = jnp.where(core == 0, own, other), jnp.where(core == 0, other, own)
    return jnp.concatenate([first, second], 1)[None], shares


def solution(mesh):
    dp, seq = mesh.shape["dp"], mesh.shape["seq"]
    fine = Mesh(mesh.devices.reshape(4, dp // 4, seq // 2, 2), ("zl", "yx", "zh", "core"))
    rows = P(("zl", "yx"), ("zh", "core"), None)
    return jax.shard_map(
        per_device, mesh=fine, in_specs=(rows, P(), rows),
        out_specs=(rows, P(None, ("zl", "yx"))), check_vma=False,
    )
```

time: 991 us -> 116 us (0.12)
  the two profiles are of different devices: /device:TPU:256 before, /device:TPU:1 now
where the time goes in v2:
time: 116 us; the launch traced here: 115 us
  starting transfers between devices  63.4 us (55%)
  waiting for transfers between devices  33.9 us (29%)
  Pallas kernels  10.8 us (9%)
  local copies, waits for them, and re-layouts  5.02 us (4%)
  other arithmetic  1.16 us (1%)
    ppermute x1, starting transfers between devices, per_device(): received = lax.ppermute(send, 'core', swap)  16.1 us
    ppermute x1, starting transfers between devices, per_device(): cross = lax.ppermute(cross, line, to_cross)  12.7 us
    all_to_all x1, starting transfers between devices, per_device(): lax.all_to_all(rows.reshape(8 * chips, TAPS * few), ('core', 'zl', 'zh'),...  12.2 us
    ppermute x1, waiting for transfers between devices, per_device(): wrap = lax.ppermute(wrap, line, hops(3))  11.3 us
    pallas_call x7, Pallas kernels, call(): pl.pallas_call(kernel, out_shape=[jax.ShapeDtypeStruct(s, t) for s, t in...  10.8 us
    all_to_all x1, starting transfers between devices, per_device(): lax.all_to_all(rows, 'yx', 0, 0, tiled=True)  9.15 us
    all_to_all x1, waiting for transfers between devices, per_device(): lax.all_to_all(rows, 'yx', 0, 0, tiled=True)  8.68 us
    all_to_all x1, waiting for transfers between devices, per_device(): lax.all_to_all(rows.reshape(8 * chips, TAPS * few), ('core', 'zl', 'zh'),...  8.24 us
  transfers between devices with their start and end apart: 9, of which 6 were waited for; matrix products, arithmetic and copies ran while one was open for 1% of the time, Pallas kernels for 5%

profile of v2, /device:TPU:1, one launch (start us, length us, event | category | flops | bytes accessed | tf_op | source)
XLA Modules:
  0.0 115.1 jit_solution(16270017335919472051)
XLA Ops:
  0.6 0.1 pad_add_fusion.scalars
  0.7 0.0 copy-start
  0.7 1.5 %copy-done = bf16[1,128,7680]{2,1,0:T(8,128)(2,1)S(1)} copy-done((bf16[1,128,7680]{2,1,0:T(8,128)(2,1)S(1)}, bf16[1,128,7680]{2,1,0:T(8,128)(2,1)}, u32[]{:S(2)}) %copy-start) | copy-done | bytes 1966104
  2.3 0.0 copy-start.1
  2.3 1.1 copy-done.1
  3.3 0.0 copy-start.2
  3.3 0.8 shard_map.50
  4.2 16.1 %collective-permute-start = (bf16[128,5120]{1,0:T(8,128)(2,1)S(1)}, bf16[128,5120]{1,0:T(8,128)(2,1)S(1)}, u32[]{:S(2)}, u32[]{:S(2)}) collective-permute-start(bf16[128,5120]{1,0:T(8,128)(2,1)S(1)} %get-tuple-element.18.send_ref), channel_id=1, source_target_pairs={{0,1},{1,0},{2,3},{3,2},{4,5},{5,4},{6,7},{7,6},{8,9},{9,8},{10,11... | collective-permute-start | bytes 3932168 | tf_op jit(solution)/shard_map/ppermute | solution.py:298
  20.3 0.0 copy-done.2
  20.3 0.6 shard_map.51.taps_ref
  20.8 2.1 %collective-permute-done.received_ref = bf16[128,5120]{1,0:T(8,128)(2,1)S(1)} collective-permute-done((bf16[128,5120]{1,0:T(8,128)(2,1)S(1)}, bf16[128,5120]{1,0:T(8,128)(2,1)S(1)}, u32[]{:S(2)}, u32[]{:S(2)}) %collective-permute-start) | collective-permute-done | bytes 1310752 | tf_op jit(solution)/shard_map/ppermute | solution.py:298
  22.9 2.3 %shard_map.52 = (bf16[10,144,128]{2,1,0:T(8,128)(2,1)S(1)}, bf16[10,136,128]{2,1,0:T(8,128)(2,1)S(1)}) custom-call(s32[2]{0:T(128)S(1)} %pad_add_fusion.scalars, bf16[128,5120]{1,0:T(8,128)(2,1)S(1)} %get-tuple-element.17.keep_ref, bf16[128,5120]{1,0:T(8,128)(2,1)S(1)} %collective-permute-done.received_ref, f32[4,5120]{1,0:T(4,128)S(1)} %shard_map.51.taps_ref), custom_call_target="tpu_custom_call" | custom-call | tf_op jit(solution)/shard_map/pallas_call | solution.py:25
  25.2 1.3 %collective-permute-start.3 = (bf16[10,144,128]{2,1,0:T(8,128)(2,1)S(1)}, bf16[10,144,128]{2,1,0:T(8,128)(2,1)S(1)}, u32[]{:S(2)}, u32[]{:S(2)}) collective-permute-start(bf16[10,144,128]{2,1,0:T(8,128)(2,1)S(1)} %get-tuple-element.19.message_ref), channel_id=1, source_target_pairs={{0,2},{2,4},{4,6},{3,1},{5,3},{7,5},{8,10},{10,12},{12,14},{11,9},... | collective-permute-start | bytes 1105928 | tf_op jit(solution)/shard_map/ppermute | solution.py:309
  26.5 1.3 %collective-permute-start.4 = (bf16[10,144,128]{2,1,0:T(8,128)(2,1)S(1)}, bf16[10,144,128]{2,1,0:T(8,128)(2,1)S(1)}, u32[]{:S(2)}, u32[]{:S(2)}) collective-permute-start(bf16[10,144,128]{2,1,0:T(8,128)(2,1)S(1)} %get-tuple-element.19.message_ref), channel_id=1, source_target_pairs={{0,4},{2,6},{5,1},{7,3},{8,12},{10,14},{13,9},{15,11},{16,20},{18,... | collective-permute-start | bytes 1105928 | tf_op jit(solution)/shard_map/ppermute | solution.py:310
  27.8 1.3 %collective-permute-start.5 = (bf16[10,136,128]{2,1,0:T(8,128)(2,1)S(1)}, bf16[10,136,128]{2,1,0:T(8,128)(2,1)S(1)}, u32[]{:S(2)}, u32[]{:S(2)}) collective-permute-start(bf16[10,136,128]{2,1,0:T(8,128)(2,1)S(1)} %get-tuple-element.27), channel_id=1, source_target_pairs={{0,6},{7,1},{8,14},{15,9},{16,22},{23,17},{24,30},{31,25},{32,38},... | collective-permute-start | bytes 1044488 | tf_op jit(solution)/shard_map/ppermute | solution.py:311
  29.1 0.6 shard_map.53
  29.7 7.3 %collective-permute-start.1 = (bf16[4,3840]{1,0:T(4,128)(2,1)S(1)}, bf16[4,3840]{1,0:T(4,128)(2,1)S(1)}, u32[]{:S(2)}, u32[]{:S(2)}) collective-permute-start(bf16[4,3840]{1,0:T(4,128)(2,1)S(1)} %get-tuple-element.20), channel_id=1, source_target_pairs={{1,3},{3,5},{5,7},{2,0},{4,2},{6,4},{9,11},{11,13},{13,15},{10,8},... | collective-permute-start | bytes 92168 | tf_op jit(solution)/shard_map/ppermute | solution.py:312
  37.0 12.7 %collective-permute-start.2 = (bf16[4,3840]{1,0:T(4,128)(2,1)S(1)}, bf16[4,3840]{1,0:T(4,128)(2,1)S(1)}, u32[]{:S(2)}, u32[]{:S(2)}) collective-permute-start(bf16[4,3840]{1,0:T(4,128)(2,1)S(1)} %get-tuple-element.21), channel_id=1, source_target_pairs={{1,2},{3,4},{5,6},{2,1},{4,3},{6,5},{9,10},{11,12},{13,14},{10,9},... | collective-permute-start | bytes 92168 | tf_op jit(solution)/shard_map/ppermute | solution.py:313
  49.7 0.0 collective-permute-done.1.same_ref
  49.7 2.9 %collective-permute-done.2.cross_ref = bf16[4,3840]{1,0:T(4,128)(2,1)S(1)} collective-permute-done((bf16[4,3840]{1,0:T(4,128)(2,1)S(1)}, bf16[4,3840]{1,0:T(4,128)(2,1)S(1)}, u32[]{:S(2)}, u32[]{:S(2)}) %collective-permute-start.2) | collective-permute-done | bytes 30752 | tf_op jit(solution)/shard_map/ppermute | solution.py:313
  52.6 3.1 %shard_map.54 = (f32[272,1280]{1,0:T(8,128)S(1)}, bf16[272,1280]{1,0:T(8,128)(2,1)S(1)}, f32[272,1280]{1,0:T(8,128)S(1)}, bf16[16,1280]{1,0:T(8,128)(2,1)S(1)}, bf16[16,1280]{1,0:T(8,128)(2,1)S(1)}) custom-call(s32[2]{0:T(128)S(1)} %pad_add_fusion.scalars, bf16[128,5120]{1,0:T(8,128)(2,1)S(1)} %get-tuple-element.17.keep_ref, ...), custom_call_target="tpu_custom_call" | custom-call | tf_op jit(solution)/shard_map/pallas_call | solution.py:25
  55.7 11.3 %collective-permute-done.5.wrap_ref = bf16[10,136,128]{2,1,0:T(8,128)(2,1)S(1)} collective-permute-done((bf16[10,136,128]{2,1,0:T(8,128)(2,1)S(1)}, bf16[10,136,128]{2,1,0:T(8,128)(2,1)S(1)}, u32[]{:S(2)}, u32[]{:S(2)}) %collective-permute-start.5) | collective-permute-done | bytes 348192 | tf_op jit(solution)/shard_map/ppermute | solution.py:311
  66.9 0.0 collective-permute-done.3.near_ref
  66.9 0.8 collective-permute-done.4.far_ref
  67.8 2.2 %shard_map.55 = (f32[272,1280]{1,0:T(8,128)S(1)}, f32[4,1280]{1,0:T(4,128)S(1)}) custom-call(s32[2]{0:T(128)S(1)} %pad_add_fusion.scalars, f32[272,1280]{1,0:T(8,128)S(1)} %get-tuple-element.22.inside_ref, bf16[272,1280]{1,0:T(8,128)(2,1)S(1)} %get-tuple-element.23.a_ref, f32[272,1280]{1,0:T(8,128)S(1)} %get-tuple-element.24.raw_ref, ...), custom_call_target="tpu_custom_call" | custom-call | tf_op jit(solution)/shard_map/pallas_call | solution.py:25
  70.0 0.2 reshape.33
  70.1 0.1 copy.6
  70.2 0.8 all_to_all.19
  71.0 9.1 %all-to-all-start = ((f32[32,1,160]{2,1,0:T(1,128)}), f32[32,1,160]{2,1,0:T(1,128)S(1)}, u32[]{:S(2)}, u32[]{:S(2)}) async-start(f32[32,1,160]{2,1,0:T(1,128)} %all_to_all.19), calls=%async_computation | async-start | bytes 65536 | tf_op jit(solution)/shard_map/all_to_all | solution.py:330
  80.2 8.7 %all-to-all-done = f32[32,1,160]{2,1,0:T(1,128)S(1)} async-done(((f32[32,1,160]{2,1,0:T(1,128)}), f32[32,1,160]{2,1,0:T(1,128)S(1)}, u32[]{:S(2)}, u32[]{:S(2)}) %all-to-all-start) | async-done | bytes 20512 | tf_op jit(solution)/shard_map/all_to_all | solution.py:330
  88.9 0.1 reduce_sum.18
  88.9 0.1 broadcast_in_dim.25
  89.0 0.6 broadcast_in_dim.26
  89.6 12.2 %all-to-all-start.1 = ((f32[32,1,80]{2,1,0:T(1,128)}), f32[32,1,80]{2,1,0:T(1,128)S(1)}, u32[]{:S(2)}, u32[]{:S(2)}) async-start(f32[32,1,80]{2,1,0:T(1,128)} %bitcast.6), calls=%async_computation.1 | async-start | bytes 32768 | tf_op jit(solution)/shard_map/all_to_all | solution.py:332
  101.8 1.2 %shard_map.56 = (bf16[128,1280]{1,0:T(8,128)(2,1)S(1)}, bf16[128,1280]{1,0:T(8,128)(2,1)S(1)}) custom-call(s32[2]{0:T(128)S(1)} %pad_add_fusion.scalars, f32[272,1280]{1,0:T(8,128)S(1)} %get-tuple-element.28.kept_ref, f32[4,5120]{1,0:T(4,128)S(1)} %shard_map.51.taps_ref), custom_call_target="tpu_custom_call" | custom-call | tf_op jit(solution)/shard_map/pallas_call | solution.py:25
  103.0 2.1 %collective-permute-start.6 = (bf16[128,1280]{1,0:T(8,128)(2,1)S(1)}, bf16[128,1280]{1,0:T(8,128)(2,1)S(1)}, u32[]{:S(2)}, u32[]{:S(2)}) collective-permute-start(bf16[128,1280]{1,0:T(8,128)(2,1)S(1)} %get-tuple-element.30), channel_id=1, source_target_pairs={{0,1},{1,0},{2,3},{3,2},{4,5},{5,4},{6,7},{7,6},{8,9},{9,8},{10,11... | collective-permute-start | bytes 983048 | tf_op jit(solution)/shard_map/ppermute | solution.py:343
  105.2 8.2 %all-to-all-done.1 = f32[32,1,80]{2,1,0:T(1,128)S(1)} async-done(((f32[32,1,80]{2,1,0:T(1,128)}), f32[32,1,80]{2,1,0:T(1,128)S(1)}, u32[]{:S(2)}, u32[]{:S(2)}) %all-to-all-start.1) | async-done | bytes 10272 | tf_op jit(solution)/shard_map/all_to_all | solution.py:332
  113.4 0.1 select_reduce_fusion
  113.5 0.7 div.31
  114.2 0.0 collective-permute-done.6
  114.2 0.9 maximum_bitcast_fusion
  (3 shorter events, 0.1 us)
Async XLA Ops:
  0.7 1.5 %copy-start = (bf16[1,128,7680]{2,1,0:T(8,128)(2,1)S(1)}, bf16[1,128,7680]{2,1,0:T(8,128)(2,1)}, u32[]{:S(2)}) copy-start(bf16[1,128,7680]{2,1,0:T(8,128)(2,1)} %param.3) | copy-start | bytes 5898244
  2.3 1.1 copy-start.1
  3.3 16.9 %copy-start.2 = (f32[4,7680]{1,0:T(4,128)S(1)}, f32[4,7680]{1,0:T(4,128)}, u32[]{:S(2)}) copy-start(f32[4,7680]{1,0:T(4,128)} %w_ref.1) | copy-start | bytes 368644
  4.2 18.7 %collective-permute-start = (bf16[128,5120]{1,0:T(8,128)(2,1)S(1)}, bf16[128,5120]{1,0:T(8,128)(2,1)S(1)}, u32[]{:S(2)}, u32[]{:S(2)}) collective-permute-start(bf16[128,5120]{1,0:T(8,128)(2,1)S(1)} %get-tuple-element.18.send_ref), channel_id=1, source_target_pairs={{0,1},{1,0},{2,3},{3,2},{4,5},{5,4},{6,7},{7,6},{8,9},{9,8},{10,11... | collective-permute-start | bytes 3932168 | tf_op jit(solution)/shard_map/ppermute | solution.py:298
  25.2 41.8 %collective-permute-start.3 = (bf16[10,144,128]{2,1,0:T(8,128)(2,1)S(1)}, bf16[10,144,128]{2,1,0:T(8,128)(2,1)S(1)}, u32[]{:S(2)}, u32[]{:S(2)}) collective-permute-start(bf16[10,144,128]{2,1,0:T(8,128)(2,1)S(1)} %get-tuple-element.19.message_ref), channel_id=1, source_target_pairs={{0,2},{2,4},{4,6},{3,1},{5,3},{7,5},{8,10},{10,12},{12,14},{11,9},... | collective-permute-start | bytes 1105928 | tf_op jit(solution)/shard_map/ppermute | solution.py:309
  26.5 41.3 %collective-permute-start.4 = (bf16[10,144,128]{2,1,0:T(8,128)(2,1)S(1)}, bf16[10,144,128]{2,1,0:T(8,128)(2,1)S(1)}, u32[]{:S(2)}, u32[]{:S(2)}) collective-permute-start(bf16[10,144,128]{2,1,0:T(8,128)(2,1)S(1)} %get-tuple-element.19.message_ref), channel_id=1, source_target_pairs={{0,4},{2,6},{5,1},{7,3},{8,12},{10,14},{13,9},{15,11},{16,20},{18,... | collective-permute-start | bytes 1105928 | tf_op jit(solution)/shard_map/ppermute | solution.py:310
  27.8 39.2 %collective-permute-start.5 = (bf16[10,136,128]{2,1,0:T(8,128)(2,1)S(1)}, bf16[10,136,128]{2,1,0:T(8,128)(2,1)S(1)}, u32[]{:S(2)}, u32[]{:S(2)}) collective-permute-start(bf16[10,136,128]{2,1,0:T(8,128)(2,1)S(1)} %get-tuple-element.27), channel_id=1, source_target_pairs={{0,6},{7,1},{8,14},{15,9},{16,22},{23,17},{24,30},{31,25},{32,38},... | collective-permute-start | bytes 1044488 | tf_op jit(solution)/shard_map/ppermute | solution.py:311
  29.7 20.0 %collective-permute-start.1 = (bf16[4,3840]{1,0:T(4,128)(2,1)S(1)}, bf16[4,3840]{1,0:T(4,128)(2,1)S(1)}, u32[]{:S(2)}, u32[]{:S(2)}) collective-permute-start(bf16[4,3840]{1,0:T(4,128)(2,1)S(1)} %get-tuple-element.20), channel_id=1, source_target_pairs={{1,3},{3,5},{5,7},{2,0},{4,2},{6,4},{9,11},{11,13},{13,15},{10,8},... | collective-permute-start | bytes 92168 | tf_op jit(solution)/shard_map/ppermute | solution.py:312
  37.0 15.6 %collective-permute-start.2 = (bf16[4,3840]{1,0:T(4,128)(2,1)S(1)}, bf16[4,3840]{1,0:T(4,128)(2,1)S(1)}, u32[]{:S(2)}, u32[]{:S(2)}) collective-permute-start(bf16[4,3840]{1,0:T(4,128)(2,1)S(1)} %get-tuple-element.21), channel_id=1, source_target_pairs={{1,2},{3,4},{5,6},{2,1},{4,3},{6,5},{9,10},{11,12},{13,14},{10,9},... | collective-permute-start | bytes 92168 | tf_op jit(solution)/shard_map/ppermute | solution.py:313
  71.0 17.9 %all-to-all-start = ((f32[32,1,160]{2,1,0:T(1,128)}), f32[32,1,160]{2,1,0:T(1,128)S(1)}, u32[]{:S(2)}, u32[]{:S(2)}) async-start(f32[32,1,160]{2,1,0:T(1,128)} %all_to_all.19), calls=%async_computation | async-start | bytes 65536 | tf_op jit(solution)/shard_map/all_to_all | solution.py:330
  89.6 23.8 %all-to-all-start.1 = ((f32[32,1,80]{2,1,0:T(1,128)}), f32[32,1,80]{2,1,0:T(1,128)S(1)}, u32[]{:S(2)}, u32[]{:S(2)}) async-start(f32[32,1,80]{2,1,0:T(1,128)} %bitcast.6), calls=%async_computation.1 | async-start | bytes 32768 | tf_op jit(solution)/shard_map/all_to_all | solution.py:332
  103.0 11.1 %collective-permute-start.6 = (bf16[128,1280]{1,0:T(8,128)(2,1)S(1)}, bf16[128,1280]{1,0:T(8,128)(2,1)S(1)}, u32[]{:S(2)}, u32[]{:S(2)}) collective-permute-start(bf16[128,1280]{1,0:T(8,128)(2,1)S(1)} %get-tuple-element.30), channel_id=1, source_target_pairs={{0,1},{1,0},{2,3},{3,2},{4,5},{5,4},{6,7},{7,6},{8,9},{9,8},{10,11... | collective-permute-start | bytes 983048 | tf_op jit(solution)/shard_map/ppermute | solution.py:343

commit v3 on v2

--- a/solution.py
+++ b/solution.py
@@ -86,7 +86,7 @@
         fill(1)
 
 
-def taps_kernel(scalars, w_ref, taps_ref):
+def taps_kernel(scalars, w_ref, fitting_ref, taps_ref):
     width = taps_ref.shape[1] // 4
     row = lax.broadcasted_iota(jnp.int32, (TAPS, width), 0)
     unit = jnp.where(row == 0, 1.0, 0.0).astype(F32)
@@ -139,7 +139,7 @@
             firsts.append(front * first_rows if group == LEFT else front)
             lasts.append(padded_ref[PRE + PAIR - 4 : PRE + PAIR, :])
         left, right = value_refs[(2 * head) % 4], value_refs[(2 * head + 1) % 4]
-        state = tn(left[...], right[...]).astype(BF16)
+        state = tn(right[...], left[...]).astype(BF16)
         firsts, lasts = jnp.concatenate(firsts, 0), jnp.concatenate(lasts, 0)
         for ref in (message_ref, wrap_ref):
             ref[head, 0:HEAD, :] = state
@@ -159,9 +159,38 @@
             out_ref[:, slot * width : (slot + 1) * width] = rows
 
 
+def products_kernel(
+    scalars, keep_ref, received_ref, taps_ref, after_ref, products_ref, fold_ref, rows_ref, *padded_refs
+):
+    core = scalars[0]
+    width = keep_ref.shape[1] // 4
+    for ref in padded_refs:
+        ref[0:PRE, :] = jnp.zeros((PRE, HEAD), F32)
+    row = lax.broadcasted_iota(jnp.int32, (PAIR, HEAD), 0)
+    for head in range(width // HEAD):
+        a_ref, raw_ref = (padded_refs[(2 * head + k) % 4] for k in range(2))
+        at = lanes(A, head, width)
+        gather_rows(core, keep_ref, received_ref, at, a_ref)
+        gather_rows(core, keep_ref, received_ref, lanes(RAW, head, width), raw_ref)
+        a = convolved(a_ref, taps_ref[:, at], PRE, PAIR)
+        a = jnp.where(row >= TAPS - 1, a, 0.0).astype(BF16)
+        for j in range(TAPS):
+            shifted = raw_ref[PRE - j : PRE - j + PAIR, :].astype(BF16)
+            products_ref[head, j] = tn(a, shifted) * (1.0 / HEAD)
+    few = width // 2 // rows_ref.shape[0]
+    place = lax.broadcasted_iota(jnp.int32, fold_ref.shape, 1)
+    column = lax.broadcasted_iota(jnp.int32, fold_ref.shape, 0)
+    place = lax.rem(place, fold_ref.shape[1] // 2)
+    fits = (lax.rem(column, few) == lax.rem(place, few)) & (place < TAPS * few)
+    fold_ref[...] = jnp.where(fits, 1.0, 0.0).astype(BF16)
+    device = lax.broadcasted_iota(jnp.int32, rows_ref.shape, 0) * few
+    column = lax.broadcasted_iota(jnp.int32, rows_ref.shape, 1)
+    rows_ref[...] = jnp.where((column >= device) & (column < device + few), 1.0, 0.0)
+
+
 def inside_kernel(
     scalars, keep_ref, received_ref, same_ref, cross_ref, taps_ref,
-    kept_ref, a_ref, raw_ref, left_tail_ref, b_tail_ref, *scratch,
+    kept_ref, a_ref, left_tail_ref, b_tail_ref, terms_ref, front_ref, *scratch,
 ):
     core = scalars[0]
     width = keep_ref.shape[1] // 4
@@ -195,7 +224,7 @@
             padded_ref[0:PRE, :] = jnp.concatenate([none, front], 0)
             padded_ref[PRE + PAIR : LONG, :] = jnp.concatenate([back, none], 0)
             if group == RAW:
-                raw_ref[:, to] = padded_ref[...]
+                raw_ref = padded_ref
                 continue
             taps = taps_ref[:, at]
             for first in (0, ROWS):
@@ -212,56 +241,89 @@
         a_ref[:, to] = a
         scores = (nt(a, b) * mask).astype(BF16)
         kept_ref[:, to] = nn(scores, left)
-
-
-def kept_kernel(
-    scalars, inside_ref, a_ref, raw_ref, left_tail_ref, b_tail_ref, near_ref, far_ref, wrap_ref,
-    taps_ref, kept_ref, terms_ref, edge_ref,
-):
-    core = scalars[0]
-    width = a_ref.shape[1]
-    row = lax.broadcasted_iota(jnp.int32, (8, HEAD), 0)
-    nothing = jnp.zeros((8, HEAD), F32)
-    for head in range(width // HEAD):
-        to = lanes(0, head, width)
-        near, far, wrap = (r[head, HEAD:, :].astype(F32) for r in (near_ref, far_ref, wrap_ref))
-        near = jnp.where(core == 0, near[0:EDGE], near[EDGE : 2 * EDGE])
-        first, last = far[0:EDGE], far[EDGE : 2 * EDGE]
-        rows = []
-        seams = []
-        for zero, one in (((last, near), (near, first)), ((wrap, first), (last, wrap))):
-            seams.append([jnp.where(core == 0, *pair) for pair in zip(zero, one)])
-        for group, at in ((LEFT, slice(0, 4)), (B, slice(4, 8))):
-            taps = taps_ref[:, lanes(group, head, width)]
-            for turn, seam in enumerate(seams):
-                part = edge_ref.at[2 * (group // 2) + turn]
-                part[0:8, :] = jnp.concatenate([seam[0][at], seam[1][at]], 0)
-                part[8:16, :] = nothing
-                total = convolved(part, taps, 4, 8)
-                rows.append(jnp.where(row < TAPS - 1, total, 0.0))
-        left = jnp.concatenate(rows[0:2], 0).astype(BF16)
-        right = jnp.concatenate(rows[2:4], 0).astype(BF16)
-        state = (
-            near_ref[head, 0:HEAD, :].astype(F32) + far_ref[head, 0:HEAD, :].astype(F32)
-            + wrap_ref[head, 0:HEAD, :].astype(F32)
-            + tn(left, right) + tn(left_tail_ref[:, to], b_tail_ref[:, to])
-        ).astype(BF16)
-        kept_ref[:, to] = inside_ref[:, to] + nt(a_ref[:, to], state) * (1.0 / HEAD)
+        front_ref[:, to] = raw_ref[0 : PRE + 8, :]
         sums = [jnp.zeros((8, HEAD), F32)] * TAPS
         for first in range(0, PAIR, 64):
             kept = kept_ref[first : first + 64, to]
             for j in range(TAPS):
                 start = PRE + first - j
-                term = kept * raw_ref[start : start + 64, to]
+                term = kept * raw_ref[start : start + 64, :]
                 sums[j] = sums[j] + jnp.sum(term.reshape(8, 8, HEAD), 0)
         terms_ref[:, to] = jnp.concatenate([jnp.sum(s, 0, keepdims=True) for s in sums], 0)
 
 
-def input_kernel(scalars, kept_ref, taps_ref, own_ref, send_ref, grad_ref):
+def terms_kernel(
+    scalars, terms_ref, products_ref, a_ref, front_ref, left_tail_ref, b_tail_ref,
+    near_ref, far_ref, wrap_ref, taps_ref, fold_ref, rows_ref,
+    states_ref, shares_ref, edge_ref, seam_ref, total_ref, stack_ref,
+):
+    core = scalars[0]
+    heads, width = products_ref.shape[0], terms_ref.shape[1]
+    none = jnp.zeros((8, HEAD), F32)
+    for head in range(heads):
+        to = lanes(0, head, width)
+        near, far, wrap = (r[head, HEAD:, :].astype(F32) for r in (near_ref, far_ref, wrap_ref))
+        near = jnp.where(core == 0, near[0:EDGE], near[EDGE : 2 * EDGE])
+        first, last = far[0:EDGE], far[EDGE : 2 * EDGE]
+        for turn, (zero, one) in enumerate((((last, near), (near, first)), ((wrap, first), (last, wrap)))):
+            before, after = (jnp.where(core == 0, *pair) for pair in zip(zero, one))
+            for slot, at in enumerate((slice(0, 4), slice(4, 8))):
+                edge_ref[2 * slot + turn, 0:8, to] = jnp.concatenate([before[at], after[at]], 0)
+                edge_ref[2 * slot + turn, 8:16, to] = none
+    row = lax.broadcasted_iota(jnp.int32, (8, width), 0)
+    for slot, group in enumerate((LEFT, B)):
+        taps = taps_ref[:, group * width : (group + 1) * width]
+        rows = [convolved(edge_ref.at[2 * slot + turn], taps, 4, 8) for turn in range(2)]
+        rows = [jnp.where(row < TAPS - 1, total, 0.0) for total in rows]
+        seam_ref[slot] = jnp.concatenate(rows, 0).astype(BF16)
+    row = lax.broadcasted_iota(jnp.int32, (8, HEAD), 0)
+    for head in range(heads):
+        to = lanes(0, head, width)
+        state = (
+            near_ref[head, 0:HEAD, :].astype(F32) + far_ref[head, 0:HEAD, :].astype(F32)
+            + wrap_ref[head, 0:HEAD, :].astype(F32)
+            + tn(seam_ref[1, :, to], seam_ref[0, :, to])
+            + tn(b_tail_ref[:, to], left_tail_ref[:, to])
+        ).astype(BF16)
+        states_ref[head] = state
+        front = nn(a_ref[0:16, to], state)[0:8] * (1.0 / HEAD)
+        front = jnp.where(row < TAPS - 1, front, 0.0)
+        state = state.astype(F32)
+        sums = []
+        for j in range(TAPS):
+            product = (state * products_ref[head, j]).reshape(HEAD // 8, 8, HEAD)
+            total = jnp.sum(product, 0) + front * front_ref[PRE - j : PRE - j + 8, to]
+            sums.append(jnp.sum(total, 0, keepdims=True))
+        total_ref[:, to] = terms_ref[:, to] + jnp.concatenate(sums, 0)
+    half = width // 2
+    spread = rows_ref.shape[0]
+    fitting = rows_ref[...]
+    for part in range(2):
+        for j in range(TAPS):
+            at = (part * TAPS + j) * spread
+            line = total_ref[j : j + 1, part * half : (part + 1) * half]
+            stack_ref[at : at + spread, :] = fitting * line
+    folded = nn(stack_ref[...].astype(BF16), fold_ref[...])
+    few = half // spread
+    place = lax.broadcasted_iota(jnp.int32, (spread, fold_ref.shape[1]), 1)
+    gathered = jnp.zeros((spread, fold_ref.shape[1]), F32)
+    for part in range(2):
+        for j in range(TAPS):
+            at = (part * TAPS + j) * spread
+            begin = part * (fold_ref.shape[1] // 2) + j * few
+            here = (place >= begin) & (place < begin + few)
+            gathered = gathered + jnp.where(here, folded[at : at + spread], 0.0)
+    shares_ref[...] = gathered.reshape(shares_ref.shape)
+
+
+def input_kernel(
+    scalars, inside_ref, a_ref, states_ref, taps_ref, after_ref, own_ref, send_ref, grad_ref, kept_ref
+):
     core = scalars[0]
     width = own_ref.shape[1]
     for head in range(width // HEAD):
         to = lanes(0, head, width)
+        kept_ref[:, to] = inside_ref[:, to] + nn(a_ref[:, to], states_ref[head]) * (1.0 / HEAD)
         taps = taps_ref[:, lanes(RAW, head, width)]
         for first in range(0, PAIR, 64):
             grad = taps[0:1] * kept_ref[first : first + 64, to]
@@ -279,6 +341,7 @@
     chips = lax.axis_size("zh")
     core, chip, low = lax.axis_index("core"), lax.axis_index("zh"), lax.axis_index("zl")
     scalars = jnp.stack([core, chip]).astype(jnp.int32)
+    fitting = (jnp.arange(8 * chips) // (4 * chips) == low // 2).astype(F32)[:, None]
     swap = [(0, 1), (1, 0)]
     line = ("zh", "core")
 
@@ -294,7 +357,7 @@
         pack_kernel, [((ROWS, 4 * width), BF16)] * 2, [pltpu.SemaphoreType.DMA((8,))],
         scalars, x, g, space=pl.BlockSpec(memory_space=pl.ANY), limit=8,
     )
-    (taps,) = call(taps_kernel, [((TAPS, 4 * width), F32)], [], scalars, conv_weight)
+    (taps,) = call(taps_kernel, [((TAPS, 4 * width), F32)], [], scalars, conv_weight, fitting)
     received = lax.ppermute(send, "core", swap)
     padded = [pltpu.VMEM((LONG, HEAD), F32)] * 4
     message, wrap = call(
@@ -311,35 +374,45 @@
     wrap = lax.ppermute(wrap, line, hops(3))
     same = lax.ppermute(same, line, to_same)
     cross = lax.ppermute(cross, line, to_cross)
-    inside, a, raw, left_tail, b_tail = call(
+    spread = lax.axis_size("yx")
+    few = width // 2 // spread
+    part = -(-TAPS * few // HEAD) * HEAD
+    tail = ((16, width), BF16)
+    products, fold, rows = call(
+        products_kernel,
+        [
+            ((heads, TAPS, HEAD, HEAD), F32), ((width // 2, 2 * part), BF16),
+            ((spread, width // 2), F32),
+        ],
+        padded, scalars, keep, received, taps, message,
+    )
+    inside, a, left_tail, b_tail, terms, front = call(
         inside_kernel,
-        [((EXT, width), F32), ((EXT, width), BF16), ((LONG, width), F32)]
-        + [((16, width), BF16)] * 2,
+        [
+            ((EXT, width), F32), ((EXT, width), BF16), tail, tail, ((TAPS, width), F32),
+            ((PRE + 8, width), F32),
+        ],
         padded + [pltpu.VMEM((EXT, HEAD), BF16)] * 4,
         scalars, keep, received, same, cross, taps,
     )
-    kept, terms = call(
-        kept_kernel, [((EXT, width), F32), ((TAPS, width), F32)],
-        [pltpu.VMEM((4, 16, HEAD), F32)],
-        scalars, inside, a, raw, left_tail, b_tail, near, far, wrap, taps,
-    )
-
-    spread = lax.axis_size("yx")
-    few = width // 2 // spread
-    rows = terms.reshape(TAPS, 2, spread, few).transpose(2, 1, 0, 3).reshape(spread, 2 * TAPS * few)
-    summed = jnp.sum(lax.all_to_all(rows, "yx", 0, 0, tiled=True), 0).reshape(2, TAPS * few)
-    rows = jnp.broadcast_to(summed[None, None, :, None], (2, 2, 2, chips, TAPS * few))
-    rows = lax.all_to_all(
-        rows.reshape(8 * chips, TAPS * few), ("core", "zl", "zh"), 0, 0, tiled=True
-    )
-    fitting = (jnp.arange(8 * chips) // (4 * chips) == low // 2)[:, None]
-    share = jnp.sum(jnp.where(fitting, rows, 0.0), 0).reshape(TAPS, few)
-    shares = share / (lax.axis_size("zl") * spread)
-
+    states, rows = call(
+        terms_kernel, [((heads, HEAD, HEAD), BF16), ((spread, 1, 2 * part), F32)],
+        [
+            pltpu.VMEM((4, 16, width), F32), pltpu.VMEM((2, 16, width), BF16),
+            pltpu.VMEM((TAPS, width), F32), pltpu.VMEM((2 * TAPS * spread, width // 2), F32),
+        ],
+        scalars, terms, products, a, front, left_tail, b_tail, near, far, wrap, taps, fold, rows,
+    )
+    rows = jnp.sum(lax.all_to_all(rows, "yx", 0, 0, tiled=True), (0, 1)).reshape(2, part)
+    rows = jnp.broadcast_to(rows[None, None, :, None], (2, 2, 2, chips, part)).reshape(8 * chips, part)
     own, sent = call(
-        input_kernel, [((ROWS, width), BF16)] * 2, [pltpu.VMEM((PAIR, width), BF16)],
-        scalars, kept, taps,
-    )
+        input_kernel, [((ROWS, width), BF16)] * 2,
+        [pltpu.VMEM((PAIR, width), BF16), pltpu.VMEM((EXT, width), F32)],
+        scalars, inside, a, states, taps, rows,
+    )
+    rows = lax.all_to_all(rows, ("core", "zl", "zh"), 0, 0, tiled=True)
+    share = jnp.sum(rows * fitting, 0)[: TAPS * few].reshape(TAPS, few)
+    shares = share * (1.0 / (lax.axis_size("zl") * spread))
     other = lax.ppermute(sent, "core", swap)
     first, second = jnp.where(core == 0, own, other), jnp.where(core == 0, other, own)
     return jnp.concatenate([first, second], 1)[None], shares

time: 116 us -> 117 us (level)
  Pallas kernels: 10.8 us -> 16.3 us
  waiting for transfers between devices: 33.9 us -> 28.8 us
    ppermute x1, waiting for transfers between devices: 11.3 us -> 5.64 us  [per_device(): wrap = lax.ppermute(wrap, line, hops(3))]
    pallas_call x7 -> x8, Pallas kernels: 10.8 us -> 16.3 us  [call(): pl.pallas_call(kernel, out_shape=[jax.ShapeDtypeStruct(s, t) for s, t in...]
    ppermute x1, waiting for transfers between devices: 2.87 us -> 4.49 us  [per_device(): cross = lax.ppermute(cross, line, to_cross)]
    unnamed x6 -> x10, local copies, waits for them, and re-layouts: 2.64 us -> 3.73 us
  transfers between devices with their start and end apart: 9 -> 9, of which waited for: 6 -> 5; matrix products, arithmetic and copies ran while one was open for 1% -> 1% of each run, Pallas kernels for 5% -> 8%
where the time goes in v3:
time: 117 us
  starting transfers between devices  64.5 us (55%)
  waiting for transfers between devices  28.8 us (25%)
  Pallas kernels  16.3 us (14%)
  local copies, waits for them, and re-layouts  5 us (4%)
  other arithmetic  1.17 us (1%)
    pallas_call x8, Pallas kernels, call(): pl.pallas_call(kernel, out_shape=[jax.ShapeDtypeStruct(s, t) for s, t in...  16.3 us
    ppermute x1, starting transfers between devices, per_device(): received = lax.ppermute(send, 'core', swap)  16.1 us
    ppermute x1, starting transfers between devices, per_device(): cross = lax.ppermute(cross, line, to_cross)  12.7 us
    all_to_all x1, starting transfers between devices, per_device(): rows = lax.all_to_all(rows, ('core', 'zl', 'zh'), 0, 0, tiled=True)  12.6 us
    all_to_all x1, starting transfers between devices, per_device(): lax.all_to_all(rows, 'yx', 0, 0, tiled=True)  9.85 us
    all_to_all x1, waiting for transfers between devices, per_device(): lax.all_to_all(rows, 'yx', 0, 0, tiled=True)  8.69 us
    all_to_all x1, waiting for transfers between devices, per_device(): rows = lax.all_to_all(rows, ('core', 'zl', 'zh'), 0, 0, tiled=True)  7.72 us
    ppermute x1, starting transfers between devices, per_device(): same = lax.ppermute(same, line, to_same)  7.29 us
  transfers between devices with their start and end apart: 9, of which 5 were waited for; matrix products, arithmetic and copies ran while one was open for 1% of the time, Pallas kernels for 8%

profile of v3, /device:TPU:1, one launch (start us, length us, event | category | flops | bytes accessed | tf_op | source)
XLA Modules:
  0.0 116.6 jit_solution(7408098742289940604)
XLA Ops:
  0.6 0.1 pad_add_fusion.scalars
  0.7 0.0 copy-start
  0.7 1.5 %copy-done = bf16[1,128,7680]{2,1,0:T(8,128)(2,1)S(1)} copy-done((bf16[1,128,7680]{2,1,0:T(8,128)(2,1)S(1)}, bf16[1,128,7680]{2,1,0:T(8,128)(2,1)}, u32[]{:S(2)}) %copy-start) | copy-done | bytes 1966104
  2.3 0.0 copy-start.3
  2.3 1.1 copy-done.3
  3.3 0.0 copy-start.4
  3.3 1.9 %shard_map.50 = (bf16[128,5120]{1,0:T(8,128)(2,1)S(1)}, bf16[128,5120]{1,0:T(8,128)(2,1)}) custom-call(s32[2]{0:T(128)S(1)} %pad_add_fusion.scalars, bf16[128,7680]{1,0:T(8,128)(2,1)S(1)} %bitcast.10, bf16[128,2560]{1,0:T(8,128)(2,1)S(1)} %bitcast.11), custom_call_target="tpu_custom_call" | custom-call | tf_op jit(solution)/shard_map/pallas_call | solution.py:25
  5.3 16.1 %collective-permute-start = (bf16[128,5120]{1,0:T(8,128)(2,1)}, bf16[128,5120]{1,0:T(8,128)(2,1)S(1)}, u32[]{:S(2)}, u32[]{:S(2)}) collective-permute-start(bf16[128,5120]{1,0:T(8,128)(2,1)} %get-tuple-element.22.send_ref), channel_id=1, source_target_pairs={{0,1},{1,0},{2,3},{3,2},{4,5},{5,4},{6,7},{7,6},{8,9},{9,8},{10,11... | collective-permute-start | bytes 3932168 | tf_op jit(solution)/shard_map/ppermute | solution.py:361
  21.4 0.0 copy-done.4
  21.4 0.6 shard_map.51.taps_ref
  22.0 2.2 %collective-permute-done.received_ref = bf16[128,5120]{1,0:T(8,128)(2,1)S(1)} collective-permute-done((bf16[128,5120]{1,0:T(8,128)(2,1)}, bf16[128,5120]{1,0:T(8,128)(2,1)S(1)}, u32[]{:S(2)}, u32[]{:S(2)}) %collective-permute-start) | collective-permute-done | bytes 1310752 | tf_op jit(solution)/shard_map/ppermute | solution.py:361
  24.2 2.1 %shard_map.52 = (bf16[10,144,128]{2,1,0:T(8,128)(2,1)S(1)}, bf16[10,136,128]{2,1,0:T(8,128)(2,1)S(1)}) custom-call(s32[2]{0:T(128)S(1)} %pad_add_fusion.scalars, bf16[128,5120]{1,0:T(8,128)(2,1)S(1)} %get-tuple-element.21.keep_ref, bf16[128,5120]{1,0:T(8,128)(2,1)S(1)} %collective-permute-done.received_ref, f32[4,5120]{1,0:T(4,128)S(1)} %shard_map.51.taps_ref), custom_call_target="tpu_custom_call" | custom-call | tf_op jit(solution)/shard_map/pallas_call | solution.py:25
  26.3 1.3 %collective-permute-start.3 = (bf16[10,144,128]{2,1,0:T(8,128)(2,1)S(1)}, bf16[10,144,128]{2,1,0:T(8,128)(2,1)S(1)}, u32[]{:S(2)}, u32[]{:S(2)}) collective-permute-start(bf16[10,144,128]{2,1,0:T(8,128)(2,1)S(1)} %get-tuple-element.23.message_ref.after_ref), channel_id=1, source_target_pairs={{0,2},{2,4},{4,6},{3,1},{5,3},{7,5},{8,10},{10,12},{12,14},{11,9},... | collective-permute-start | bytes 1105928 | tf_op jit(solution)/shard_map/ppermute | solution.py:372
  27.6 1.3 %collective-permute-start.4 = (bf16[10,144,128]{2,1,0:T(8,128)(2,1)S(1)}, bf16[10,144,128]{2,1,0:T(8,128)(2,1)S(1)}, u32[]{:S(2)}, u32[]{:S(2)}) collective-permute-start(bf16[10,144,128]{2,1,0:T(8,128)(2,1)S(1)} %get-tuple-element.23.message_ref.after_ref), channel_id=1, source_target_pairs={{0,4},{2,6},{5,1},{7,3},{8,12},{10,14},{13,9},{15,11},{16,20},{18,... | collective-permute-start | bytes 1105928 | tf_op jit(solution)/shard_map/ppermute | solution.py:373
  28.9 1.3 %collective-permute-start.5 = (bf16[10,136,128]{2,1,0:T(8,128)(2,1)S(1)}, bf16[10,136,128]{2,1,0:T(8,128)(2,1)S(1)}, u32[]{:S(2)}, u32[]{:S(2)}) collective-permute-start(bf16[10,136,128]{2,1,0:T(8,128)(2,1)S(1)} %get-tuple-element.33), channel_id=1, source_target_pairs={{0,6},{7,1},{8,14},{15,9},{16,22},{23,17},{24,30},{31,25},{32,38},... | collective-permute-start | bytes 1044488 | tf_op jit(solution)/shard_map/ppermute | solution.py:374
  30.2 1.4 %shard_map.53 = (bf16[4,3840]{1,0:T(4,128)(2,1)S(1)}, bf16[4,3840]{1,0:T(4,128)(2,1)S(1)}) custom-call(s32[2]{0:T(128)S(1)} %pad_add_fusion.scalars, bf16[128,5120]{1,0:T(8,128)(2,1)S(1)} %get-tuple-element.21.keep_ref, bf16[128,5120]{1,0:T(8,128)(2,1)} %get-tuple-element.22.send_ref, bf16[10,144,128]{2,1,0:T(8,128)(2,1)S(1)} %get-tuple-element.23.message_ref.after_ref), custom_call_target="tpu_custom_call" | custom-call | tf_op jit(solution)/shard_map/pallas_call | solution.py:25
  31.6 7.3 %collective-permute-start.1 = (bf16[4,3840]{1,0:T(4,128)(2,1)S(1)}, bf16[4,3840]{1,0:T(4,128)(2,1)S(1)}, u32[]{:S(2)}, u32[]{:S(2)}) collective-permute-start(bf16[4,3840]{1,0:T(4,128)(2,1)S(1)} %get-tuple-element.24), channel_id=1, source_target_pairs={{1,3},{3,5},{5,7},{2,0},{4,2},{6,4},{9,11},{11,13},{13,15},{10,8},... | collective-permute-start | bytes 92168 | tf_op jit(solution)/shard_map/ppermute | solution.py:375
  38.9 12.7 %collective-permute-start.2 = (bf16[4,3840]{1,0:T(4,128)(2,1)S(1)}, bf16[4,3840]{1,0:T(4,128)(2,1)S(1)}, u32[]{:S(2)}, u32[]{:S(2)}) collective-permute-start(bf16[4,3840]{1,0:T(4,128)(2,1)S(1)} %get-tuple-element.25), channel_id=1, source_target_pairs={{1,2},{3,4},{5,6},{2,1},{4,3},{6,5},{9,10},{11,12},{13,14},{10,9},... | collective-permute-start | bytes 92168 | tf_op jit(solution)/shard_map/ppermute | solution.py:376
  51.6 1.9 %shard_map.55 = (f32[10,4,128,128]{3,2,1,0:T(8,128)S(1)}, bf16[640,256]{1,0:T(8,128)(2,1)S(1)}, f32[32,640]{1,0:T(8,128)S(1)}) custom-call(s32[2]{0:T(128)S(1)} %pad_add_fusion.scalars, bf16[128,5120]{1,0:T(8,128)(2,1)S(1)} %get-tuple-element.21.keep_ref, bf16[128,5120]{1,0:T(8,128)(2,1)S(1)} %collective-permute-done.received_ref, ...), custom_call_target="tpu_custom_call" | custom-call | tf_op jit(solution)/shard_map/pallas_call | solution.py:25
  53.5 0.0 collective-permute-done.1.same_ref
  53.5 4.5 %collective-permute-done.2.cross_ref = bf16[4,3840]{1,0:T(4,128)(2,1)S(1)} collective-permute-done((bf16[4,3840]{1,0:T(4,128)(2,1)S(1)}, bf16[4,3840]{1,0:T(4,128)(2,1)S(1)}, u32[]{:S(2)}, u32[]{:S(2)}) %collective-permute-start.2) | collective-permute-done | bytes 30752 | tf_op jit(solution)/shard_map/ppermute | solution.py:376
  58.0 3.5 %shard_map.54 = (f32[272,1280]{1,0:T(8,128)S(1)}, bf16[272,1280]{1,0:T(8,128)(2,1)S(1)}, bf16[16,1280]{1,0:T(8,128)(2,1)S(1)}, bf16[16,1280]{1,0:T(8,128)(2,1)S(...) custom-call(s32[2]{0:T(128)S(1)} %pad_add_fusion.scalars, bf16[128,5120]{1,0:T(8,128)(2,1)S(1)} %get-tuple-element.21.keep_ref, ...), custom_call_target="tpu_custom_call" | custom-call | tf_op jit(solution)/shard_map/pallas_call | solution.py:25
  61.5 0.0 copy-start.1
  61.5 1.1 copy-done.1
  62.6 5.6 %collective-permute-done.5.wrap_ref = bf16[10,136,128]{2,1,0:T(8,128)(2,1)S(1)} collective-permute-done((bf16[10,136,128]{2,1,0:T(8,128)(2,1)S(1)}, bf16[10,136,128]{2,1,0:T(8,128)(2,1)S(1)}, u32[]{:S(2)}, u32[]{:S(2)}) %collective-permute-start.5) | collective-permute-done | bytes 348192 | tf_op jit(solution)/shard_map/ppermute | solution.py:374
  68.2 0.0 collective-permute-done.3.near_ref
  68.2 0.0 collective-permute-done.4.far_ref
  68.2 0.0 copy-start.2
  68.2 3.2 %shard_map.56 = (bf16[10,128,128]{2,1,0:T(8,128)(2,1)S(1)}, f32[32,1,256]{2,1,0:T(1,128)}) custom-call(s32[2]{0:T(128)S(1)} %pad_add_fusion.scalars, f32[4,1280]{1,0:T(4,128)S(1)} %get-tuple-element.28.terms_ref, f32[10,4,128,128]{3,2,1,0:T(8,128)S(1)} %get-tuple-element.29.products_ref, bf16[272,1280]{1,0:T(8,128)(2,1)S(1)} %get-tuple-element.27.a_ref, ...), custom_call_target="tpu_custom_call" | custom-call | tf_op jit(solution)/shard_map/pallas_call | solution.py:25
  71.4 9.8 %all-to-all-start = ((f32[32,1,256]{2,1,0:T(1,128)}), f32[32,1,256]{2,1,0:T(1,128)S(1)}, u32[]{:S(2)}, u32[]{:S(2)}) async-start(f32[32,1,256]{2,1,0:T(1,128)} %get-tuple-element.37), calls=%async_computation | async-start | bytes 65536 | tf_op jit(solution)/shard_map/all_to_all | solution.py:406
  81.3 8.7 %all-to-all-done = f32[32,1,256]{2,1,0:T(1,128)S(1)} async-done(((f32[32,1,256]{2,1,0:T(1,128)}), f32[32,1,256]{2,1,0:T(1,128)S(1)}, u32[]{:S(2)}, u32[]{:S(2)}) %all-to-all-start) | async-done | bytes 32800 | tf_op jit(solution)/shard_map/all_to_all | solution.py:406
  90.0 0.1 reduce_sum.18
  90.0 0.6 broadcast_in_dim.12
  90.6 12.6 %all-to-all-start.1 = ((f32[32,1,128]{2,1,0:T(1,128)}), f32[32,1,128]{2,1,0:T(1,128)S(1)}, u32[]{:S(2)}, u32[]{:S(2)}) async-start(f32[32,1,128]{2,1,0:T(1,128)} %bitcast.7), calls=%async_computation.1 | async-start | bytes 32768 | tf_op jit(solution)/shard_map/all_to_all | solution.py:413
  103.3 0.0 copy-done.2
  103.3 1.7 %shard_map.57 = (bf16[128,1280]{1,0:T(8,128)(2,1)S(1)}, bf16[128,1280]{1,0:T(8,128)(2,1)S(1)}) custom-call(s32[2]{0:T(128)S(1)} %pad_add_fusion.scalars, f32[272,1280]{1,0:T(8,128)S(1)} %copy-done.2, bf16[272,1280]{1,0:T(8,128)(2,1)S(1)} %get-tuple-element.27.a_ref, bf16[10,128,128]{2,1,0:T(8,128)(2,1)S(1)} %get-tuple-element.36.states_ref, ...), custom_call_target="tpu_custom_call" | custom-call | tf_op jit(solution)/shard_map/pallas_call | solution.py:25
  105.0 2.1 %collective-permute-start.6 = (bf16[128,1280]{1,0:T(8,128)(2,1)S(1)}, bf16[128,1280]{1,0:T(8,128)(2,1)S(1)}, u32[]{:S(2)}, u32[]{:S(2)}) collective-permute-start(bf16[128,1280]{1,0:T(8,128)(2,1)S(1)} %get-tuple-element.39), channel_id=1, source_target_pairs={{0,1},{1,0},{2,3},{3,2},{4,5},{5,4},{6,7},{7,6},{8,9},{9,8},{10,11... | collective-permute-start | bytes 983048 | tf_op jit(solution)/shard_map/ppermute | solution.py:416
  107.2 7.7 %all-to-all-done.1 = f32[32,1,128]{2,1,0:T(1,128)S(1)} async-done(((f32[32,1,128]{2,1,0:T(1,128)}), f32[32,1,128]{2,1,0:T(1,128)S(1)}, u32[]{:S(2)}, u32[]{:S(2)}) %all-to-all-start.1) | async-done | bytes 16416 | tf_op jit(solution)/shard_map/all_to_all | solution.py:413
  114.9 0.1 multiply_reduce_fusion
  115.0 0.7 mul.21
  115.6 0.0 collective-permute-done.6
  115.7 0.9 maximum_bitcast_fusion
  (4 shorter events, 0.1 us)
Async XLA Ops:
  0.7 1.5 %copy-start = (bf16[1,128,7680]{2,1,0:T(8,128)(2,1)S(1)}, bf16[1,128,7680]{2,1,0:T(8,128)(2,1)}, u32[]{:S(2)}) copy-start(bf16[1,128,7680]{2,1,0:T(8,128)(2,1)} %param.3) | copy-start | bytes 5898244
  2.3 1.1 copy-start.3
  3.3 18.0 %copy-start.4 = (f32[4,7680]{1,0:T(4,128)S(1)}, f32[4,7680]{1,0:T(4,128)}, u32[]{:S(2)}) copy-start(f32[4,7680]{1,0:T(4,128)} %w_ref.1) | copy-start | bytes 368644
  5.3 18.9 %collective-permute-start = (bf16[128,5120]{1,0:T(8,128)(2,1)}, bf16[128,5120]{1,0:T(8,128)(2,1)S(1)}, u32[]{:S(2)}, u32[]{:S(2)}) collective-permute-start(bf16[128,5120]{1,0:T(8,128)(2,1)} %get-tuple-element.22.send_ref), channel_id=1, source_target_pairs={{0,1},{1,0},{2,3},{3,2},{4,5},{5,4},{6,7},{7,6},{8,9},{9,8},{10,11... | collective-permute-start | bytes 3932168 | tf_op jit(solution)/shard_map/ppermute | solution.py:361
  26.3 41.9 %collective-permute-start.3 = (bf16[10,144,128]{2,1,0:T(8,128)(2,1)S(1)}, bf16[10,144,128]{2,1,0:T(8,128)(2,1)S(1)}, u32[]{:S(2)}, u32[]{:S(2)}) collective-permute-start(bf16[10,144,128]{2,1,0:T(8,128)(2,1)S(1)} %get-tuple-element.23.message_ref.after_ref), channel_id=1, source_target_pairs={{0,2},{2,4},{4,6},{3,1},{5,3},{7,5},{8,10},{10,12},{12,14},{11,9},... | collective-permute-start | bytes 1105928 | tf_op jit(solution)/shard_map/ppermute | solution.py:372
  27.6 40.6 %collective-permute-start.4 = (bf16[10,144,128]{2,1,0:T(8,128)(2,1)S(1)}, bf16[10,144,128]{2,1,0:T(8,128)(2,1)S(1)}, u32[]{:S(2)}, u32[]{:S(2)}) collective-permute-start(bf16[10,144,128]{2,1,0:T(8,128)(2,1)S(1)} %get-tuple-element.23.message_ref.after_ref), channel_id=1, source_target_pairs={{0,4},{2,6},{5,1},{7,3},{8,12},{10,14},{13,9},{15,11},{16,20},{18,... | collective-permute-start | bytes 1105928 | tf_op jit(solution)/shard_map/ppermute | solution.py:373
  28.9 39.3 %collective-permute-start.5 = (bf16[10,136,128]{2,1,0:T(8,128)(2,1)S(1)}, bf16[10,136,128]{2,1,0:T(8,128)(2,1)S(1)}, u32[]{:S(2)}, u32[]{:S(2)}) collective-permute-start(bf16[10,136,128]{2,1,0:T(8,128)(2,1)S(1)} %get-tuple-element.33), channel_id=1, source_target_pairs={{0,6},{7,1},{8,14},{15,9},{16,22},{23,17},{24,30},{31,25},{32,38},... | collective-permute-start | bytes 1044488 | tf_op jit(solution)/shard_map/ppermute | solution.py:374
  31.6 21.9 %collective-permute-start.1 = (bf16[4,3840]{1,0:T(4,128)(2,1)S(1)}, bf16[4,3840]{1,0:T(4,128)(2,1)S(1)}, u32[]{:S(2)}, u32[]{:S(2)}) collective-permute-start(bf16[4,3840]{1,0:T(4,128)(2,1)S(1)} %get-tuple-element.24), channel_id=1, source_target_pairs={{1,3},{3,5},{5,7},{2,0},{4,2},{6,4},{9,11},{11,13},{13,15},{10,8},... | collective-permute-start | bytes 92168 | tf_op jit(solution)/shard_map/ppermute | solution.py:375
  38.9 19.1 %collective-permute-start.2 = (bf16[4,3840]{1,0:T(4,128)(2,1)S(1)}, bf16[4,3840]{1,0:T(4,128)(2,1)S(1)}, u32[]{:S(2)}, u32[]{:S(2)}) collective-permute-start(bf16[4,3840]{1,0:T(4,128)(2,1)S(1)} %get-tuple-element.25), channel_id=1, source_target_pairs={{1,2},{3,4},{5,6},{2,1},{4,3},{6,5},{9,10},{11,12},{13,14},{10,9},... | collective-permute-start | bytes 92168 | tf_op jit(solution)/shard_map/ppermute | solution.py:376
  61.5 1.1 copy-start.1
  68.2 35.0 %copy-start.2 = (f32[272,1280]{1,0:T(8,128)S(1)}, f32[272,1280]{1,0:T(8,128)}, u32[]{:S(2)}) copy-start(f32[272,1280]{1,0:T(8,128)} %copy-done.1) | copy-start | bytes 4177924
  71.4 18.6 %all-to-all-start = ((f32[32,1,256]{2,1,0:T(1,128)}), f32[32,1,256]{2,1,0:T(1,128)S(1)}, u32[]{:S(2)}, u32[]{:S(2)}) async-start(f32[32,1,256]{2,1,0:T(1,128)} %get-tuple-element.37), calls=%async_computation | async-start | bytes 65536 | tf_op jit(solution)/shard_map/all_to_all | solution.py:406
  90.6 24.2 %all-to-all-start.1 = ((f32[32,1,128]{2,1,0:T(1,128)}), f32[32,1,128]{2,1,0:T(1,128)S(1)}, u32[]{:S(2)}, u32[]{:S(2)}) async-start(f32[32,1,128]{2,1,0:T(1,128)} %bitcast.7), calls=%async_computation.1 | async-start | bytes 32768 | tf_op jit(solution)/shard_map/all_to_all | solution.py:413
  105.0 10.6 %collective-permute-start.6 = (bf16[128,1280]{1,0:T(8,128)(2,1)S(1)}, bf16[128,1280]{1,0:T(8,128)(2,1)S(1)}, u32[]{:S(2)}, u32[]{:S(2)}) collective-permute-start(bf16[128,1280]{1,0:T(8,128)(2,1)S(1)} %get-tuple-element.39), channel_id=1, source_target_pairs={{0,1},{1,0},{2,3},{3,2},{4,5},{5,4},{6,7},{7,6},{8,9},{9,8},{10,11... | collective-permute-start | bytes 983048 | tf_op jit(solution)/shard_map/ppermute | solution.py:416

commit v4 on v3

--- a/solution.py
+++ b/solution.py
@@ -21,7 +21,7 @@
 SMEM = pl.BlockSpec(memory_space=pltpu.SMEM)
 
 
-def call(kernel, shapes, scratch, scalars, *arrays, space=VMEM, limit=32):
+def call(kernel, shapes, scratch, scalars, *arrays, space=VMEM, limit=16):
     return pl.pallas_call(
         kernel,
         out_shape=[jax.ShapeDtypeStruct(s, t) for s, t in shapes],
@@ -48,7 +48,18 @@
     return slice(group * width + head * HEAD, group * width + (head + 1) * HEAD)
 
 
-def pack_kernel(scalars, x_ref, g_ref, keep_ref, send_ref, sems):
+def fill_edges(core, keep_ref, send_ref, same_ref, cross_ref):
+    width = keep_ref.shape[1] // 4
+    edge = pl.ds(pl.multiple_of(core * (ROWS - 16), 16), 16)
+    for ref, out_ref, later in ((keep_ref, same_ref, A), (send_ref, cross_ref, B)):
+        for slot, (first, last) in enumerate(((LEFT, LEFT), (A, later), (B, RAW))):
+            zero = ref[edge, first * width : (first + 1) * width].astype(F32)[0:4]
+            one = ref[edge, last * width : (last + 1) * width].astype(F32)[12:16]
+            rows = jnp.where(core == 1, one, zero).astype(BF16)
+            out_ref[:, slot * width : (slot + 1) * width] = rows
+
+
+def pack_kernel(scalars, x_ref, g_ref, keep_ref, send_ref, same_ref, cross_ref, sems):
     core = scalars[0]
     width = keep_ref.shape[1] // 4
     of_core = (
@@ -84,6 +95,8 @@
     @pl.when(core == 1)
     def _():
         fill(1)
+
+    fill_edges(core, keep_ref, send_ref, same_ref, cross_ref)
 
 
 def taps_kernel(scalars, w_ref, fitting_ref, taps_ref):
@@ -147,16 +160,9 @@
         wrap_ref[head, HEAD:, :] = jnp.where(core == 0, lasts, firsts).astype(BF16)
 
 
-def edge_rows_kernel(scalars, keep_ref, send_ref, message_ref, same_ref, cross_ref):
-    core = scalars[0]
-    width = keep_ref.shape[1] // 4
-    edge = pl.ds(pl.multiple_of(core * (ROWS - 16), 16), 16)
-    for ref, out_ref, later in ((keep_ref, same_ref, A), (send_ref, cross_ref, B)):
-        for slot, (first, last) in enumerate(((LEFT, LEFT), (A, later), (B, RAW))):
-            zero = ref[edge, first * width : (first + 1) * width].astype(F32)[0:4]
-            one = ref[edge, last * width : (last + 1) * width].astype(F32)[12:16]
-            rows = jnp.where(core == 1, one, zero).astype(BF16)
-            out_ref[:, slot * width : (slot + 1) * width] = rows
+def hold_kernel(scalars, same_ref, cross_ref, after_ref, same_out_ref, cross_out_ref):
+    same_out_ref[...] = same_ref[...]
+    cross_out_ref[...] = cross_ref[...]
 
 
 def products_kernel(
@@ -271,24 +277,24 @@
                 edge_ref[2 * slot + turn, 0:8, to] = jnp.concatenate([before[at], after[at]], 0)
                 edge_ref[2 * slot + turn, 8:16, to] = none
     row = lax.broadcasted_iota(jnp.int32, (8, width), 0)
-    for slot, group in enumerate((LEFT, B)):
+    for slot, group, tail_ref in ((0, LEFT, left_tail_ref), (1, B, b_tail_ref)):
         taps = taps_ref[:, group * width : (group + 1) * width]
         rows = [convolved(edge_ref.at[2 * slot + turn], taps, 4, 8) for turn in range(2)]
         rows = [jnp.where(row < TAPS - 1, total, 0.0) for total in rows]
-        seam_ref[slot] = jnp.concatenate(rows, 0).astype(BF16)
+        seam_ref[slot, 0:16, :] = jnp.concatenate(rows, 0).astype(BF16)
+        seam_ref[slot, 16:32, :] = tail_ref[...]
+    every = [(head, lanes(0, head, width)) for head in range(heads)]
+    seams = [tn(seam_ref[1, :, to], seam_ref[0, :, to]) for _, to in every]
+    states = []
+    for (head, _), seam in zip(every, seams):
+        near, far, wrap = (r[head, 0:HEAD, :].astype(F32) for r in (near_ref, far_ref, wrap_ref))
+        states.append((near + far + (wrap + seam)).astype(BF16))
+    fronts = [nn(a_ref[0:16, to], state) for (_, to), state in zip(every, states)]
     row = lax.broadcasted_iota(jnp.int32, (8, HEAD), 0)
-    for head in range(heads):
-        to = lanes(0, head, width)
-        state = (
-            near_ref[head, 0:HEAD, :].astype(F32) + far_ref[head, 0:HEAD, :].astype(F32)
-            + wrap_ref[head, 0:HEAD, :].astype(F32)
-            + tn(seam_ref[1, :, to], seam_ref[0, :, to])
-            + tn(b_tail_ref[:, to], left_tail_ref[:, to])
-        ).astype(BF16)
+    for (head, to), state, front in zip(every, states, fronts):
         states_ref[head] = state
-        front = nn(a_ref[0:16, to], state)[0:8] * (1.0 / HEAD)
-        front = jnp.where(row < TAPS - 1, front, 0.0)
         state = state.astype(F32)
+        front = jnp.where(row < TAPS - 1, front[0:8] * (1.0 / HEAD), 0.0)
         sums = []
         for j in range(TAPS):
             product = (state * products_ref[head, j]).reshape(HEAD // 8, 8, HEAD)
@@ -334,6 +340,16 @@
     send_ref[...] = grad_ref[pl.ds(pl.multiple_of((1 - core) * ROWS, ROWS), ROWS), :]
 
 
+def join_kernel(scalars, own_ref, other_ref, out_ref):
+    width = own_ref.shape[1]
+    for core, parts in enumerate(((own_ref, other_ref), (other_ref, own_ref))):
+
+        @pl.when(scalars[0] == core)
+        def _():
+            for half, part in enumerate(parts):
+                out_ref[:, half * width : (half + 1) * width] = part[...]
+
+
 def per_device(qkv_input, conv_weight, out_cotangent):
     x, g = qkv_input[0], out_cotangent[0]
     width = g.shape[1] // 2
@@ -353,8 +369,9 @@
     to_same = [(2 * c + 1, 2 * c + 3) for c in pairs] + [(2 * c + 2, 2 * c) for c in pairs]
     to_cross = [(2 * c + 1, 2 * c + 2) for c in pairs] + [(2 * c + 2, 2 * c + 1) for c in pairs]
 
-    keep, send = call(
-        pack_kernel, [((ROWS, 4 * width), BF16)] * 2, [pltpu.SemaphoreType.DMA((8,))],
+    keep, send, same, cross = call(
+        pack_kernel, [((ROWS, 4 * width), BF16)] * 2 + [((4, 3 * width), BF16)] * 2,
+        [pltpu.SemaphoreType.DMA((8,))],
         scalars, x, g, space=pl.BlockSpec(memory_space=pl.ANY), limit=8,
     )
     (taps,) = call(taps_kernel, [((TAPS, 4 * width), F32)], [], scalars, conv_weight, fitting)
@@ -367,7 +384,7 @@
         scalars, keep, received, taps,
     )
     same, cross = call(
-        edge_rows_kernel, [((4, 3 * width), BF16)] * 2, [], scalars, keep, send, message
+        hold_kernel, [((4, 3 * width), BF16)] * 2, [], scalars, same, cross, message
     )
     near = lax.ppermute(message, line, hops(1))
     far = lax.ppermute(message, line, hops(2))
@@ -398,7 +415,7 @@
     states, rows = call(
         terms_kernel, [((heads, HEAD, HEAD), BF16), ((spread, 1, 2 * part), F32)],
         [
-            pltpu.VMEM((4, 16, width), F32), pltpu.VMEM((2, 16, width), BF16),
+            pltpu.VMEM((4, 16, width), F32), pltpu.VMEM((2, 32, width), BF16),
             pltpu.VMEM((TAPS, width), F32), pltpu.VMEM((2 * TAPS * spread, width // 2), F32),
         ],
         scalars, terms, products, a, front, left_tail, b_tail, near, far, wrap, taps, fold, rows,
@@ -414,8 +431,8 @@
     share = jnp.sum(rows * fitting, 0)[: TAPS * few].reshape(TAPS, few)
     shares = share * (1.0 / (lax.axis_size("zl") * spread))
     other = lax.ppermute(sent, "core", swap)
-    first, second = jnp.where(core == 0, own, other), jnp.where(core == 0, other, own)
-    return jnp.concatenate([first, second], 1)[None], shares
+    (grad,) = call(join_kernel, [((ROWS, 2 * width), BF16)], [], scalars, own, other)
+    return grad[None], shares
 
 
 def solution(mesh):

time: 117 us -> 116 us (level)
  blocking collectives: 0 us -> 17.7 us
  starting transfers between devices: 64.5 us -> 54.7 us
  waiting for transfers between devices: 28.8 us -> 21.6 us
    all_to_all x0 -> x1, blocking collectives: none -> 17.7 us  [per_device(): lax.all_to_all(rows, 'yx', 0, 0, tiled=True)]
    all_to_all x1 -> x0, starting transfers between devices: 9.85 us -> none  [per_device(): lax.all_to_all(rows, 'yx', 0, 0, tiled=True)]
    all_to_all x1 -> x0, waiting for transfers between devices: 8.69 us -> none  [per_device(): lax.all_to_all(rows, 'yx', 0, 0, tiled=True)]
    ppermute x1, waiting for transfers between devices: 5.64 us -> 9.69 us  [per_device(): wrap = lax.ppermute(wrap, line, hops(3))]
    ppermute x1, waiting for transfers between devices: 4.49 us -> 1.07 us  [per_device(): cross = lax.ppermute(cross, line, to_cross)]
    pallas_call x8 -> x9, Pallas kernels: 16.3 us -> 15.2 us  [call(): pl.pallas_call(kernel, out_shape=[jax.ShapeDtypeStruct(s, t) for s, t in...]
  transfers between devices with their start and end apart: 9 -> 8, of which waited for: 5 -> 5; matrix products, arithmetic and copies ran while one was open for 1% -> 1% of each run, Pallas kernels for 8% -> 7%
where the time goes in v4:
time: 116 us; the launch traced here: 115 us
  starting transfers between devices  54.7 us (47%)
  waiting for transfers between devices  21.6 us (19%)
  blocking collectives  17.7 us (15%)
  Pallas kernels  15.2 us (13%)
  local copies, waits for them, and re-layouts  5.01 us (4%)
    all_to_all x1, blocking collectives, per_device(): lax.all_to_all(rows, 'yx', 0, 0, tiled=True)  17.7 us
    ppermute x1, starting transfers between devices, per_device(): received = lax.ppermute(send, 'core', swap)  16.1 us
    pallas_call x9, Pallas kernels, call(): pl.pallas_call(kernel, out_shape=[jax.ShapeDtypeStruct(s, t) for s, t in...  15.2 us
    ppermute x1, starting transfers between devices, per_device(): cross = lax.ppermute(cross, line, to_cross)  12.7 us
    all_to_all x1, starting transfers between devices, per_device(): rows = lax.all_to_all(rows, ('core', 'zl', 'zh'), 0, 0, tiled=True)  12.7 us
    ppermute x1, waiting for transfers between devices, per_device(): wrap = lax.ppermute(wrap, line, hops(3))  9.69 us
    all_to_all x1, waiting for transfers between devices, per_device(): rows = lax.all_to_all(rows, ('core', 'zl', 'zh'), 0, 0, tiled=True)  7.72 us
    ppermute x1, starting transfers between devices, per_device(): same = lax.ppermute(same, line, to_same)  7.29 us
  transfers between devices with their start and end apart: 8, of which 5 were waited for; matrix products, arithmetic and copies ran while one was open for 1% of the time, Pallas kernels for 7%

profile of v4, /device:TPU:1, one launch (start us, length us, event | category | flops | bytes accessed | tf_op | source)
XLA Modules:
  0.0 115.2 jit_solution(16608438564642248666)
XLA Ops:
  0.6 0.1 pad_add_fusion.scalars
  0.7 0.0 copy-start
  0.7 1.5 %copy-done = bf16[1,128,7680]{2,1,0:T(8,128)(2,1)S(1)} copy-done((bf16[1,128,7680]{2,1,0:T(8,128)(2,1)S(1)}, bf16[1,128,7680]{2,1,0:T(8,128)(2,1)}, u32[]{:S(2)}) %copy-start) | copy-done | bytes 1966104
  2.3 0.0 copy-start.3
  2.3 1.1 copy-done.3
  3.3 0.0 copy-start.4
  3.3 1.9 %shard_map.50 = (bf16[128,5120]{1,0:T(8,128)(2,1)S(1)}, bf16[128,5120]{1,0:T(8,128)(2,1)}, bf16[4,3840]{1,0:T(4,128)(2,1)S(1)}, bf16[4,3840]{1,0:T(4,128)(2,1)S(1)}) custom-call(s32[2]{0:T(128)S(1)} %pad_add_fusion.scalars, bf16[128,7680]{1,0:T(8,128)(2,1)S(1)} %bitcast.9, bf16[128,2560]{1,0:T(8,128)(2,1)S(1)} %bitcast.10), custom_call_target="tpu_custom_call" | custom-call | tf_op jit(solution)/shard_map/pallas_call | solution.py:25
  5.3 16.1 %collective-permute-start = (bf16[128,5120]{1,0:T(8,128)(2,1)}, bf16[128,5120]{1,0:T(8,128)(2,1)S(1)}, u32[]{:S(2)}, u32[]{:S(2)}) collective-permute-start(bf16[128,5120]{1,0:T(8,128)(2,1)} %get-tuple-element.24), channel_id=1, source_target_pairs={{0,1},{1,0},{2,3},{3,2},{4,5},{5,4},{6,7},{7,6},{8,9},{9,8},{10,11... | collective-permute-start | bytes 3932168 | tf_op jit(solution)/shard_map/ppermute | solution.py:378
  21.4 0.0 copy-done.4
  21.4 0.6 shard_map.51.taps_ref
  21.9 2.2 %collective-permute-done.received_ref = bf16[128,5120]{1,0:T(8,128)(2,1)S(1)} collective-permute-done((bf16[128,5120]{1,0:T(8,128)(2,1)}, bf16[128,5120]{1,0:T(8,128)(2,1)S(1)}, u32[]{:S(2)}, u32[]{:S(2)}) %collective-permute-start) | collective-permute-done | bytes 1310752 | tf_op jit(solution)/shard_map/ppermute | solution.py:378
  24.2 2.1 %shard_map.52 = (bf16[10,144,128]{2,1,0:T(8,128)(2,1)S(1)}, bf16[10,136,128]{2,1,0:T(8,128)(2,1)S(1)}) custom-call(s32[2]{0:T(128)S(1)} %pad_add_fusion.scalars, bf16[128,5120]{1,0:T(8,128)(2,1)S(1)} %get-tuple-element.23.keep_ref, bf16[128,5120]{1,0:T(8,128)(2,1)S(1)} %collective-permute-done.received_ref, f32[4,5120]{1,0:T(4,128)S(1)} %shard_map.51.taps_ref), custom_call_target="tpu_custom_call" | custom-call | tf_op jit(solution)/shard_map/pallas_call | solution.py:25
  26.3 1.3 %collective-permute-start.3 = (bf16[10,144,128]{2,1,0:T(8,128)(2,1)S(1)}, bf16[10,144,128]{2,1,0:T(8,128)(2,1)S(1)}, u32[]{:S(2)}, u32[]{:S(2)}) collective-permute-start(bf16[10,144,128]{2,1,0:T(8,128)(2,1)S(1)} %get-tuple-element.27.after_ref), channel_id=1, source_target_pairs={{0,2},{2,4},{4,6},{3,1},{5,3},{7,5},{8,10},{10,12},{12,14},{11,9},... | collective-permute-start | bytes 1105928 | tf_op jit(solution)/shard_map/ppermute | solution.py:389
  27.6 1.3 %collective-permute-start.4 = (bf16[10,144,128]{2,1,0:T(8,128)(2,1)S(1)}, bf16[10,144,128]{2,1,0:T(8,128)(2,1)S(1)}, u32[]{:S(2)}, u32[]{:S(2)}) collective-permute-start(bf16[10,144,128]{2,1,0:T(8,128)(2,1)S(1)} %get-tuple-element.27.after_ref), channel_id=1, source_target_pairs={{0,4},{2,6},{5,1},{7,3},{8,12},{10,14},{13,9},{15,11},{16,20},{18,... | collective-permute-start | bytes 1105928 | tf_op jit(solution)/shard_map/ppermute | solution.py:390
  28.9 1.3 %collective-permute-start.5 = (bf16[10,136,128]{2,1,0:T(8,128)(2,1)S(1)}, bf16[10,136,128]{2,1,0:T(8,128)(2,1)S(1)}, u32[]{:S(2)}, u32[]{:S(2)}) collective-permute-start(bf16[10,136,128]{2,1,0:T(8,128)(2,1)S(1)} %get-tuple-element.37), channel_id=1, source_target_pairs={{0,6},{7,1},{8,14},{15,9},{16,22},{23,17},{24,30},{31,25},{32,38},... | collective-permute-start | bytes 1044488 | tf_op jit(solution)/shard_map/ppermute | solution.py:391
  30.2 0.5 shard_map.53
  30.7 7.3 %collective-permute-start.1 = (bf16[4,3840]{1,0:T(4,128)(2,1)S(1)}, bf16[4,3840]{1,0:T(4,128)(2,1)S(1)}, u32[]{:S(2)}, u32[]{:S(2)}) collective-permute-start(bf16[4,3840]{1,0:T(4,128)(2,1)S(1)} %get-tuple-element.28), channel_id=1, source_target_pairs={{1,3},{3,5},{5,7},{2,0},{4,2},{6,4},{9,11},{11,13},{13,15},{10,8},... | collective-permute-start | bytes 92168 | tf_op jit(solution)/shard_map/ppermute | solution.py:392
  38.0 12.7 %collective-permute-start.2 = (bf16[4,3840]{1,0:T(4,128)(2,1)S(1)}, bf16[4,3840]{1,0:T(4,128)(2,1)S(1)}, u32[]{:S(2)}, u32[]{:S(2)}) collective-permute-start(bf16[4,3840]{1,0:T(4,128)(2,1)S(1)} %get-tuple-element.29), channel_id=1, source_target_pairs={{1,2},{3,4},{5,6},{2,1},{4,3},{6,5},{9,10},{11,12},{13,14},{10,9},... | collective-permute-start | bytes 92168 | tf_op jit(solution)/shard_map/ppermute | solution.py:393
  50.7 1.9 %shard_map.55 = (f32[10,4,128,128]{3,2,1,0:T(8,128)S(1)}, bf16[640,256]{1,0:T(8,128)(2,1)S(1)}, f32[32,640]{1,0:T(8,128)S(1)}) custom-call(s32[2]{0:T(128)S(1)} %pad_add_fusion.scalars, bf16[128,5120]{1,0:T(8,128)(2,1)S(1)} %get-tuple-element.23.keep_ref, bf16[128,5120]{1,0:T(8,128)(2,1)S(1)} %collective-permute-done.received_ref, ...), custom_call_target="tpu_custom_call" | custom-call | tf_op jit(solution)/shard_map/pallas_call | solution.py:25
  52.6 0.0 collective-permute-done.1.same_ref
  52.6 1.1 collective-permute-done.2.cross_ref
  53.7 3.5 %shard_map.54 = (f32[272,1280]{1,0:T(8,128)S(1)}, bf16[272,1280]{1,0:T(8,128)(2,1)S(1)}, bf16[16,1280]{1,0:T(8,128)(2,1)S(1)}, bf16[16,1280]{1,0:T(8,128)(2,1)S(...) custom-call(s32[2]{0:T(128)S(1)} %pad_add_fusion.scalars, bf16[128,5120]{1,0:T(8,128)(2,1)S(1)} %get-tuple-element.23.keep_ref, ...), custom_call_target="tpu_custom_call" | custom-call | tf_op jit(solution)/shard_map/pallas_call | solution.py:25
  57.2 0.0 copy-start.1
  57.2 1.1 copy-done.1
  58.3 9.7 %collective-permute-done.5.wrap_ref = bf16[10,136,128]{2,1,0:T(8,128)(2,1)S(1)} collective-permute-done((bf16[10,136,128]{2,1,0:T(8,128)(2,1)S(1)}, bf16[10,136,128]{2,1,0:T(8,128)(2,1)S(1)}, u32[]{:S(2)}, u32[]{:S(2)}) %collective-permute-start.5) | collective-permute-done | bytes 348192 | tf_op jit(solution)/shard_map/ppermute | solution.py:391
  68.0 0.0 collective-permute-done.3.near_ref
  68.0 0.8 collective-permute-done.4.far_ref
  68.8 0.0 copy-start.2
  68.8 1.5 %shard_map.56 = (bf16[10,128,128]{2,1,0:T(8,128)(2,1)S(1)}, f32[32,1,256]{2,1,0:T(1,128)S(1)}) custom-call(s32[2]{0:T(128)S(1)} %pad_add_fusion.scalars, f32[4,1280]{1,0:T(4,128)S(1)} %get-tuple-element.32.terms_ref, f32[10,4,128,128]{3,2,1,0:T(8,128)S(1)} %get-tuple-element.33.products_ref, bf16[272,1280]{1,0:T(8,128)(2,1)S(1)} %get-tuple-element.31.a_ref, ...), custom_call_target="tpu_custom_call" | custom-call | tf_op jit(solution)/shard_map/pallas_call | solution.py:25
  70.4 17.7 %all_to_all.17 = f32[32,1,256]{2,1,0:T(1,128)S(1)} all-to-all(f32[32,1,256]{2,1,0:T(1,128)S(1)} %get-tuple-element.41), channel_id=1, replica_groups=mesh['zl'=4,'yx'=32,'zh'=4,'core'=2] {'yx'}, dimensions={0} | all-to-all | bytes 65536 | tf_op jit(solution)/shard_map/all_to_all | solution.py:423
  88.0 0.1 reduce_sum.18
  88.1 0.6 broadcast_in_dim.12
  88.7 12.7 %all-to-all-start.1 = ((f32[32,1,128]{2,1,0:T(1,128)}), f32[32,1,128]{2,1,0:T(1,128)S(1)}, u32[]{:S(2)}, u32[]{:S(2)}) async-start(f32[32,1,128]{2,1,0:T(1,128)} %bitcast.7), calls=%async_computation.1 | async-start | bytes 32768 | tf_op jit(solution)/shard_map/all_to_all | solution.py:430
  101.4 0.0 copy-done.2
  101.4 1.7 %shard_map.57 = (bf16[128,1280]{1,0:T(8,128)(2,1)S(1)}, bf16[128,1280]{1,0:T(8,128)(2,1)S(1)}) custom-call(s32[2]{0:T(128)S(1)} %pad_add_fusion.scalars, f32[272,1280]{1,0:T(8,128)S(1)} %copy-done.2, bf16[272,1280]{1,0:T(8,128)(2,1)S(1)} %get-tuple-element.31.a_ref, bf16[10,128,128]{2,1,0:T(8,128)(2,1)S(1)} %get-tuple-element.40.states_ref, ...), custom_call_target="tpu_custom_call" | custom-call | tf_op jit(solution)/shard_map/pallas_call | solution.py:25
  103.2 2.1 %collective-permute-start.6 = (bf16[128,1280]{1,0:T(8,128)(2,1)S(1)}, bf16[128,1280]{1,0:T(8,128)(2,1)S(1)}, u32[]{:S(2)}, u32[]{:S(2)}) collective-permute-start(bf16[128,1280]{1,0:T(8,128)(2,1)S(1)} %get-tuple-element.43), channel_id=1, source_target_pairs={{0,1},{1,0},{2,3},{3,2},{4,5},{5,4},{6,7},{7,6},{8,9},{9,8},{10,11... | collective-permute-start | bytes 983048 | tf_op jit(solution)/shard_map/ppermute | solution.py:433
  105.3 7.7 %all-to-all-done.1 = f32[32,1,128]{2,1,0:T(1,128)S(1)} async-done(((f32[32,1,128]{2,1,0:T(1,128)}), f32[32,1,128]{2,1,0:T(1,128)S(1)}, u32[]{:S(2)}, u32[]{:S(2)}) %all-to-all-start.1) | async-done | bytes 16416 | tf_op jit(solution)/shard_map/all_to_all | solution.py:430
  113.0 0.1 multiply_reduce_fusion
  113.1 0.7 mul.21
  113.8 0.0 collective-permute-done.6.other_ref
  113.8 1.4 %shard_map.58 = bf16[128,2560]{1,0:T(8,128)(2,1)} custom-call(s32[2]{0:T(128)S(1)} %pad_add_fusion.scalars, bf16[128,1280]{1,0:T(8,128)(2,1)S(1)} %get-tuple-element.42.own_ref, bf16[128,1280]{1,0:T(8,128)(2,1)S(1)} %collective-permute-done.6.other_ref), custom_call_target="tpu_custom_call" | custom-call | tf_op jit(solution)/shard_map/pallas_call | solution.py:25
  (3 shorter events, 0.0 us)
Async XLA Ops:
  0.7 1.5 %copy-start = (bf16[1,128,7680]{2,1,0:T(8,128)(2,1)S(1)}, bf16[1,128,7680]{2,1,0:T(8,128)(2,1)}, u32[]{:S(2)}) copy-start(bf16[1,128,7680]{2,1,0:T(8,128)(2,1)} %param.3) | copy-start | bytes 5898244
  2.3 1.1 copy-start.3
  3.3 18.0 %copy-start.4 = (f32[4,7680]{1,0:T(4,128)S(1)}, f32[4,7680]{1,0:T(4,128)}, u32[]{:S(2)}) copy-start(f32[4,7680]{1,0:T(4,128)} %w_ref.1) | copy-start | bytes 368644
  5.3 18.9 %collective-permute-start = (bf16[128,5120]{1,0:T(8,128)(2,1)}, bf16[128,5120]{1,0:T(8,128)(2,1)S(1)}, u32[]{:S(2)}, u32[]{:S(2)}) collective-permute-start(bf16[128,5120]{1,0:T(8,128)(2,1)} %get-tuple-element.24), channel_id=1, source_target_pairs={{0,1},{1,0},{2,3},{3,2},{4,5},{5,4},{6,7},{7,6},{8,9},{9,8},{10,11... | collective-permute-start | bytes 3932168 | tf_op jit(solution)/shard_map/ppermute | solution.py:378
  26.3 41.7 %collective-permute-start.3 = (bf16[10,144,128]{2,1,0:T(8,128)(2,1)S(1)}, bf16[10,144,128]{2,1,0:T(8,128)(2,1)S(1)}, u32[]{:S(2)}, u32[]{:S(2)}) collective-permute-start(bf16[10,144,128]{2,1,0:T(8,128)(2,1)S(1)} %get-tuple-element.27.after_ref), channel_id=1, source_target_pairs={{0,2},{2,4},{4,6},{3,1},{5,3},{7,5},{8,10},{10,12},{12,14},{11,9},... | collective-permute-start | bytes 1105928 | tf_op jit(solution)/shard_map/ppermute | solution.py:389
  27.6 41.3 %collective-permute-start.4 = (bf16[10,144,128]{2,1,0:T(8,128)(2,1)S(1)}, bf16[10,144,128]{2,1,0:T(8,128)(2,1)S(1)}, u32[]{:S(2)}, u32[]{:S(2)}) collective-permute-start(bf16[10,144,128]{2,1,0:T(8,128)(2,1)S(1)} %get-tuple-element.27.after_ref), channel_id=1, source_target_pairs={{0,4},{2,6},{5,1},{7,3},{8,12},{10,14},{13,9},{15,11},{16,20},{18,... | collective-permute-start | bytes 1105928 | tf_op jit(solution)/shard_map/ppermute | solution.py:390
  28.9 39.1 %collective-permute-start.5 = (bf16[10,136,128]{2,1,0:T(8,128)(2,1)S(1)}, bf16[10,136,128]{2,1,0:T(8,128)(2,1)S(1)}, u32[]{:S(2)}, u32[]{:S(2)}) collective-permute-start(bf16[10,136,128]{2,1,0:T(8,128)(2,1)S(1)} %get-tuple-element.37), channel_id=1, source_target_pairs={{0,6},{7,1},{8,14},{15,9},{16,22},{23,17},{24,30},{31,25},{32,38},... | collective-permute-start | bytes 1044488 | tf_op jit(solution)/shard_map/ppermute | solution.py:391
  30.7 21.9 %collective-permute-start.1 = (bf16[4,3840]{1,0:T(4,128)(2,1)S(1)}, bf16[4,3840]{1,0:T(4,128)(2,1)S(1)}, u32[]{:S(2)}, u32[]{:S(2)}) collective-permute-start(bf16[4,3840]{1,0:T(4,128)(2,1)S(1)} %get-tuple-element.28), channel_id=1, source_target_pairs={{1,3},{3,5},{5,7},{2,0},{4,2},{6,4},{9,11},{11,13},{13,15},{10,8},... | collective-permute-start | bytes 92168 | tf_op jit(solution)/shard_map/ppermute | solution.py:392
  38.0 15.7 %collective-permute-start.2 = (bf16[4,3840]{1,0:T(4,128)(2,1)S(1)}, bf16[4,3840]{1,0:T(4,128)(2,1)S(1)}, u32[]{:S(2)}, u32[]{:S(2)}) collective-permute-start(bf16[4,3840]{1,0:T(4,128)(2,1)S(1)} %get-tuple-element.29), channel_id=1, source_target_pairs={{1,2},{3,4},{5,6},{2,1},{4,3},{6,5},{9,10},{11,12},{13,14},{10,9},... | collective-permute-start | bytes 92168 | tf_op jit(solution)/shard_map/ppermute | solution.py:393
  57.2 1.1 copy-start.1
  68.8 32.5 %copy-start.2 = (f32[272,1280]{1,0:T(8,128)S(1)}, f32[272,1280]{1,0:T(8,128)}, u32[]{:S(2)}) copy-start(f32[272,1280]{1,0:T(8,128)} %copy-done.1) | copy-start | bytes 4177924
  88.7 24.3 %all-to-all-start.1 = ((f32[32,1,128]{2,1,0:T(1,128)}), f32[32,1,128]{2,1,0:T(1,128)S(1)}, u32[]{:S(2)}, u32[]{:S(2)}) async-start(f32[32,1,128]{2,1,0:T(1,128)} %bitcast.7), calls=%async_computation.1 | async-start | bytes 32768 | tf_op jit(solution)/shard_map/all_to_all | solution.py:430
  103.2 10.6 %collective-permute-start.6 = (bf16[128,1280]{1,0:T(8,128)(2,1)S(1)}, bf16[128,1280]{1,0:T(8,128)(2,1)S(1)}, u32[]{:S(2)}, u32[]{:S(2)}) collective-permute-start(bf16[128,1280]{1,0:T(8,128)(2,1)S(1)} %get-tuple-element.43), channel_id=1, source_target_pairs={{0,1},{1,0},{2,3},{3,2},{4,5},{5,4},{6,7},{7,6},{8,9},{9,8},{10,11... | collective-permute-start | bytes 983048 | tf_op jit(solution)/shard_map/ppermute | solution.py:433

commit v5 on v4

--- a/solution.py
+++ b/solution.py
@@ -48,18 +48,18 @@
     return slice(group * width + head * HEAD, group * width + (head + 1) * HEAD)
 
 
-def fill_edges(core, keep_ref, send_ref, same_ref, cross_ref):
+def fill_edges(core, keep_ref, send_ref):
     width = keep_ref.shape[1] // 4
     edge = pl.ds(pl.multiple_of(core * (ROWS - 16), 16), 16)
-    for ref, out_ref, later in ((keep_ref, same_ref, A), (send_ref, cross_ref, B)):
-        for slot, (first, last) in enumerate(((LEFT, LEFT), (A, later), (B, RAW))):
-            zero = ref[edge, first * width : (first + 1) * width].astype(F32)[0:4]
-            one = ref[edge, last * width : (last + 1) * width].astype(F32)[12:16]
-            rows = jnp.where(core == 1, one, zero).astype(BF16)
-            out_ref[:, slot * width : (slot + 1) * width] = rows
-
-
-def pack_kernel(scalars, x_ref, g_ref, keep_ref, send_ref, same_ref, cross_ref, sems):
+    none = jnp.zeros((12, width), F32)
+    for slot, (first, last) in enumerate(((LEFT, LEFT), (A, A), (B, RAW), (RAW, RAW))):
+        zero = keep_ref[edge, first * width : (first + 1) * width].astype(F32)[0:4]
+        one = keep_ref[edge, last * width : (last + 1) * width].astype(F32)[12:16]
+        rows = jnp.concatenate([jnp.where(core == 1, one, zero), none], 0)
+        send_ref[ROWS : ROWS + 16, slot * width : (slot + 1) * width] = rows.astype(BF16)
+
+
+def pack_kernel(scalars, x_ref, g_ref, before_ref, keep_ref, send_ref, sems):
     core = scalars[0]
     width = keep_ref.shape[1] // 4
     of_core = (
@@ -75,7 +75,7 @@
             lanes_out = slice(slot * width, (slot + 1) * width)
             copies.append(
                 pltpu.make_async_copy(
-                    source_ref.at[:, lanes_in], out_ref.at[:, lanes_out], sems.at[len(copies)]
+                    source_ref.at[:, lanes_in], out_ref.at[0:ROWS, lanes_out], sems.at[len(copies)]
                 )
             )
 
@@ -96,10 +96,10 @@
     def _():
         fill(1)
 
-    fill_edges(core, keep_ref, send_ref, same_ref, cross_ref)
-
-
-def taps_kernel(scalars, w_ref, fitting_ref, taps_ref):
+    fill_edges(core, keep_ref, send_ref)
+
+
+def taps_kernel(scalars, w_ref, taps_ref):
     width = taps_ref.shape[1] // 4
     row = lax.broadcasted_iota(jnp.int32, (TAPS, width), 0)
     unit = jnp.where(row == 0, 1.0, 0.0).astype(F32)
@@ -116,7 +116,7 @@
     own = pl.ds(pl.multiple_of(PRE + core * ROWS, 8), ROWS)
     other = pl.ds(pl.multiple_of(PRE + (1 - core) * ROWS, 8), ROWS)
     padded_ref[own, :] = keep_ref[:, at].astype(F32)
-    padded_ref[other, :] = received_ref[:, at].astype(F32)
+    padded_ref[other, :] = received_ref[0:ROWS, at].astype(F32)
 
 
 def convolved(padded_ref, taps, start, count):
@@ -126,7 +126,12 @@
     return total
 
 
-def states_kernel(scalars, keep_ref, received_ref, taps_ref, message_ref, wrap_ref, *scratch):
+def half_of(one_ref, two_ref, head):
+    first = one_ref.shape[0]
+    return (one_ref, head) if head < first else (two_ref, head - first)
+
+
+def states_kernel(scalars, keep_ref, received_ref, taps_ref, one_ref, two_ref, wrap_ref, *scratch):
     core, chip = scalars[0], scalars[1]
     width = keep_ref.shape[1] // 4
     padded_refs, value_refs = scratch[:4], scratch[4:]
@@ -154,15 +159,32 @@
         left, right = value_refs[(2 * head) % 4], value_refs[(2 * head + 1) % 4]
         state = tn(right[...], left[...]).astype(BF16)
         firsts, lasts = jnp.concatenate(firsts, 0), jnp.concatenate(lasts, 0)
-        for ref in (message_ref, wrap_ref):
-            ref[head, 0:HEAD, :] = state
-        message_ref[head, HEAD:, :] = jnp.concatenate([firsts, lasts], 0).astype(BF16)
+        message_ref, at = half_of(one_ref, two_ref, head)
+        message_ref[at, 0:HEAD, :] = state
+        third = jnp.where(
+            core == 0,
+            received_ref[ROWS - 16 : ROWS, lanes(RAW, head, width)].astype(F32)[12:16],
+            received_ref[0:16, lanes(A, head, width)].astype(F32)[0:4],
+        )
+        others = [
+            received_ref[ROWS : ROWS + 16, lanes(slot, head, width)].astype(F32)[0:4] for slot in range(3)
+        ]
+        message_ref[at, HEAD:, :] = jnp.concatenate([firsts, lasts, third, *others], 0).astype(BF16)
+        wrap_ref[head, 0:HEAD, :] = state
         wrap_ref[head, HEAD:, :] = jnp.where(core == 0, lasts, firsts).astype(BF16)
 
 
-def hold_kernel(scalars, same_ref, cross_ref, after_ref, same_out_ref, cross_out_ref):
-    same_out_ref[...] = same_ref[...]
-    cross_out_ref[...] = cross_ref[...]
+def partner_kernel(scalars, near_one_ref, near_two_ref, out_ref):
+    width = out_ref.shape[1] // 3
+    for head in range(width // HEAD):
+        near_ref, at = half_of(near_one_ref, near_two_ref, head)
+        rows = near_ref[at, HEAD + 2 * EDGE :, :].astype(F32)
+        for slot in range(3):
+            out_ref[:, lanes(slot, head, width)] = rows[4 * slot + 4 : 4 * slot + 8].astype(BF16)
+
+
+def hand_on_kernel(scalars, message_ref, after_ref, out_ref):
+    out_ref[...] = message_ref[:, 0 : out_ref.shape[1], :]
 
 
 def products_kernel(
@@ -195,14 +217,13 @@
 
 
 def inside_kernel(
-    scalars, keep_ref, received_ref, same_ref, cross_ref, taps_ref,
+    scalars, keep_ref, received_ref, near_one_ref, near_two_ref, other_ref, taps_ref,
     kept_ref, a_ref, left_tail_ref, b_tail_ref, terms_ref, front_ref, *scratch,
 ):
     core = scalars[0]
     width = keep_ref.shape[1] // 4
     padded_refs, value_refs = scratch[:4], scratch[4:]
-    same, cross = same_ref[...].astype(F32), cross_ref[...].astype(F32)
-    before, after = jnp.where(core == 1, same, cross), jnp.where(core == 1, cross, same)
+    other = other_ref[...].astype(F32)
     row = lax.broadcasted_iota(jnp.int32, (EXT, EXT), 0)
     column = lax.broadcasted_iota(jnp.int32, (EXT, EXT), 1)
     causal = jnp.where(column <= row, 1.0 / HEAD, 0.0)
@@ -219,16 +240,21 @@
     for head in range(width // HEAD):
         to = lanes(0, head, width)
         values = []
+        near_ref, half = half_of(near_one_ref, near_two_ref, head)
+        near = near_ref[half, HEAD:, :].astype(F32)
+        first, last, third = near[0:EDGE], near[EDGE : 2 * EDGE], near[2 * EDGE : 2 * EDGE + 4]
+        partner = [other[:, lanes(slot, head, width)] for slot in range(3)]
+        befores = zip((last[0:4], third, last[4:8], third), (partner[0], partner[1], partner[1], partner[2]))
+        afters = zip((partner[0], partner[1], partner[2], third), (first[0:4], third, first[4:8], third))
+        befores, afters = ([jnp.where(core == 0, *pair) for pair in pairs] for pairs in (befores, afters))
         for group in (LEFT, A, B, RAW):
             padded_ref = padded_refs[turn % 4]
             value_ref = value_refs[turn % 4]
             turn += 1
             at = lanes(group, head, width)
             gather_rows(core, keep_ref, received_ref, at, padded_ref)
-            front = before[:, lanes((0, 1, 1, 2)[group], head, width)]
-            back = after[:, lanes((0, 1, 2, 2)[group], head, width)]
-            padded_ref[0:PRE, :] = jnp.concatenate([none, front], 0)
-            padded_ref[PRE + PAIR : LONG, :] = jnp.concatenate([back, none], 0)
+            padded_ref[0:PRE, :] = jnp.concatenate([none, befores[group]], 0)
+            padded_ref[PRE + PAIR : LONG, :] = jnp.concatenate([afters[group], none], 0)
             if group == RAW:
                 raw_ref = padded_ref
                 continue
@@ -260,7 +286,7 @@
 
 def terms_kernel(
     scalars, terms_ref, products_ref, a_ref, front_ref, left_tail_ref, b_tail_ref,
-    near_ref, far_ref, wrap_ref, taps_ref, fold_ref, rows_ref,
+    near_one_ref, near_two_ref, far_one_ref, far_two_ref, wrap_ref, taps_ref, fold_ref, rows_ref,
     states_ref, shares_ref, edge_ref, seam_ref, total_ref, stack_ref,
 ):
     core = scalars[0]
@@ -268,7 +294,10 @@
     none = jnp.zeros((8, HEAD), F32)
     for head in range(heads):
         to = lanes(0, head, width)
-        near, far, wrap = (r[head, HEAD:, :].astype(F32) for r in (near_ref, far_ref, wrap_ref))
+        near_ref, at = half_of(near_one_ref, near_two_ref, head)
+        far_ref, _ = half_of(far_one_ref, far_two_ref, head)
+        near, far = (r[at, HEAD : HEAD + 2 * EDGE, :].astype(F32) for r in (near_ref, far_ref))
+        wrap = wrap_ref[head, HEAD:, :].astype(F32)
         near = jnp.where(core == 0, near[0:EDGE], near[EDGE : 2 * EDGE])
         first, last = far[0:EDGE], far[EDGE : 2 * EDGE]
         for turn, (zero, one) in enumerate((((last, near), (near, first)), ((wrap, first), (last, wrap)))):
@@ -287,7 +316,10 @@
     seams = [tn(seam_ref[1, :, to], seam_ref[0, :, to]) for _, to in every]
     states = []
     for (head, _), seam in zip(every, seams):
-        near, far, wrap = (r[head, 0:HEAD, :].astype(F32) for r in (near_ref, far_ref, wrap_ref))
+        near_ref, at = half_of(near_one_ref, near_two_ref, head)
+        far_ref, _ = half_of(far_one_ref, far_two_ref, head)
+        near, far = (r[at, 0:HEAD, :].astype(F32) for r in (near_ref, far_ref))
+        wrap = wrap_ref[head, 0:HEAD, :].astype(F32)
         states.append((near + far + (wrap + seam)).astype(BF16))
     fronts = [nn(a_ref[0:16, to], state) for (_, to), state in zip(every, states)]
     row = lax.broadcasted_iota(jnp.int32, (8, HEAD), 0)
@@ -365,32 +397,23 @@
         later = [(2 * c, 2 * (c + by)) for c in range(chips - by)]
         return later + [(2 * (c + by) + 1, 2 * c + 1) for c in range(chips - by)]
 
-    pairs = range(chips - 1)
-    to_same = [(2 * c + 1, 2 * c + 3) for c in pairs] + [(2 * c + 2, 2 * c) for c in pairs]
-    to_cross = [(2 * c + 1, 2 * c + 2) for c in pairs] + [(2 * c + 2, 2 * c + 1) for c in pairs]
-
-    keep, send, same, cross = call(
-        pack_kernel, [((ROWS, 4 * width), BF16)] * 2 + [((4, 3 * width), BF16)] * 2,
+    keep, send = call(
+        pack_kernel, [((rows, 4 * width), BF16) for rows in (ROWS, ROWS + 16)],
         [pltpu.SemaphoreType.DMA((8,))],
-        scalars, x, g, space=pl.BlockSpec(memory_space=pl.ANY), limit=8,
-    )
-    (taps,) = call(taps_kernel, [((TAPS, 4 * width), F32)], [], scalars, conv_weight, fitting)
+        scalars, x, g, fitting, space=pl.BlockSpec(memory_space=pl.ANY), limit=8,
+    )
+    (taps,) = call(taps_kernel, [((TAPS, 4 * width), F32)], [], scalars, conv_weight)
     received = lax.ppermute(send, "core", swap)
     padded = [pltpu.VMEM((LONG, HEAD), F32)] * 4
-    message, wrap = call(
-        states_kernel,
-        [((heads, HEAD + size, HEAD), BF16) for size in (2 * EDGE, EDGE)],
+    message = ((heads // 2, HEAD + 4 * EDGE, HEAD), BF16)
+    one, two, wrap = call(
+        states_kernel, [message, message, ((heads, HEAD + EDGE, HEAD), BF16)],
         padded + [pltpu.VMEM((PAIR, HEAD), BF16)] * 4,
         scalars, keep, received, taps,
     )
-    same, cross = call(
-        hold_kernel, [((4, 3 * width), BF16)] * 2, [], scalars, same, cross, message
-    )
-    near = lax.ppermute(message, line, hops(1))
-    far = lax.ppermute(message, line, hops(2))
+    near_one = lax.ppermute(one, line, hops(1))
+    near_two = lax.ppermute(two, line, hops(1))
     wrap = lax.ppermute(wrap, line, hops(3))
-    same = lax.ppermute(same, line, to_same)
-    cross = lax.ppermute(cross, line, to_cross)
     spread = lax.axis_size("yx")
     few = width // 2 // spread
     part = -(-TAPS * few // HEAD) * HEAD
@@ -401,8 +424,18 @@
             ((heads, TAPS, HEAD, HEAD), F32), ((width // 2, 2 * part), BF16),
             ((spread, width // 2), F32),
         ],
-        padded, scalars, keep, received, taps, message,
-    )
+        padded, scalars, keep, received, taps, one,
+    )
+    handed = ((heads // 2, HEAD + 2 * EDGE, HEAD), BF16)
+    onward = [pair for pair in hops(1) if pair not in ((0, 2), (2 * chips - 1, 2 * chips - 3))]
+    far_one, far_two = (
+        lax.ppermute(call(hand_on_kernel, [handed], [], scalars, near, fold)[0], line, onward)
+        for near in (near_one, near_two)
+    )
+    (partner,) = call(
+        partner_kernel, [((4, 3 * width), BF16)], [], scalars, near_one, near_two
+    )
+    partner = lax.ppermute(partner, "core", swap)
     inside, a, left_tail, b_tail, terms, front = call(
         inside_kernel,
         [
@@ -410,7 +443,7 @@
             ((PRE + 8, width), F32),
         ],
         padded + [pltpu.VMEM((EXT, HEAD), BF16)] * 4,
-        scalars, keep, received, same, cross, taps,
+        scalars, keep, received, near_one, near_two, partner, taps,
     )
     states, rows = call(
         terms_kernel, [((heads, HEAD, HEAD), BF16), ((spread, 1, 2 * part), F32)],
@@ -418,7 +451,8 @@
             pltpu.VMEM((4, 16, width), F32), pltpu.VMEM((2, 32, width), BF16),
             pltpu.VMEM((TAPS, width), F32), pltpu.VMEM((2 * TAPS * spread, width // 2), F32),
         ],
-        scalars, terms, products, a, front, left_tail, b_tail, near, far, wrap, taps, fold, rows,
+        scalars, terms, products, a, front, left_tail, b_tail,
+        near_one, near_two, far_one, far_two, wrap, taps, fold, rows,
     )
     rows = jnp.sum(lax.all_to_all(rows, "yx", 0, 0, tiled=True), (0, 1)).reshape(2, part)
     rows = jnp.broadcast_to(rows[None, None, :, None], (2, 2, 2, chips, part)).reshape(8 * chips, part)

time: 116 us -> 110 us (0.948)
  starting transfers between devices: 54.7 us -> 40.1 us
  waiting for transfers between devices: 21.6 us -> 31.3 us
    ppermute x4 -> x5, waiting for transfers between devices: 1.92 us -> 21.3 us  [the longest x1 12.5 us: per_device(): near_one = lax.ppermute(one, line, hops(1))]
    ppermute x4 -> x5, starting transfers between devices: 22.6 us -> 7.09 us  [the longest x2 2.58 us: per_device(): lax.ppermute(call(hand_on_kernel, [handed], [], scalars, near, fold)[0],...]
    ppermute x1, waiting for transfers between devices: 9.69 us -> 0.01 us  [per_device(): wrap = lax.ppermute(wrap, line, hops(3))]
    unnamed x10 -> x6, local copies, waits for them, and re-layouts: 3.74 us -> 2.64 us
    pallas_call x9 -> x11, Pallas kernels: 15.2 us -> 15.4 us  [call(): pl.pallas_call(kernel, out_shape=[jax.ShapeDtypeStruct(s, t) for s, t in...]
  transfers between devices with their start and end apart: 8 -> 9, of which waited for: 5 -> 7; matrix products, arithmetic and copies ran while one was open for 1% -> 1% of each run, Pallas kernels for 7% -> 9%
where the time goes in v5:
time: 110 us
  starting transfers between devices  40.1 us (36%)
  waiting for transfers between devices  31.3 us (28%)
  blocking collectives  18.2 us (17%)
  Pallas kernels  15.4 us (14%)
  local copies, waits for them, and re-layouts  3.91 us (4%)
    all_to_all x1, blocking collectives, per_device(): lax.all_to_all(rows, 'yx', 0, 0, tiled=True)  18.2 us
    ppermute x1, starting transfers between devices, per_device(): received = lax.ppermute(send, 'core', swap)  16.1 us
    pallas_call x11, Pallas kernels, call(): pl.pallas_call(kernel, out_shape=[jax.ShapeDtypeStruct(s, t) for s, t in...  15.4 us
    all_to_all x1, starting transfers between devices, per_device(): rows = lax.all_to_all(rows, ('core', 'zl', 'zh'), 0, 0, tiled=True)  13.6 us
    ppermute x1, waiting for transfers between devices, per_device(): near_one = lax.ppermute(one, line, hops(1))  12.5 us
    all_to_all x1, waiting for transfers between devices, per_device(): rows = lax.all_to_all(rows, ('core', 'zl', 'zh'), 0, 0, tiled=True)  7.7 us
    ppermute x2, waiting for transfers between devices, per_device(): lax.ppermute(call(hand_on_kernel, [handed], [], scalars, near, fold)[0],...  5.18 us
    unnamed x6, local copies, waits for them, and re-layouts  2.64 us
  transfers between devices with their start and end apart: 9, of which 7 were waited for; matrix products, arithmetic and copies ran while one was open for 1% of the time, Pallas kernels for 9%

profile of v5, /device:TPU:1, one launch (start us, length us, event | category | flops | bytes accessed | tf_op | source)
XLA Modules:
  0.0 110.0 jit_solution(12388225123686036290)
XLA Ops:
  0.7 0.1 pad_add_fusion.scalars
  0.7 0.0 copy-start
  0.7 1.5 %copy-done = bf16[1,128,7680]{2,1,0:T(8,128)(2,1)S(1)} copy-done((bf16[1,128,7680]{2,1,0:T(8,128)(2,1)S(1)}, bf16[1,128,7680]{2,1,0:T(8,128)(2,1)}, u32[]{:S(2)}) %copy-start) | copy-done | bytes 1966104
  2.3 0.0 copy-start.1
  2.3 1.1 copy-done.1
  3.4 0.0 copy-start.2
  3.4 0.9 shard_map.50
  4.3 16.1 %collective-permute-start = (bf16[144,5120]{1,0:T(8,128)(2,1)S(1)}, bf16[144,5120]{1,0:T(8,128)(2,1)S(1)}, u32[]{:S(2)}, u32[]{:S(2)}) collective-permute-start(bf16[144,5120]{1,0:T(8,128)(2,1)S(1)} %get-tuple-element.21), channel_id=1, source_target_pairs={{0,1},{1,0},{2,3},{3,2},{4,5},{5,4},{6,7},{7,6},{8,9},{9,8},{10,11... | collective-permute-start | bytes 4423688 | tf_op jit(solution)/shard_map/ppermute | solution.py:406
  20.3 0.0 copy-done.2
  20.3 0.6 shard_map.51.taps_ref
  20.9 2.3 %collective-permute-done.received_ref = bf16[144,5120]{1,0:T(8,128)(2,1)S(1)} collective-permute-done((bf16[144,5120]{1,0:T(8,128)(2,1)S(1)}, bf16[144,5120]{1,0:T(8,128)(2,1)S(1)}, u32[]{:S(2)}, u32[]{:S(2)}) %collective-permute-start) | collective-permute-done | bytes 1474592 | tf_op jit(solution)/shard_map/ppermute | solution.py:406
  23.2 1.7 %shard_map.52 = (bf16[5,160,128]{2,1,0:T(8,128)(2,1)S(1)}, bf16[5,160,128]{2,1,0:T(8,128)(2,1)S(1)}, bf16[10,136,128]{2,1,0:T(8,128)(2,1)S(1)}) custom-call(s32[2]{0:T(128)S(1)} %pad_add_fusion.scalars, bf16[128,5120]{1,0:T(8,128)(2,1)S(1)} %get-tuple-element.20.keep_ref, bf16[144,5120]{1,0:T(8,128)(2,1)S(1)} %collective-permute-done.received_ref, ...), custom_call_target="tpu_custom_call" | custom-call | tf_op jit(solution)/shard_map/pallas_call | solution.py:25
  24.9 1.3 %collective-permute-start.1 = (bf16[5,160,128]{2,1,0:T(8,128)(2,1)S(1)}, bf16[5,160,128]{2,1,0:T(8,128)(2,1)S(1)}, u32[]{:S(2)}, u32[]{:S(2)}) collective-permute-start(bf16[5,160,128]{2,1,0:T(8,128)(2,1)S(1)} %get-tuple-element.22.after_ref), channel_id=1, source_target_pairs={{0,2},{2,4},{4,6},{3,1},{5,3},{7,5},{8,10},{10,12},{12,14},{11,9},... | collective-permute-start | bytes 614408 | tf_op jit(solution)/shard_map/ppermute | solution.py:414
  26.2 1.3 %collective-permute-start.2 = (bf16[5,160,128]{2,1,0:T(8,128)(2,1)S(1)}, bf16[5,160,128]{2,1,0:T(8,128)(2,1)S(1)}, u32[]{:S(2)}, u32[]{:S(2)}) collective-permute-start(bf16[5,160,128]{2,1,0:T(8,128)(2,1)S(1)} %get-tuple-element.23), channel_id=1, source_target_pairs={{0,2},{2,4},{4,6},{3,1},{5,3},{7,5},{8,10},{10,12},{12,14},{11,9},... | collective-permute-start | bytes 614408 | tf_op jit(solution)/shard_map/ppermute | solution.py:415
  27.5 1.3 %collective-permute-start.6 = (bf16[10,136,128]{2,1,0:T(8,128)(2,1)S(1)}, bf16[10,136,128]{2,1,0:T(8,128)(2,1)S(1)}, u32[]{:S(2)}, u32[]{:S(2)}) collective-permute-start(bf16[10,136,128]{2,1,0:T(8,128)(2,1)S(1)} %get-tuple-element.32), channel_id=1, source_target_pairs={{0,6},{7,1},{8,14},{15,9},{16,22},{23,17},{24,30},{31,25},{32,38},... | collective-permute-start | bytes 1044488 | tf_op jit(solution)/shard_map/ppermute | solution.py:416
  28.8 1.9 %shard_map.55 = (f32[10,4,128,128]{3,2,1,0:T(8,128)S(1)}, bf16[640,256]{1,0:T(8,128)(2,1)S(1)}, f32[32,640]{1,0:T(8,128)S(1)}) custom-call(s32[2]{0:T(128)S(1)} %pad_add_fusion.scalars, bf16[128,5120]{1,0:T(8,128)(2,1)S(1)} %get-tuple-element.20.keep_ref, bf16[144,5120]{1,0:T(8,128)(2,1)S(1)} %collective-permute-done.received_ref, ...), custom_call_target="tpu_custom_call" | custom-call | tf_op jit(solution)/shard_map/pallas_call | solution.py:25
  30.8 12.5 %collective-permute-done.1.near_one_ref.message_ref = bf16[5,160,128]{2,1,0:T(8,128)(2,1)S(1)} collective-permute-done((bf16[5,160,128]{2,1,0:T(8,128)(2,1)S(1)}, bf16[5,160,128]{2,1,0:T(8,128)(2,1)S(1)}, u32[]{:S(2)}, u32[]{:S(2)}) %collective-permute-start.1) | collective-permute-done | bytes 204832 | tf_op jit(solution)/shard_map/ppermute | solution.py:414
  43.3 0.6 shard_map.56
  43.9 1.3 %collective-permute-start.4 = (bf16[5,144,128]{2,1,0:T(8,128)(2,1)S(1)}, bf16[5,144,128]{2,1,0:T(8,128)(2,1)S(1)}, u32[]{:S(2)}, u32[]{:S(2)}) collective-permute-start(bf16[5,144,128]{2,1,0:T(8,128)(2,1)S(1)} %shard_map.56), channel_id=1, source_target_pairs={{2,4},{4,6},{3,1},{5,3},{10,12},{12,14},{11,9},{13,11},{18,20},{20... | collective-permute-start | bytes 552968 | tf_op jit(solution)/shard_map/ppermute | solution.py:432
  45.2 2.4 %collective-permute-done.2.near_two_ref.message_ref = bf16[5,160,128]{2,1,0:T(8,128)(2,1)S(1)} collective-permute-done((bf16[5,160,128]{2,1,0:T(8,128)(2,1)S(1)}, bf16[5,160,128]{2,1,0:T(8,128)(2,1)S(1)}, u32[]{:S(2)}, u32[]{:S(2)}) %collective-permute-start.2) | collective-permute-done | bytes 204832 | tf_op jit(solution)/shard_map/ppermute | solution.py:415
  47.6 0.6 shard_map.57
  48.2 1.3 %collective-permute-start.5 = (bf16[5,144,128]{2,1,0:T(8,128)(2,1)S(1)}, bf16[5,144,128]{2,1,0:T(8,128)(2,1)S(1)}, u32[]{:S(2)}, u32[]{:S(2)}) collective-permute-start(bf16[5,144,128]{2,1,0:T(8,128)(2,1)S(1)} %shard_map.57), channel_id=1, source_target_pairs={{2,4},{4,6},{3,1},{5,3},{10,12},{12,14},{11,9},{13,11},{18,20},{20... | collective-permute-start | bytes 552968 | tf_op jit(solution)/shard_map/ppermute | solution.py:432
  49.5 0.6 shard_map.53
  50.0 1.9 %collective-permute-start.3 = (bf16[4,3840]{1,0:T(4,128)(2,1)S(1)}, bf16[4,3840]{1,0:T(4,128)(2,1)S(1)}, u32[]{:S(2)}, u32[]{:S(2)}) collective-permute-start(bf16[4,3840]{1,0:T(4,128)(2,1)S(1)} %shard_map.53), channel_id=1, source_target_pairs={{0,1},{1,0},{2,3},{3,2},{4,5},{5,4},{6,7},{7,6},{8,9},{9,8},{10,11... | collective-permute-start | bytes 92168 | tf_op jit(solution)/shard_map/ppermute | solution.py:438
  51.9 1.2 %collective-permute-done.3.other_ref = bf16[4,3840]{1,0:T(4,128)(2,1)S(1)} collective-permute-done((bf16[4,3840]{1,0:T(4,128)(2,1)S(1)}, bf16[4,3840]{1,0:T(4,128)(2,1)S(1)}, u32[]{:S(2)}, u32[]{:S(2)}) %collective-permute-start.3) | collective-permute-done | bytes 30752 | tf_op jit(solution)/shard_map/ppermute | solution.py:438
  53.1 3.9 %shard_map.54 = (f32[272,1280]{1,0:T(8,128)S(1)}, bf16[272,1280]{1,0:T(8,128)(2,1)S(1)}, bf16[16,1280]{1,0:T(8,128)(2,1)S(1)}, bf16[16,1280]{1,0:T(8,128)(2,1)S(...) custom-call(s32[2]{0:T(128)S(1)} %pad_add_fusion.scalars, bf16[128,5120]{1,0:T(8,128)(2,1)S(1)} %get-tuple-element.20.keep_ref, ...), custom_call_target="tpu_custom_call" | custom-call | tf_op jit(solution)/shard_map/pallas_call | solution.py:25
  57.0 0.0 collective-permute-done.6.wrap_ref
  57.0 3.2 %collective-permute-done.4.far_one_ref = bf16[5,144,128]{2,1,0:T(8,128)(2,1)S(1)} collective-permute-done((bf16[5,144,128]{2,1,0:T(8,128)(2,1)S(1)}, bf16[5,144,128]{2,1,0:T(8,128)(2,1)S(1)}, u32[]{:S(2)}, u32[]{:S(2)}) %collective-permute-start.4) | collective-permute-done | bytes 184352 | tf_op jit(solution)/shard_map/ppermute | solution.py:432
  60.2 2.0 %collective-permute-done.5.far_two_ref = bf16[5,144,128]{2,1,0:T(8,128)(2,1)S(1)} collective-permute-done((bf16[5,144,128]{2,1,0:T(8,128)(2,1)S(1)}, bf16[5,144,128]{2,1,0:T(8,128)(2,1)S(1)}, u32[]{:S(2)}, u32[]{:S(2)}) %collective-permute-start.5) | collective-permute-done | bytes 184352 | tf_op jit(solution)/shard_map/ppermute | solution.py:432
  62.2 1.5 %shard_map.58 = (bf16[10,128,128]{2,1,0:T(8,128)(2,1)S(1)}, f32[32,1,256]{2,1,0:T(1,128)S(1)}) custom-call(s32[2]{0:T(128)S(1)} %pad_add_fusion.scalars, f32[4,1280]{1,0:T(4,128)S(1)} %get-tuple-element.26.terms_ref, f32[10,4,128,128]{3,2,1,0:T(8,128)S(1)} %get-tuple-element.27.products_ref, bf16[272,1280]{1,0:T(8,128)(2,1)S(1)} %get-tuple-element.25.a_ref, ...), custom_call_target="tpu_custom_call" | custom-call | tf_op jit(solution)/shard_map/pallas_call | solution.py:25
  63.7 18.2 %all_to_all.17 = f32[32,1,256]{2,1,0:T(1,128)S(1)} all-to-all(f32[32,1,256]{2,1,0:T(1,128)S(1)} %get-tuple-element.35), channel_id=1, replica_groups=mesh['zl'=4,'yx'=32,'zh'=4,'core'=2] {'yx'}, dimensions={0} | all-to-all | bytes 65536 | tf_op jit(solution)/shard_map/all_to_all | solution.py:457
  81.9 0.1 reduce_sum.18
  81.9 0.6 broadcast_in_dim.12
  82.6 13.6 %all-to-all-start.1 = ((f32[32,1,128]{2,1,0:T(1,128)}), f32[32,1,128]{2,1,0:T(1,128)S(1)}, u32[]{:S(2)}, u32[]{:S(2)}) async-start(f32[32,1,128]{2,1,0:T(1,128)} %bitcast.7), calls=%async_computation.1 | async-start | bytes 32768 | tf_op jit(solution)/shard_map/all_to_all | solution.py:464
  96.1 1.8 %shard_map.59 = (bf16[128,1280]{1,0:T(8,128)(2,1)S(1)}, bf16[128,1280]{1,0:T(8,128)(2,1)S(1)}) custom-call(s32[2]{0:T(128)S(1)} %pad_add_fusion.scalars, f32[272,1280]{1,0:T(8,128)S(1)} %get-tuple-element.24.inside_ref, bf16[272,1280]{1,0:T(8,128)(2,1)S(1)} %get-tuple-element.25.a_ref, bf16[10,128,128]{2,1,0:T(8,128)(2,1)S(1)} %get-tuple-element.34.states_ref, ...), custom_call_target="tpu_custom_call" | custom-call | tf_op jit(solution)/shard_map/pallas_call | solution.py:25
  97.9 2.1 %collective-permute-start.7 = (bf16[128,1280]{1,0:T(8,128)(2,1)S(1)}, bf16[128,1280]{1,0:T(8,128)(2,1)S(1)}, u32[]{:S(2)}, u32[]{:S(2)}) collective-permute-start(bf16[128,1280]{1,0:T(8,128)(2,1)S(1)} %get-tuple-element.37), channel_id=1, source_target_pairs={{0,1},{1,0},{2,3},{3,2},{4,5},{5,4},{6,7},{7,6},{8,9},{9,8},{10,11... | collective-permute-start | bytes 983048 | tf_op jit(solution)/shard_map/ppermute | solution.py:467
  100.1 7.7 %all-to-all-done.1 = f32[32,1,128]{2,1,0:T(1,128)S(1)} async-done(((f32[32,1,128]{2,1,0:T(1,128)}), f32[32,1,128]{2,1,0:T(1,128)S(1)}, u32[]{:S(2)}, u32[]{:S(2)}) %all-to-all-start.1) | async-done | bytes 16416 | tf_op jit(solution)/shard_map/all_to_all | solution.py:464
  107.8 0.1 multiply_reduce_fusion
  107.9 0.7 mul.21
  108.5 0.0 collective-permute-done.7.other_ref
  108.5 1.4 %shard_map.60 = bf16[128,2560]{1,0:T(8,128)(2,1)} custom-call(s32[2]{0:T(128)S(1)} %pad_add_fusion.scalars, bf16[128,1280]{1,0:T(8,128)(2,1)S(1)} %get-tuple-element.36.own_ref, bf16[128,1280]{1,0:T(8,128)(2,1)S(1)} %collective-permute-done.7.other_ref), custom_call_target="tpu_custom_call" | custom-call | tf_op jit(solution)/shard_map/pallas_call | solution.py:25
  (3 shorter events, 0.0 us)
Async XLA Ops:
  0.7 1.5 %copy-start = (bf16[1,128,7680]{2,1,0:T(8,128)(2,1)S(1)}, bf16[1,128,7680]{2,1,0:T(8,128)(2,1)}, u32[]{:S(2)}) copy-start(bf16[1,128,7680]{2,1,0:T(8,128)(2,1)} %param.3) | copy-start | bytes 5898244
  2.3 1.1 copy-start.1
  3.4 17.0 %copy-start.2 = (f32[4,7680]{1,0:T(4,128)S(1)}, f32[4,7680]{1,0:T(4,128)}, u32[]{:S(2)}) copy-start(f32[4,7680]{1,0:T(4,128)} %w_ref.1) | copy-start | bytes 368644
  4.3 18.9 %collective-permute-start = (bf16[144,5120]{1,0:T(8,128)(2,1)S(1)}, bf16[144,5120]{1,0:T(8,128)(2,1)S(1)}, u32[]{:S(2)}, u32[]{:S(2)}) collective-permute-start(bf16[144,5120]{1,0:T(8,128)(2,1)S(1)} %get-tuple-element.21), channel_id=1, source_target_pairs={{0,1},{1,0},{2,3},{3,2},{4,5},{5,4},{6,7},{7,6},{8,9},{9,8},{10,11... | collective-permute-start | bytes 4423688 | tf_op jit(solution)/shard_map/ppermute | solution.py:406
  24.9 18.4 %collective-permute-start.1 = (bf16[5,160,128]{2,1,0:T(8,128)(2,1)S(1)}, bf16[5,160,128]{2,1,0:T(8,128)(2,1)S(1)}, u32[]{:S(2)}, u32[]{:S(2)}) collective-permute-start(bf16[5,160,128]{2,1,0:T(8,128)(2,1)S(1)} %get-tuple-element.22.after_ref), channel_id=1, source_target_pairs={{0,2},{2,4},{4,6},{3,1},{5,3},{7,5},{8,10},{10,12},{12,14},{11,9},... | collective-permute-start | bytes 614408 | tf_op jit(solution)/shard_map/ppermute | solution.py:414
  26.2 21.3 %collective-permute-start.2 = (bf16[5,160,128]{2,1,0:T(8,128)(2,1)S(1)}, bf16[5,160,128]{2,1,0:T(8,128)(2,1)S(1)}, u32[]{:S(2)}, u32[]{:S(2)}) collective-permute-start(bf16[5,160,128]{2,1,0:T(8,128)(2,1)S(1)} %get-tuple-element.23), channel_id=1, source_target_pairs={{0,2},{2,4},{4,6},{3,1},{5,3},{7,5},{8,10},{10,12},{12,14},{11,9},... | collective-permute-start | bytes 614408 | tf_op jit(solution)/shard_map/ppermute | solution.py:415
  27.5 29.4 %collective-permute-start.6 = (bf16[10,136,128]{2,1,0:T(8,128)(2,1)S(1)}, bf16[10,136,128]{2,1,0:T(8,128)(2,1)S(1)}, u32[]{:S(2)}, u32[]{:S(2)}) collective-permute-start(bf16[10,136,128]{2,1,0:T(8,128)(2,1)S(1)} %get-tuple-element.32), channel_id=1, source_target_pairs={{0,6},{7,1},{8,14},{15,9},{16,22},{23,17},{24,30},{31,25},{32,38},... | collective-permute-start | bytes 1044488 | tf_op jit(solution)/shard_map/ppermute | solution.py:416
  43.9 16.3 %collective-permute-start.4 = (bf16[5,144,128]{2,1,0:T(8,128)(2,1)S(1)}, bf16[5,144,128]{2,1,0:T(8,128)(2,1)S(1)}, u32[]{:S(2)}, u32[]{:S(2)}) collective-permute-start(bf16[5,144,128]{2,1,0:T(8,128)(2,1)S(1)} %shard_map.56), channel_id=1, source_target_pairs={{2,4},{4,6},{3,1},{5,3},{10,12},{12,14},{11,9},{13,11},{18,20},{20... | collective-permute-start | bytes 552968 | tf_op jit(solution)/shard_map/ppermute | solution.py:432
  48.2 14.0 %collective-permute-start.5 = (bf16[5,144,128]{2,1,0:T(8,128)(2,1)S(1)}, bf16[5,144,128]{2,1,0:T(8,128)(2,1)S(1)}, u32[]{:S(2)}, u32[]{:S(2)}) collective-permute-start(bf16[5,144,128]{2,1,0:T(8,128)(2,1)S(1)} %shard_map.57), channel_id=1, source_target_pairs={{2,4},{4,6},{3,1},{5,3},{10,12},{12,14},{11,9},{13,11},{18,20},{20... | collective-permute-start | bytes 552968 | tf_op jit(solution)/shard_map/ppermute | solution.py:432
  50.0 3.1 %collective-permute-start.3 = (bf16[4,3840]{1,0:T(4,128)(2,1)S(1)}, bf16[4,3840]{1,0:T(4,128)(2,1)S(1)}, u32[]{:S(2)}, u32[]{:S(2)}) collective-permute-start(bf16[4,3840]{1,0:T(4,128)(2,1)S(1)} %shard_map.53), channel_id=1, source_target_pairs={{0,1},{1,0},{2,3},{3,2},{4,5},{5,4},{6,7},{7,6},{8,9},{9,8},{10,11... | collective-permute-start | bytes 92168 | tf_op jit(solution)/shard_map/ppermute | solution.py:438
  82.6 25.2 %all-to-all-start.1 = ((f32[32,1,128]{2,1,0:T(1,128)}), f32[32,1,128]{2,1,0:T(1,128)S(1)}, u32[]{:S(2)}, u32[]{:S(2)}) async-start(f32[32,1,128]{2,1,0:T(1,128)} %bitcast.7), calls=%async_computation.1 | async-start | bytes 32768 | tf_op jit(solution)/shard_map/all_to_all | solution.py:464
  97.9 10.6 %collective-permute-start.7 = (bf16[128,1280]{1,0:T(8,128)(2,1)S(1)}, bf16[128,1280]{1,0:T(8,128)(2,1)S(1)}, u32[]{:S(2)}, u32[]{:S(2)}) collective-permute-start(bf16[128,1280]{1,0:T(8,128)(2,1)S(1)} %get-tuple-element.37), channel_id=1, source_target_pairs={{0,1},{1,0},{2,3},{3,2},{4,5},{5,4},{6,7},{7,6},{8,9},{9,8},{10,11... | collective-permute-start | bytes 983048 | tf_op jit(solution)/shard_map/ppermute | solution.py:467

commit v6 on v5

--- a/solution.py
+++ b/solution.py
@@ -131,7 +131,7 @@
     return (one_ref, head) if head < first else (two_ref, head - first)
 
 
-def states_kernel(scalars, keep_ref, received_ref, taps_ref, one_ref, two_ref, wrap_ref, *scratch):
+def states_kernel(scalars, keep_ref, received_ref, taps_ref, message_ref, *scratch, begin=0):
     core, chip = scalars[0], scalars[1]
     width = keep_ref.shape[1] // 4
     padded_refs, value_refs = scratch[:4], scratch[4:]
@@ -140,7 +140,8 @@
     row = lax.broadcasted_iota(jnp.int32, (ROWS, HEAD), 0)
     kept_rows = (row >= TAPS - 1) | (chip == 0)
     first_rows = jnp.where(chip == 0, 0.0, 1.0)
-    for head in range(width // HEAD):
+    for place in range(message_ref.shape[0]):
+        head = begin + place
         firsts, lasts = [], []
         for turn, group in enumerate((LEFT, B)):
             padded_ref = padded_refs[(2 * head + turn) % 4]
@@ -157,10 +158,7 @@
             firsts.append(front * first_rows if group == LEFT else front)
             lasts.append(padded_ref[PRE + PAIR - 4 : PRE + PAIR, :])
         left, right = value_refs[(2 * head) % 4], value_refs[(2 * head + 1) % 4]
-        state = tn(right[...], left[...]).astype(BF16)
-        firsts, lasts = jnp.concatenate(firsts, 0), jnp.concatenate(lasts, 0)
-        message_ref, at = half_of(one_ref, two_ref, head)
-        message_ref[at, 0:HEAD, :] = state
+        message_ref[place, 0:HEAD, :] = tn(right[...], left[...]).astype(BF16)
         third = jnp.where(
             core == 0,
             received_ref[ROWS - 16 : ROWS, lanes(RAW, head, width)].astype(F32)[12:16],
@@ -169,9 +167,19 @@
         others = [
             received_ref[ROWS : ROWS + 16, lanes(slot, head, width)].astype(F32)[0:4] for slot in range(3)
         ]
-        message_ref[at, HEAD:, :] = jnp.concatenate([firsts, lasts, third, *others], 0).astype(BF16)
-        wrap_ref[head, 0:HEAD, :] = state
-        wrap_ref[head, HEAD:, :] = jnp.where(core == 0, lasts, firsts).astype(BF16)
+        message_ref[place, HEAD:, :] = jnp.concatenate([*firsts, *lasts, third, *others], 0).astype(BF16)
+
+
+def second_states_kernel(
+    scalars, keep_ref, received_ref, taps_ref, one_ref, after_ref, two_ref, wrap_ref, *scratch
+):
+    states_kernel(scalars, keep_ref, received_ref, taps_ref, two_ref, *scratch, begin=one_ref.shape[0])
+    for head in range(wrap_ref.shape[0]):
+        message_ref, at = half_of(one_ref, two_ref, head)
+        wrap_ref[head, 0:HEAD, :] = message_ref[at, 0:HEAD, :]
+        edges = message_ref[at, HEAD : HEAD + 2 * EDGE, :].astype(F32)
+        edges = jnp.where(scalars[0] == 0, edges[EDGE:], edges[:EDGE])
+        wrap_ref[head, HEAD:, :] = edges.astype(BF16)
 
 
 def partner_kernel(scalars, near_one_ref, near_two_ref, out_ref):
@@ -372,7 +380,8 @@
     send_ref[...] = grad_ref[pl.ds(pl.multiple_of((1 - core) * ROWS, ROWS), ROWS), :]
 
 
-def join_kernel(scalars, own_ref, other_ref, out_ref):
+def join_kernel(scalars, own_ref, other_ref, fitting_ref, out_ref, fitting_out_ref):
+    fitting_out_ref[...] = fitting_ref[...]
     width = own_ref.shape[1]
     for core, parts in enumerate(((own_ref, other_ref), (other_ref, own_ref))):
 
@@ -400,20 +409,16 @@
     keep, send = call(
         pack_kernel, [((rows, 4 * width), BF16) for rows in (ROWS, ROWS + 16)],
         [pltpu.SemaphoreType.DMA((8,))],
-        scalars, x, g, fitting, space=pl.BlockSpec(memory_space=pl.ANY), limit=8,
+        scalars, *(pltpu.with_memory_space_constraint(each, pltpu.HBM) for each in (x, g)), fitting,
+        space=pl.BlockSpec(memory_space=pl.ANY), limit=8,
     )
     (taps,) = call(taps_kernel, [((TAPS, 4 * width), F32)], [], scalars, conv_weight)
     received = lax.ppermute(send, "core", swap)
     padded = [pltpu.VMEM((LONG, HEAD), F32)] * 4
-    message = ((heads // 2, HEAD + 4 * EDGE, HEAD), BF16)
-    one, two, wrap = call(
-        states_kernel, [message, message, ((heads, HEAD + EDGE, HEAD), BF16)],
-        padded + [pltpu.VMEM((PAIR, HEAD), BF16)] * 4,
-        scalars, keep, received, taps,
-    )
+    message, second = (((many, HEAD + 4 * EDGE, HEAD), BF16) for many in (6 * heads // 10, heads - 6 * heads // 10))
+    buffers = padded + [pltpu.VMEM((PAIR, HEAD), BF16)] * 4
+    (one,) = call(states_kernel, [message], buffers, scalars, keep, received, taps)
     near_one = lax.ppermute(one, line, hops(1))
-    near_two = lax.ppermute(two, line, hops(1))
-    wrap = lax.ppermute(wrap, line, hops(3))
     spread = lax.axis_size("yx")
     few = width // 2 // spread
     part = -(-TAPS * few // HEAD) * HEAD
@@ -426,10 +431,17 @@
         ],
         padded, scalars, keep, received, taps, one,
     )
-    handed = ((heads // 2, HEAD + 2 * EDGE, HEAD), BF16)
+    two, wrap = call(
+        second_states_kernel, [second, ((heads, HEAD + EDGE, HEAD), BF16)], buffers,
+        scalars, keep, received, taps, one, fold,
+    )
+    near_two = lax.ppermute(two, line, hops(1))
+    wrap = lax.ppermute(wrap, line, hops(3))
     onward = [pair for pair in hops(1) if pair not in ((0, 2), (2 * chips - 1, 2 * chips - 3))]
     far_one, far_two = (
-        lax.ppermute(call(hand_on_kernel, [handed], [], scalars, near, fold)[0], line, onward)
+        lax.ppermute(call(
+            hand_on_kernel, [((near.shape[0], HEAD + 2 * EDGE, HEAD), BF16)], [], scalars, near, fold
+        )[0], line, onward)
         for near in (near_one, near_two)
     )
     (partner,) = call(
@@ -462,11 +474,12 @@
         scalars, inside, a, states, taps, rows,
     )
     rows = lax.all_to_all(rows, ("core", "zl", "zh"), 0, 0, tiled=True)
+    other = lax.ppermute(sent, "core", swap)
+    grad, fitting = call(
+        join_kernel, [((ROWS, 2 * width), BF16), (fitting.shape, F32)], [], scalars, own, other, fitting
+    )
     share = jnp.sum(rows * fitting, 0)[: TAPS * few].reshape(TAPS, few)
-    shares = share * (1.0 / (lax.axis_size("zl") * spread))
-    other = lax.ppermute(sent, "core", swap)
-    (grad,) = call(join_kernel, [((ROWS, 2 * width), BF16)], [], scalars, own, other)
-    return grad[None], shares
+    return grad[None], share * (1.0 / (lax.axis_size("zl") * spread))
 
 
 def solution(mesh):

time: 110 us -> 116 us (1.055)
  starting transfers between devices: 40.1 us -> 45.7 us
  local copies, waits for them, and re-layouts: 3.91 us -> 1.27 us
  Pallas kernels: 15.4 us -> 17.7 us
    ppermute x1, starting transfers between devices: 1.92 us -> 6.49 us  [per_device(): partner = lax.ppermute(partner, 'core', swap)]
    ppermute x2, waiting for transfers between devices: 5.18 us -> 7.83 us  [per_device(): lax.ppermute(call(hand_on_kernel, [((near.shape[0], HEAD + 2 * EDGE, HEAD...]
    unnamed x6 -> x2, local copies, waits for them, and re-layouts: 2.64 us -> 0.01 us
    all_to_all x1, waiting for transfers between devices: 7.7 us -> 10.1 us  [per_device(): rows = lax.all_to_all(rows, ('core', 'zl', 'zh'), 0, 0, tiled=True)]
    ppermute x1, waiting for transfers between devices: 2.41 us -> 0.01 us  [per_device(): near_two = lax.ppermute(two, line, hops(1))]
    pallas_call x11 -> x12, Pallas kernels: 15.4 us -> 17.7 us  [call(): pl.pallas_call(kernel, out_shape=[jax.ShapeDtypeStruct(s, t) for s, t in...]
    ppermute x1, waiting for transfers between devices: 12.5 us -> 10.3 us  [per_device(): near_one = lax.ppermute(one, line, hops(1))]
    all_to_all x1, starting transfers between devices: 13.6 us -> 14.8 us  [per_device(): rows = lax.all_to_all(rows, ('core', 'zl', 'zh'), 0, 0, tiled=True)]
  transfers between devices with their start and end apart: 9 -> 9, of which waited for: 7 -> 5; matrix products, arithmetic and copies ran while one was open for 1% -> 0% of each run, Pallas kernels for 9% -> 9%
where the time goes in v6:
time: 116 us; the launch traced here: 115 us
  starting transfers between devices  45.7 us (39%)
  waiting for transfers between devices  31.4 us (27%)
  blocking collectives  18.2 us (16%)
  Pallas kernels  17.7 us (15%)
  local copies, waits for them, and re-layouts  1.27 us (1%)
    all_to_all x1, blocking collectives, per_device(): lax.all_to_all(rows, 'yx', 0, 0, tiled=True)  18.2 us
    pallas_call x12, Pallas kernels, call(): pl.pallas_call(kernel, out_shape=[jax.ShapeDtypeStruct(s, t) for s, t in...  17.7 us
    ppermute x1, starting transfers between devices, per_device(): received = lax.ppermute(send, 'core', swap)  16 us
    all_to_all x1, starting transfers between devices, per_device(): rows = lax.all_to_all(rows, ('core', 'zl', 'zh'), 0, 0, tiled=True)  14.8 us
    ppermute x1, waiting for transfers between devices, per_device(): near_one = lax.ppermute(one, line, hops(1))  10.3 us
    all_to_all x1, waiting for transfers between devices, per_device(): rows = lax.all_to_all(rows, ('core', 'zl', 'zh'), 0, 0, tiled=True)  10.1 us
    ppermute x2, waiting for transfers between devices, per_device(): lax.ppermute(call(hand_on_kernel, [((near.shape[0], HEAD + 2 * EDGE, HEAD...  7.83 us
    ppermute x1, starting transfers between devices, per_device(): partner = lax.ppermute(partner, 'core', swap)  6.49 us
  transfers between devices with their start and end apart: 9, of which 5 were waited for; matrix products, arithmetic and copies ran while one was open for 0% of the time, Pallas kernels for 9%

profile of v6, /device:TPU:1, one launch (start us, length us, event | category | flops | bytes accessed | tf_op | source)
XLA Modules:
  0.0 115.4 jit_solution(10176879279787191328)
XLA Ops:
  0.6 0.0 copy-start
  0.7 0.1 pad_add_fusion.scalars
  0.8 2.3 %shard_map.50 = (bf16[128,5120]{1,0:T(8,128)(2,1)S(1)}, bf16[144,5120]{1,0:T(8,128)(2,1)S(1)}) custom-call(s32[2]{0:T(128)S(1)} %pad_add_fusion.scalars, bf16[128,7680]{1,0:T(8,128)(2,1)} %bitcast.9, bf16[128,2560]{1,0:T(8,128)(2,1)} %bitcast.10, f32[32,1]{1,0:T(8,128)S(1)} %fusion.4.before_ref.fitting_ref), custom_call_target="tpu_custom_call" | custom-call | tf_op jit(solution)/shard_map/pallas_call | solution.py:25
  3.1 16.0 %collective-permute-start = (bf16[144,5120]{1,0:T(8,128)(2,1)S(1)}, bf16[144,5120]{1,0:T(8,128)(2,1)S(1)}, u32[]{:S(2)}, u32[]{:S(2)}) collective-permute-start(bf16[144,5120]{1,0:T(8,128)(2,1)S(1)} %get-tuple-element.22), channel_id=1, source_target_pairs={{0,1},{1,0},{2,3},{3,2},{4,5},{5,4},{6,7},{7,6},{8,9},{9,8},{10,11... | collective-permute-start | bytes 4423688 | tf_op jit(solution)/shard_map/ppermute | solution.py:416
  19.2 0.0 copy-done
  19.2 0.6 shard_map.51.taps_ref
  19.7 2.3 %collective-permute-done.received_ref = bf16[144,5120]{1,0:T(8,128)(2,1)S(1)} collective-permute-done((bf16[144,5120]{1,0:T(8,128)(2,1)S(1)}, bf16[144,5120]{1,0:T(8,128)(2,1)S(1)}, u32[]{:S(2)}, u32[]{:S(2)}) %collective-permute-start) | collective-permute-done | bytes 1474592 | tf_op jit(solution)/shard_map/ppermute | solution.py:416
  22.0 1.4 %shard_map.52.after_ref.one_ref = bf16[6,160,128]{2,1,0:T(8,128)(2,1)S(1)} custom-call(s32[2]{0:T(128)S(1)} %pad_add_fusion.scalars, bf16[128,5120]{1,0:T(8,128)(2,1)S(1)} %get-tuple-element.21.keep_ref, bf16[144,5120]{1,0:T(8,128)(2,1)S(1)} %collective-permute-done.received_ref, f32[4,5120]{1,0:T(4,128)S(1)} %shard_map.51.taps_ref), custom_call_target="tpu_custom_call" | custom-call | tf_op jit(solution)/shard_map/pallas_call | solution.py:25
  23.4 1.3 %collective-permute-start.1 = (bf16[6,160,128]{2,1,0:T(8,128)(2,1)S(1)}, bf16[6,160,128]{2,1,0:T(8,128)(2,1)S(1)}, u32[]{:S(2)}, u32[]{:S(2)}) collective-permute-start(bf16[6,160,128]{2,1,0:T(8,128)(2,1)S(1)} %shard_map.52.after_ref.one_ref), channel_id=1, source_target_pairs={{0,2},{2,4},{4,6},{3,1},{5,3},{7,5},{8,10},{10,12},{12,14},{11,9},... | collective-permute-start | bytes 737288 | tf_op jit(solution)/shard_map/ppermute | solution.py:421
  24.7 1.9 %shard_map.53 = (f32[10,4,128,128]{3,2,1,0:T(8,128)S(1)}, bf16[640,256]{1,0:T(8,128)(2,1)S(1)}, f32[32,640]{1,0:T(8,128)S(1)}) custom-call(s32[2]{0:T(128)S(1)} %pad_add_fusion.scalars, bf16[128,5120]{1,0:T(8,128)(2,1)S(1)} %get-tuple-element.21.keep_ref, bf16[144,5120]{1,0:T(8,128)(2,1)S(1)} %collective-permute-done.received_ref, ...), custom_call_target="tpu_custom_call" | custom-call | tf_op jit(solution)/shard_map/pallas_call | solution.py:25
  26.7 1.2 %shard_map.54 = (bf16[4,160,128]{2,1,0:T(8,128)(2,1)S(1)}, bf16[10,136,128]{2,1,0:T(8,128)(2,1)S(1)}) custom-call(s32[2]{0:T(128)S(1)} %pad_add_fusion.scalars, bf16[128,5120]{1,0:T(8,128)(2,1)S(1)} %get-tuple-element.21.keep_ref, bf16[144,5120]{1,0:T(8,128)(2,1)S(1)} %collective-permute-done.received_ref, f32[4,5120]{1,0:T(4,128)S(1)} %shard_map.51.taps_ref, ...), custom_call_target="tpu_custom_call" | custom-call | tf_op jit(solution)/shard_map/pallas_call | solution.py:25
  27.9 1.3 %collective-permute-start.6 = (bf16[10,136,128]{2,1,0:T(8,128)(2,1)S(1)}, bf16[10,136,128]{2,1,0:T(8,128)(2,1)S(1)}, u32[]{:S(2)}, u32[]{:S(2)}) collective-permute-start(bf16[10,136,128]{2,1,0:T(8,128)(2,1)S(1)} %get-tuple-element.32), channel_id=1, source_target_pairs={{0,6},{7,1},{8,14},{15,9},{16,22},{23,17},{24,30},{31,25},{32,38},... | collective-permute-start | bytes 1044488 | tf_op jit(solution)/shard_map/ppermute | solution.py:439
  29.2 1.3 %collective-permute-start.2 = (bf16[4,160,128]{2,1,0:T(8,128)(2,1)S(1)}, bf16[4,160,128]{2,1,0:T(8,128)(2,1)S(1)}, u32[]{:S(2)}, u32[]{:S(2)}) collective-permute-start(bf16[4,160,128]{2,1,0:T(8,128)(2,1)S(1)} %get-tuple-element.24), channel_id=1, source_target_pairs={{0,2},{2,4},{4,6},{3,1},{5,3},{7,5},{8,10},{10,12},{12,14},{11,9},... | collective-permute-start | bytes 491528 | tf_op jit(solution)/shard_map/ppermute | solution.py:438
  30.5 10.3 %collective-permute-done.1.near_one_ref.message_ref = bf16[6,160,128]{2,1,0:T(8,128)(2,1)S(1)} collective-permute-done((bf16[6,160,128]{2,1,0:T(8,128)(2,1)S(1)}, bf16[6,160,128]{2,1,0:T(8,128)(2,1)S(1)}, u32[]{:S(2)}, u32[]{:S(2)}) %collective-permute-start.1) | collective-permute-done | bytes 245792 | tf_op jit(solution)/shard_map/ppermute | solution.py:421
  40.8 0.6 shard_map.57
  41.4 1.3 %collective-permute-start.4 = (bf16[6,144,128]{2,1,0:T(8,128)(2,1)S(1)}, bf16[6,144,128]{2,1,0:T(8,128)(2,1)S(1)}, u32[]{:S(2)}, u32[]{:S(2)}) collective-permute-start(bf16[6,144,128]{2,1,0:T(8,128)(2,1)S(1)} %shard_map.57), channel_id=1, source_target_pairs={{2,4},{4,6},{3,1},{5,3},{10,12},{12,14},{11,9},{13,11},{18,20},{20... | collective-permute-start | bytes 663560 | tf_op jit(solution)/shard_map/ppermute | solution.py:442
  42.7 0.0 collective-permute-done.2.near_two_ref.message_ref
  42.7 0.6 shard_map.58
  43.3 1.3 %collective-permute-start.5 = (bf16[4,144,128]{2,1,0:T(8,128)(2,1)S(1)}, bf16[4,144,128]{2,1,0:T(8,128)(2,1)S(1)}, u32[]{:S(2)}, u32[]{:S(2)}) collective-permute-start(bf16[4,144,128]{2,1,0:T(8,128)(2,1)S(1)} %shard_map.58), channel_id=1, source_target_pairs={{2,4},{4,6},{3,1},{5,3},{10,12},{12,14},{11,9},{13,11},{18,20},{20... | collective-permute-start | bytes 442376 | tf_op jit(solution)/shard_map/ppermute | solution.py:442
  44.6 0.6 shard_map.55
  45.1 6.5 %collective-permute-start.3 = (bf16[4,3840]{1,0:T(4,128)(2,1)S(1)}, bf16[4,3840]{1,0:T(4,128)(2,1)S(1)}, u32[]{:S(2)}, u32[]{:S(2)}) collective-permute-start(bf16[4,3840]{1,0:T(4,128)(2,1)S(1)} %shard_map.55), channel_id=1, source_target_pairs={{0,1},{1,0},{2,3},{3,2},{4,5},{5,4},{6,7},{7,6},{8,9},{9,8},{10,11... | collective-permute-start | bytes 92168 | tf_op jit(solution)/shard_map/ppermute | solution.py:450
  51.6 0.8 collective-permute-done.3.other_ref
  52.5 3.8 %shard_map.56 = (f32[272,1280]{1,0:T(8,128)S(1)}, bf16[272,1280]{1,0:T(8,128)(2,1)S(1)}, bf16[16,1280]{1,0:T(8,128)(2,1)S(1)}, bf16[16,1280]{1,0:T(8,128)(2,1)S(...) custom-call(s32[2]{0:T(128)S(1)} %pad_add_fusion.scalars, bf16[128,5120]{1,0:T(8,128)(2,1)S(1)} %get-tuple-element.21.keep_ref, ...), custom_call_target="tpu_custom_call" | custom-call | tf_op jit(solution)/shard_map/pallas_call | solution.py:25
  56.3 7.8 %collective-permute-done.5.far_two_ref = bf16[4,144,128]{2,1,0:T(8,128)(2,1)S(1)} collective-permute-done((bf16[4,144,128]{2,1,0:T(8,128)(2,1)S(1)}, bf16[4,144,128]{2,1,0:T(8,128)(2,1)S(1)}, u32[]{:S(2)}, u32[]{:S(2)}) %collective-permute-start.5) | collective-permute-done | bytes 147488 | tf_op jit(solution)/shard_map/ppermute | solution.py:442
  64.1 0.0 collective-permute-done.6.wrap_ref
  64.1 0.0 collective-permute-done.4.far_one_ref
  64.2 1.5 %shard_map.59 = (bf16[10,128,128]{2,1,0:T(8,128)(2,1)S(1)}, f32[32,1,256]{2,1,0:T(1,128)S(1)}) custom-call(s32[2]{0:T(128)S(1)} %pad_add_fusion.scalars, f32[4,1280]{1,0:T(4,128)S(1)} %get-tuple-element.27.terms_ref, f32[10,4,128,128]{3,2,1,0:T(8,128)S(1)} %get-tuple-element.28.products_ref, bf16[272,1280]{1,0:T(8,128)(2,1)S(1)} %get-tuple-element.26.a_ref, ...), custom_call_target="tpu_custom_call" | custom-call | tf_op jit(solution)/shard_map/pallas_call | solution.py:25
  65.7 18.2 %all_to_all.17 = f32[32,1,256]{2,1,0:T(1,128)S(1)} all-to-all(f32[32,1,256]{2,1,0:T(1,128)S(1)} %get-tuple-element.35), channel_id=1, replica_groups=mesh['zl'=4,'yx'=32,'zh'=4,'core'=2] {'yx'}, dimensions={0} | all-to-all | bytes 65536 | tf_op jit(solution)/shard_map/all_to_all | solution.py:469
  83.9 0.1 reduce_sum.18
  83.9 0.6 broadcast_in_dim.12
  84.5 1.7 %shard_map.60 = (bf16[128,1280]{1,0:T(8,128)(2,1)S(1)}, bf16[128,1280]{1,0:T(8,128)(2,1)S(1)}) custom-call(s32[2]{0:T(128)S(1)} %pad_add_fusion.scalars, f32[272,1280]{1,0:T(8,128)S(1)} %get-tuple-element.25.inside_ref, bf16[272,1280]{1,0:T(8,128)(2,1)S(1)} %get-tuple-element.26.a_ref, bf16[10,128,128]{2,1,0:T(8,128)(2,1)S(1)} %get-tuple-element.34.states_ref, ...), custom_call_target="tpu_custom_call" | custom-call | tf_op jit(solution)/shard_map/pallas_call | solution.py:25
  86.3 1.9 %collective-permute-start.7 = (bf16[128,1280]{1,0:T(8,128)(2,1)S(1)}, bf16[128,1280]{1,0:T(8,128)(2,1)S(1)}, u32[]{:S(2)}, u32[]{:S(2)}) collective-permute-start(bf16[128,1280]{1,0:T(8,128)(2,1)S(1)} %get-tuple-element.37), channel_id=1, source_target_pairs={{0,1},{1,0},{2,3},{3,2},{4,5},{5,4},{6,7},{7,6},{8,9},{9,8},{10,11... | collective-permute-start | bytes 983048 | tf_op jit(solution)/shard_map/ppermute | solution.py:477
  88.2 14.8 %all-to-all-start.1 = ((f32[32,1,128]{2,1,0:T(1,128)}), f32[32,1,128]{2,1,0:T(1,128)S(1)}, u32[]{:S(2)}, u32[]{:S(2)}) async-start(f32[32,1,128]{2,1,0:T(1,128)} %bitcast.7), calls=%async_computation.1 | async-start | bytes 32768 | tf_op jit(solution)/shard_map/all_to_all | solution.py:476
  103.0 0.0 collective-permute-done.7.other_ref
  103.0 1.4 %shard_map.61 = (bf16[128,2560]{1,0:T(8,128)(2,1)}, f32[32,1]{1,0:T(8,128)S(1)}) custom-call(s32[2]{0:T(128)S(1)} %pad_add_fusion.scalars, bf16[128,1280]{1,0:T(8,128)(2,1)S(1)} %get-tuple-element.36.own_ref, bf16[128,1280]{1,0:T(8,128)(2,1)S(1)} %collective-permute-done.7.other_ref, f32[32,1]{1,0:T(8,128)S(1)} %fusion.4.before_ref.fitting_ref), custom_call_target="tpu_custom_call" | custom-call | tf_op jit(solution)/shard_map/pallas_call | solution.py:25
  104.4 0.1 reduce
  104.5 10.1 %all-to-all-done.1 = f32[32,1,128]{2,1,0:T(1,128)S(1)} async-done(((f32[32,1,128]{2,1,0:T(1,128)}), f32[32,1,128]{2,1,0:T(1,128)S(1)}, u32[]{:S(2)}, u32[]{:S(2)}) %all-to-all-start.1) | async-done | bytes 16416 | tf_op jit(solution)/shard_map/all_to_all | solution.py:476
  114.6 0.1 multiply_reduce_fusion
  114.7 0.7 mul.24
  (2 shorter events, 0.0 us)
Async XLA Ops:
  0.6 18.5 %copy-start = (f32[4,7680]{1,0:T(4,128)S(1)}, f32[4,7680]{1,0:T(4,128)}, u32[]{:S(2)}) copy-start(f32[4,7680]{1,0:T(4,128)} %w_ref.1) | copy-start | bytes 368644
  3.1 18.9 %collective-permute-start = (bf16[144,5120]{1,0:T(8,128)(2,1)S(1)}, bf16[144,5120]{1,0:T(8,128)(2,1)S(1)}, u32[]{:S(2)}, u32[]{:S(2)}) collective-permute-start(bf16[144,5120]{1,0:T(8,128)(2,1)S(1)} %get-tuple-element.22), channel_id=1, source_target_pairs={{0,1},{1,0},{2,3},{3,2},{4,5},{5,4},{6,7},{7,6},{8,9},{9,8},{10,11... | collective-permute-start | bytes 4423688 | tf_op jit(solution)/shard_map/ppermute | solution.py:416
  23.4 17.4 %collective-permute-start.1 = (bf16[6,160,128]{2,1,0:T(8,128)(2,1)S(1)}, bf16[6,160,128]{2,1,0:T(8,128)(2,1)S(1)}, u32[]{:S(2)}, u32[]{:S(2)}) collective-permute-start(bf16[6,160,128]{2,1,0:T(8,128)(2,1)S(1)} %shard_map.52.after_ref.one_ref), channel_id=1, source_target_pairs={{0,2},{2,4},{4,6},{3,1},{5,3},{7,5},{8,10},{10,12},{12,14},{11,9},... | collective-permute-start | bytes 737288 | tf_op jit(solution)/shard_map/ppermute | solution.py:421
  27.9 36.3 %collective-permute-start.6 = (bf16[10,136,128]{2,1,0:T(8,128)(2,1)S(1)}, bf16[10,136,128]{2,1,0:T(8,128)(2,1)S(1)}, u32[]{:S(2)}, u32[]{:S(2)}) collective-permute-start(bf16[10,136,128]{2,1,0:T(8,128)(2,1)S(1)} %get-tuple-element.32), channel_id=1, source_target_pairs={{0,6},{7,1},{8,14},{15,9},{16,22},{23,17},{24,30},{31,25},{32,38},... | collective-permute-start | bytes 1044488 | tf_op jit(solution)/shard_map/ppermute | solution.py:439
  29.2 13.5 %collective-permute-start.2 = (bf16[4,160,128]{2,1,0:T(8,128)(2,1)S(1)}, bf16[4,160,128]{2,1,0:T(8,128)(2,1)S(1)}, u32[]{:S(2)}, u32[]{:S(2)}) collective-permute-start(bf16[4,160,128]{2,1,0:T(8,128)(2,1)S(1)} %get-tuple-element.24), channel_id=1, source_target_pairs={{0,2},{2,4},{4,6},{3,1},{5,3},{7,5},{8,10},{10,12},{12,14},{11,9},... | collective-permute-start | bytes 491528 | tf_op jit(solution)/shard_map/ppermute | solution.py:438
  41.4 22.8 %collective-permute-start.4 = (bf16[6,144,128]{2,1,0:T(8,128)(2,1)S(1)}, bf16[6,144,128]{2,1,0:T(8,128)(2,1)S(1)}, u32[]{:S(2)}, u32[]{:S(2)}) collective-permute-start(bf16[6,144,128]{2,1,0:T(8,128)(2,1)S(1)} %shard_map.57), channel_id=1, source_target_pairs={{2,4},{4,6},{3,1},{5,3},{10,12},{12,14},{11,9},{13,11},{18,20},{20... | collective-permute-start | bytes 663560 | tf_op jit(solution)/shard_map/ppermute | solution.py:442
  43.3 20.9 %collective-permute-start.5 = (bf16[4,144,128]{2,1,0:T(8,128)(2,1)S(1)}, bf16[4,144,128]{2,1,0:T(8,128)(2,1)S(1)}, u32[]{:S(2)}, u32[]{:S(2)}) collective-permute-start(bf16[4,144,128]{2,1,0:T(8,128)(2,1)S(1)} %shard_map.58), channel_id=1, source_target_pairs={{2,4},{4,6},{3,1},{5,3},{10,12},{12,14},{11,9},{13,11},{18,20},{20... | collective-permute-start | bytes 442376 | tf_op jit(solution)/shard_map/ppermute | solution.py:442
  45.1 7.3 %collective-permute-start.3 = (bf16[4,3840]{1,0:T(4,128)(2,1)S(1)}, bf16[4,3840]{1,0:T(4,128)(2,1)S(1)}, u32[]{:S(2)}, u32[]{:S(2)}) collective-permute-start(bf16[4,3840]{1,0:T(4,128)(2,1)S(1)} %shard_map.55), channel_id=1, source_target_pairs={{0,1},{1,0},{2,3},{3,2},{4,5},{5,4},{6,7},{7,6},{8,9},{9,8},{10,11... | collective-permute-start | bytes 92168 | tf_op jit(solution)/shard_map/ppermute | solution.py:450
  86.3 16.7 %collective-permute-start.7 = (bf16[128,1280]{1,0:T(8,128)(2,1)S(1)}, bf16[128,1280]{1,0:T(8,128)(2,1)S(1)}, u32[]{:S(2)}, u32[]{:S(2)}) collective-permute-start(bf16[128,1280]{1,0:T(8,128)(2,1)S(1)} %get-tuple-element.37), channel_id=1, source_target_pairs={{0,1},{1,0},{2,3},{3,2},{4,5},{5,4},{6,7},{7,6},{8,9},{9,8},{10,11... | collective-permute-start | bytes 983048 | tf_op jit(solution)/shard_map/ppermute | solution.py:477
  88.2 26.4 %all-to-all-start.1 = ((f32[32,1,128]{2,1,0:T(1,128)}), f32[32,1,128]{2,1,0:T(1,128)S(1)}, u32[]{:S(2)}, u32[]{:S(2)}) async-start(f32[32,1,128]{2,1,0:T(1,128)} %bitcast.7), calls=%async_computation.1 | async-start | bytes 32768 | tf_op jit(solution)/shard_map/all_to_all | solution.py:476

commit v7 on v6

--- a/solution.py
+++ b/solution.py
@@ -171,9 +171,12 @@
 
 
 def second_states_kernel(
-    scalars, keep_ref, received_ref, taps_ref, one_ref, after_ref, two_ref, wrap_ref, *scratch
+    scalars, keep_ref, received_ref, taps_ref, one_ref, after_ref, two_ref, *scratch
 ):
     states_kernel(scalars, keep_ref, received_ref, taps_ref, two_ref, *scratch, begin=one_ref.shape[0])
+
+
+def wrap_kernel(scalars, one_ref, two_ref, wrap_ref):
     for head in range(wrap_ref.shape[0]):
         message_ref, at = half_of(one_ref, two_ref, head)
         wrap_ref[head, 0:HEAD, :] = message_ref[at, 0:HEAD, :]
@@ -380,8 +383,7 @@
     send_ref[...] = grad_ref[pl.ds(pl.multiple_of((1 - core) * ROWS, ROWS), ROWS), :]
 
 
-def join_kernel(scalars, own_ref, other_ref, fitting_ref, out_ref, fitting_out_ref):
-    fitting_out_ref[...] = fitting_ref[...]
+def join_kernel(scalars, own_ref, other_ref, out_ref):
     width = own_ref.shape[1]
     for core, parts in enumerate(((own_ref, other_ref), (other_ref, own_ref))):
 
@@ -431,11 +433,11 @@
         ],
         padded, scalars, keep, received, taps, one,
     )
-    two, wrap = call(
-        second_states_kernel, [second, ((heads, HEAD + EDGE, HEAD), BF16)], buffers,
-        scalars, keep, received, taps, one, fold,
+    (two,) = call(
+        second_states_kernel, [second], buffers, scalars, keep, received, taps, one, fold
     )
     near_two = lax.ppermute(two, line, hops(1))
+    (wrap,) = call(wrap_kernel, [((heads, HEAD + EDGE, HEAD), BF16)], [], scalars, one, two)
     wrap = lax.ppermute(wrap, line, hops(3))
     onward = [pair for pair in hops(1) if pair not in ((0, 2), (2 * chips - 1, 2 * chips - 3))]
     far_one, far_two = (
@@ -475,9 +477,7 @@
     )
     rows = lax.all_to_all(rows, ("core", "zl", "zh"), 0, 0, tiled=True)
     other = lax.ppermute(sent, "core", swap)
-    grad, fitting = call(
-        join_kernel, [((ROWS, 2 * width), BF16), (fitting.shape, F32)], [], scalars, own, other, fitting
-    )
+    (grad,) = call(join_kernel, [((ROWS, 2 * width), BF16)], [], scalars, own, other)
     share = jnp.sum(rows * fitting, 0)[: TAPS * few].reshape(TAPS, few)
     return grad[None], share * (1.0 / (lax.axis_size("zl") * spread))
 

time: 116 us -> 109 us (0.940)
  waiting for transfers between devices: 31.4 us -> 27.6 us
  starting transfers between devices: 45.7 us -> 42 us
    all_to_all x1, starting transfers between devices: 14.8 us -> 10.1 us  [per_device(): rows = lax.all_to_all(rows, ('core', 'zl', 'zh'), 0, 0, tiled=True)]
    all_to_all x1, waiting for transfers between devices: 10.1 us -> 7.7 us  [per_device(): rows = lax.all_to_all(rows, ('core', 'zl', 'zh'), 0, 0, tiled=True)]
    pallas_call x12 -> x13, Pallas kernels: 17.7 us -> 18.2 us  [call(): pl.pallas_call(kernel, out_shape=[jax.ShapeDtypeStruct(s, t) for s, t in...]
  transfers between devices with their start and end apart: 9 -> 9, of which waited for: 5 -> 5; matrix products, arithmetic and copies ran while one was open for 0% -> 1% of each run, Pallas kernels for 9% -> 11%
where the time goes in v7:
time: 109 us; the launch traced here: 108 us
  starting transfers between devices  42 us (39%)
  waiting for transfers between devices  27.6 us (25%)
  Pallas kernels  18.2 us (17%)
  blocking collectives  18.2 us (17%)
  local copies, waits for them, and re-layouts  1.28 us (1%)
    pallas_call x13, Pallas kernels, call(): pl.pallas_call(kernel, out_shape=[jax.ShapeDtypeStruct(s, t) for s, t in...  18.2 us
    all_to_all x1, blocking collectives, per_device(): lax.all_to_all(rows, 'yx', 0, 0, tiled=True)  18.2 us
    ppermute x1, starting transfers between devices, per_device(): received = lax.ppermute(send, 'core', swap)  16 us
    all_to_all x1, starting transfers between devices, per_device(): rows = lax.all_to_all(rows, ('core', 'zl', 'zh'), 0, 0, tiled=True)  10.1 us
    ppermute x1, waiting for transfers between devices, per_device(): near_one = lax.ppermute(one, line, hops(1))  9.83 us
    all_to_all x1, waiting for transfers between devices, per_device(): rows = lax.all_to_all(rows, ('core', 'zl', 'zh'), 0, 0, tiled=True)  7.7 us
    ppermute x1, starting transfers between devices, per_device(): partner = lax.ppermute(partner, 'core', swap)  7.29 us
    ppermute x2, waiting for transfers between devices, per_device(): lax.ppermute(call(hand_on_kernel, [((near.shape[0], HEAD + 2 * EDGE, HEAD...  6.93 us
  transfers between devices with their start and end apart: 9, of which 5 were waited for; matrix products, arithmetic and copies ran while one was open for 1% of the time, Pallas kernels for 11%

profile of v7, /device:TPU:1, one launch (start us, length us, event | category | flops | bytes accessed | tf_op | source)
XLA Modules:
  0.0 108.4 jit_solution(7429706315947915147)
XLA Ops:
  0.6 0.0 copy-start
  0.7 0.1 pad_add_fusion.scalars
  0.8 2.3 %shard_map.50 = (bf16[128,5120]{1,0:T(8,128)(2,1)S(1)}, bf16[144,5120]{1,0:T(8,128)(2,1)S(1)}) custom-call(s32[2]{0:T(128)S(1)} %pad_add_fusion.scalars, bf16[128,7680]{1,0:T(8,128)(2,1)} %bitcast.9, bf16[128,2560]{1,0:T(8,128)(2,1)} %bitcast.11, f32[32,1]{1,0:T(8,128)S(1)} %fusion.4.before_ref), custom_call_target="tpu_custom_call" | custom-call | tf_op jit(solution)/shard_map/pallas_call | solution.py:25
  3.1 16.0 %collective-permute-start = (bf16[144,5120]{1,0:T(8,128)(2,1)S(1)}, bf16[144,5120]{1,0:T(8,128)(2,1)S(1)}, u32[]{:S(2)}, u32[]{:S(2)}) collective-permute-start(bf16[144,5120]{1,0:T(8,128)(2,1)S(1)} %get-tuple-element.18), channel_id=1, source_target_pairs={{0,1},{1,0},{2,3},{3,2},{4,5},{5,4},{6,7},{7,6},{8,9},{9,8},{10,11... | collective-permute-start | bytes 4423688 | tf_op jit(solution)/shard_map/ppermute | solution.py:418
  19.2 0.0 copy-done
  19.2 0.6 shard_map.51.taps_ref
  19.7 2.3 %collective-permute-done.received_ref = bf16[144,5120]{1,0:T(8,128)(2,1)S(1)} collective-permute-done((bf16[144,5120]{1,0:T(8,128)(2,1)S(1)}, bf16[144,5120]{1,0:T(8,128)(2,1)S(1)}, u32[]{:S(2)}, u32[]{:S(2)}) %collective-permute-start) | collective-permute-done | bytes 1474592 | tf_op jit(solution)/shard_map/ppermute | solution.py:418
  22.0 1.4 %shard_map.52.after_ref.one_ref = bf16[6,160,128]{2,1,0:T(8,128)(2,1)S(1)} custom-call(s32[2]{0:T(128)S(1)} %pad_add_fusion.scalars, bf16[128,5120]{1,0:T(8,128)(2,1)S(1)} %get-tuple-element.17.keep_ref, bf16[144,5120]{1,0:T(8,128)(2,1)S(1)} %collective-permute-done.received_ref, f32[4,5120]{1,0:T(4,128)S(1)} %shard_map.51.taps_ref), custom_call_target="tpu_custom_call" | custom-call | tf_op jit(solution)/shard_map/pallas_call | solution.py:25
  23.4 1.3 %collective-permute-start.1 = (bf16[6,160,128]{2,1,0:T(8,128)(2,1)S(1)}, bf16[6,160,128]{2,1,0:T(8,128)(2,1)S(1)}, u32[]{:S(2)}, u32[]{:S(2)}) collective-permute-start(bf16[6,160,128]{2,1,0:T(8,128)(2,1)S(1)} %shard_map.52.after_ref.one_ref), channel_id=1, source_target_pairs={{0,2},{2,4},{4,6},{3,1},{5,3},{7,5},{8,10},{10,12},{12,14},{11,9},... | collective-permute-start | bytes 737288 | tf_op jit(solution)/shard_map/ppermute | solution.py:423
  24.7 1.9 %shard_map.53 = (f32[10,4,128,128]{3,2,1,0:T(8,128)S(1)}, bf16[640,256]{1,0:T(8,128)(2,1)S(1)}, f32[32,640]{1,0:T(8,128)S(1)}) custom-call(s32[2]{0:T(128)S(1)} %pad_add_fusion.scalars, bf16[128,5120]{1,0:T(8,128)(2,1)S(1)} %get-tuple-element.17.keep_ref, bf16[144,5120]{1,0:T(8,128)(2,1)S(1)} %collective-permute-done.received_ref, ...), custom_call_target="tpu_custom_call" | custom-call | tf_op jit(solution)/shard_map/pallas_call | solution.py:25
  26.7 1.2 %shard_map.54.two_ref = bf16[4,160,128]{2,1,0:T(8,128)(2,1)S(1)} custom-call(s32[2]{0:T(128)S(1)} %pad_add_fusion.scalars, bf16[128,5120]{1,0:T(8,128)(2,1)S(1)} %get-tuple-element.17.keep_ref, bf16[144,5120]{1,0:T(8,128)(2,1)S(1)} %collective-permute-done.received_ref, f32[4,5120]{1,0:T(4,128)S(1)} %shard_map.51.taps_ref, ...), custom_call_target="tpu_custom_call" | custom-call | tf_op jit(solution)/shard_map/pallas_call | solution.py:25
  27.9 0.6 shard_map.59
  28.4 1.3 %collective-permute-start.6 = (bf16[10,136,128]{2,1,0:T(8,128)(2,1)S(1)}, bf16[10,136,128]{2,1,0:T(8,128)(2,1)S(1)}, u32[]{:S(2)}, u32[]{:S(2)}) collective-permute-start(bf16[10,136,128]{2,1,0:T(8,128)(2,1)S(1)} %shard_map.59), channel_id=1, source_target_pairs={{0,6},{7,1},{8,14},{15,9},{16,22},{23,17},{24,30},{31,25},{32,38},... | collective-permute-start | bytes 1044488 | tf_op jit(solution)/shard_map/ppermute | solution.py:441
  29.7 1.3 %collective-permute-start.2 = (bf16[4,160,128]{2,1,0:T(8,128)(2,1)S(1)}, bf16[4,160,128]{2,1,0:T(8,128)(2,1)S(1)}, u32[]{:S(2)}, u32[]{:S(2)}) collective-permute-start(bf16[4,160,128]{2,1,0:T(8,128)(2,1)S(1)} %shard_map.54.two_ref), channel_id=1, source_target_pairs={{0,2},{2,4},{4,6},{3,1},{5,3},{7,5},{8,10},{10,12},{12,14},{11,9},... | collective-permute-start | bytes 491528 | tf_op jit(solution)/shard_map/ppermute | solution.py:439
  31.0 9.8 %collective-permute-done.1.near_one_ref.message_ref = bf16[6,160,128]{2,1,0:T(8,128)(2,1)S(1)} collective-permute-done((bf16[6,160,128]{2,1,0:T(8,128)(2,1)S(1)}, bf16[6,160,128]{2,1,0:T(8,128)(2,1)S(1)}, u32[]{:S(2)}, u32[]{:S(2)}) %collective-permute-start.1) | collective-permute-done | bytes 245792 | tf_op jit(solution)/shard_map/ppermute | solution.py:423
  40.9 0.6 shard_map.57
  41.4 1.3 %collective-permute-start.4 = (bf16[6,144,128]{2,1,0:T(8,128)(2,1)S(1)}, bf16[6,144,128]{2,1,0:T(8,128)(2,1)S(1)}, u32[]{:S(2)}, u32[]{:S(2)}) collective-permute-start(bf16[6,144,128]{2,1,0:T(8,128)(2,1)S(1)} %shard_map.57), channel_id=1, source_target_pairs={{2,4},{4,6},{3,1},{5,3},{10,12},{12,14},{11,9},{13,11},{18,20},{20... | collective-permute-start | bytes 663560 | tf_op jit(solution)/shard_map/ppermute | solution.py:444
  42.7 0.0 collective-permute-done.2.near_two_ref.message_ref
  42.7 0.6 shard_map.58
  43.3 1.3 %collective-permute-start.5 = (bf16[4,144,128]{2,1,0:T(8,128)(2,1)S(1)}, bf16[4,144,128]{2,1,0:T(8,128)(2,1)S(1)}, u32[]{:S(2)}, u32[]{:S(2)}) collective-permute-start(bf16[4,144,128]{2,1,0:T(8,128)(2,1)S(1)} %shard_map.58), channel_id=1, source_target_pairs={{2,4},{4,6},{3,1},{5,3},{10,12},{12,14},{11,9},{13,11},{18,20},{20... | collective-permute-start | bytes 442376 | tf_op jit(solution)/shard_map/ppermute | solution.py:444
  44.6 0.6 shard_map.55
  45.2 7.3 %collective-permute-start.3 = (bf16[4,3840]{1,0:T(4,128)(2,1)S(1)}, bf16[4,3840]{1,0:T(4,128)(2,1)S(1)}, u32[]{:S(2)}, u32[]{:S(2)}) collective-permute-start(bf16[4,3840]{1,0:T(4,128)(2,1)S(1)} %shard_map.55), channel_id=1, source_target_pairs={{0,1},{1,0},{2,3},{3,2},{4,5},{5,4},{6,7},{7,6},{8,9},{9,8},{10,11... | collective-permute-start | bytes 92168 | tf_op jit(solution)/shard_map/ppermute | solution.py:452
  52.5 0.8 collective-permute-done.3.other_ref
  53.3 3.9 %shard_map.56 = (f32[272,1280]{1,0:T(8,128)S(1)}, bf16[272,1280]{1,0:T(8,128)(2,1)S(1)}, bf16[16,1280]{1,0:T(8,128)(2,1)S(1)}, bf16[16,1280]{1,0:T(8,128)(2,1)S(...) custom-call(s32[2]{0:T(128)S(1)} %pad_add_fusion.scalars, bf16[128,5120]{1,0:T(8,128)(2,1)S(1)} %get-tuple-element.17.keep_ref, ...), custom_call_target="tpu_custom_call" | custom-call | tf_op jit(solution)/shard_map/pallas_call | solution.py:25
  57.2 6.9 %collective-permute-done.5.far_two_ref = bf16[4,144,128]{2,1,0:T(8,128)(2,1)S(1)} collective-permute-done((bf16[4,144,128]{2,1,0:T(8,128)(2,1)S(1)}, bf16[4,144,128]{2,1,0:T(8,128)(2,1)S(1)}, u32[]{:S(2)}, u32[]{:S(2)}) %collective-permute-start.5) | collective-permute-done | bytes 147488 | tf_op jit(solution)/shard_map/ppermute | solution.py:444
  64.1 0.0 collective-permute-done.6.wrap_ref
  64.1 0.0 collective-permute-done.4.far_one_ref
  64.1 1.5 %shard_map.60 = (bf16[10,128,128]{2,1,0:T(8,128)(2,1)S(1)}, f32[32,1,256]{2,1,0:T(1,128)S(1)}) custom-call(s32[2]{0:T(128)S(1)} %pad_add_fusion.scalars, f32[4,1280]{1,0:T(4,128)S(1)} %get-tuple-element.22.terms_ref, f32[10,4,128,128]{3,2,1,0:T(8,128)S(1)} %get-tuple-element.23.products_ref, bf16[272,1280]{1,0:T(8,128)(2,1)S(1)} %get-tuple-element.21.a_ref, ...), custom_call_target="tpu_custom_call" | custom-call | tf_op jit(solution)/shard_map/pallas_call | solution.py:25
  65.6 18.2 %all_to_all.17 = f32[32,1,256]{2,1,0:T(1,128)S(1)} all-to-all(f32[32,1,256]{2,1,0:T(1,128)S(1)} %get-tuple-element.29), channel_id=1, replica_groups=mesh['zl'=4,'yx'=32,'zh'=4,'core'=2] {'yx'}, dimensions={0} | all-to-all | bytes 65536 | tf_op jit(solution)/shard_map/all_to_all | solution.py:471
  83.8 0.1 reduce_sum.18
  83.9 0.6 broadcast_in_dim.12
  84.5 10.1 %all-to-all-start.1 = ((f32[32,1,128]{2,1,0:T(1,128)}), f32[32,1,128]{2,1,0:T(1,128)S(1)}, u32[]{:S(2)}, u32[]{:S(2)}) async-start(f32[32,1,128]{2,1,0:T(1,128)} %bitcast.7), calls=%async_computation.1 | async-start | bytes 32768 | tf_op jit(solution)/shard_map/all_to_all | solution.py:478
  94.5 1.8 %shard_map.61 = (bf16[128,1280]{1,0:T(8,128)(2,1)S(1)}, bf16[128,1280]{1,0:T(8,128)(2,1)S(1)}) custom-call(s32[2]{0:T(128)S(1)} %pad_add_fusion.scalars, f32[272,1280]{1,0:T(8,128)S(1)} %get-tuple-element.20.inside_ref, bf16[272,1280]{1,0:T(8,128)(2,1)S(1)} %get-tuple-element.21.a_ref, bf16[10,128,128]{2,1,0:T(8,128)(2,1)S(1)} %get-tuple-element.28.states_ref, ...), custom_call_target="tpu_custom_call" | custom-call | tf_op jit(solution)/shard_map/pallas_call | solution.py:25
  96.3 2.1 %collective-permute-start.7 = (bf16[128,1280]{1,0:T(8,128)(2,1)S(1)}, bf16[128,1280]{1,0:T(8,128)(2,1)S(1)}, u32[]{:S(2)}, u32[]{:S(2)}) collective-permute-start(bf16[128,1280]{1,0:T(8,128)(2,1)S(1)} %get-tuple-element.31), channel_id=1, source_target_pairs={{0,1},{1,0},{2,3},{3,2},{4,5},{5,4},{6,7},{7,6},{8,9},{9,8},{10,11... | collective-permute-start | bytes 983048 | tf_op jit(solution)/shard_map/ppermute | solution.py:479
  98.5 7.7 %all-to-all-done.1 = f32[32,1,128]{2,1,0:T(1,128)S(1)} async-done(((f32[32,1,128]{2,1,0:T(1,128)}), f32[32,1,128]{2,1,0:T(1,128)S(1)}, u32[]{:S(2)}, u32[]{:S(2)}) %all-to-all-start.1) | async-done | bytes 16416 | tf_op jit(solution)/shard_map/all_to_all | solution.py:478
  106.2 0.1 multiply_reduce_fusion
  106.3 0.7 mul.21
  106.9 0.0 collective-permute-done.7.other_ref
  106.9 1.4 %shard_map.62 = bf16[128,2560]{1,0:T(8,128)(2,1)} custom-call(s32[2]{0:T(128)S(1)} %pad_add_fusion.scalars, bf16[128,1280]{1,0:T(8,128)(2,1)S(1)} %get-tuple-element.30.own_ref, bf16[128,1280]{1,0:T(8,128)(2,1)S(1)} %collective-permute-done.7.other_ref), custom_call_target="tpu_custom_call" | custom-call | tf_op jit(solution)/shard_map/pallas_call | solution.py:25
  (3 shorter events, 0.0 us)
Async XLA Ops:
  0.6 18.5 %copy-start = (f32[4,7680]{1,0:T(4,128)S(1)}, f32[4,7680]{1,0:T(4,128)}, u32[]{:S(2)}) copy-start(f32[4,7680]{1,0:T(4,128)} %w_ref.1) | copy-start | bytes 368644
  3.1 18.9 %collective-permute-start = (bf16[144,5120]{1,0:T(8,128)(2,1)S(1)}, bf16[144,5120]{1,0:T(8,128)(2,1)S(1)}, u32[]{:S(2)}, u32[]{:S(2)}) collective-permute-start(bf16[144,5120]{1,0:T(8,128)(2,1)S(1)} %get-tuple-element.18), channel_id=1, source_target_pairs={{0,1},{1,0},{2,3},{3,2},{4,5},{5,4},{6,7},{7,6},{8,9},{9,8},{10,11... | collective-permute-start | bytes 4423688 | tf_op jit(solution)/shard_map/ppermute | solution.py:418
  23.4 17.5 %collective-permute-start.1 = (bf16[6,160,128]{2,1,0:T(8,128)(2,1)S(1)}, bf16[6,160,128]{2,1,0:T(8,128)(2,1)S(1)}, u32[]{:S(2)}, u32[]{:S(2)}) collective-permute-start(bf16[6,160,128]{2,1,0:T(8,128)(2,1)S(1)} %shard_map.52.after_ref.one_ref), channel_id=1, source_target_pairs={{0,2},{2,4},{4,6},{3,1},{5,3},{7,5},{8,10},{10,12},{12,14},{11,9},... | collective-permute-start | bytes 737288 | tf_op jit(solution)/shard_map/ppermute | solution.py:423
  28.4 35.7 %collective-permute-start.6 = (bf16[10,136,128]{2,1,0:T(8,128)(2,1)S(1)}, bf16[10,136,128]{2,1,0:T(8,128)(2,1)S(1)}, u32[]{:S(2)}, u32[]{:S(2)}) collective-permute-start(bf16[10,136,128]{2,1,0:T(8,128)(2,1)S(1)} %shard_map.59), channel_id=1, source_target_pairs={{0,6},{7,1},{8,14},{15,9},{16,22},{23,17},{24,30},{31,25},{32,38},... | collective-permute-start | bytes 1044488 | tf_op jit(solution)/shard_map/ppermute | solution.py:441
  29.7 13.0 %collective-permute-start.2 = (bf16[4,160,128]{2,1,0:T(8,128)(2,1)S(1)}, bf16[4,160,128]{2,1,0:T(8,128)(2,1)S(1)}, u32[]{:S(2)}, u32[]{:S(2)}) collective-permute-start(bf16[4,160,128]{2,1,0:T(8,128)(2,1)S(1)} %shard_map.54.two_ref), channel_id=1, source_target_pairs={{0,2},{2,4},{4,6},{3,1},{5,3},{7,5},{8,10},{10,12},{12,14},{11,9},... | collective-permute-start | bytes 491528 | tf_op jit(solution)/shard_map/ppermute | solution.py:439
  41.4 22.7 %collective-permute-start.4 = (bf16[6,144,128]{2,1,0:T(8,128)(2,1)S(1)}, bf16[6,144,128]{2,1,0:T(8,128)(2,1)S(1)}, u32[]{:S(2)}, u32[]{:S(2)}) collective-permute-start(bf16[6,144,128]{2,1,0:T(8,128)(2,1)S(1)} %shard_map.57), channel_id=1, source_target_pairs={{2,4},{4,6},{3,1},{5,3},{10,12},{12,14},{11,9},{13,11},{18,20},{20... | collective-permute-start | bytes 663560 | tf_op jit(solution)/shard_map/ppermute | solution.py:444
  43.3 20.8 %collective-permute-start.5 = (bf16[4,144,128]{2,1,0:T(8,128)(2,1)S(1)}, bf16[4,144,128]{2,1,0:T(8,128)(2,1)S(1)}, u32[]{:S(2)}, u32[]{:S(2)}) collective-permute-start(bf16[4,144,128]{2,1,0:T(8,128)(2,1)S(1)} %shard_map.58), channel_id=1, source_target_pairs={{2,4},{4,6},{3,1},{5,3},{10,12},{12,14},{11,9},{13,11},{18,20},{20... | collective-permute-start | bytes 442376 | tf_op jit(solution)/shard_map/ppermute | solution.py:444
  45.2 8.1 %collective-permute-start.3 = (bf16[4,3840]{1,0:T(4,128)(2,1)S(1)}, bf16[4,3840]{1,0:T(4,128)(2,1)S(1)}, u32[]{:S(2)}, u32[]{:S(2)}) collective-permute-start(bf16[4,3840]{1,0:T(4,128)(2,1)S(1)} %shard_map.55), channel_id=1, source_target_pairs={{0,1},{1,0},{2,3},{3,2},{4,5},{5,4},{6,7},{7,6},{8,9},{9,8},{10,11... | collective-permute-start | bytes 92168 | tf_op jit(solution)/shard_map/ppermute | solution.py:452
  84.5 21.7 %all-to-all-start.1 = ((f32[32,1,128]{2,1,0:T(1,128)}), f32[32,1,128]{2,1,0:T(1,128)S(1)}, u32[]{:S(2)}, u32[]{:S(2)}) async-start(f32[32,1,128]{2,1,0:T(1,128)} %bitcast.7), calls=%async_computation.1 | async-start | bytes 32768 | tf_op jit(solution)/shard_map/all_to_all | solution.py:478
  96.3 10.6 %collective-permute-start.7 = (bf16[128,1280]{1,0:T(8,128)(2,1)S(1)}, bf16[128,1280]{1,0:T(8,128)(2,1)S(1)}, u32[]{:S(2)}, u32[]{:S(2)}) collective-permute-start(bf16[128,1280]{1,0:T(8,128)(2,1)S(1)} %get-tuple-element.31), channel_id=1, source_target_pairs={{0,1},{1,0},{2,3},{3,2},{4,5},{5,4},{6,7},{7,6},{8,9},{9,8},{10,11... | collective-permute-start | bytes 983048 | tf_op jit(solution)/shard_map/ppermute | solution.py:479

commit v8 on v7

--- a/solution.py
+++ b/solution.py
@@ -171,7 +171,7 @@
 
 
 def second_states_kernel(
-    scalars, keep_ref, received_ref, taps_ref, one_ref, after_ref, two_ref, *scratch
+    scalars, keep_ref, received_ref, taps_ref, one_ref, two_ref, *scratch
 ):
     states_kernel(scalars, keep_ref, received_ref, taps_ref, two_ref, *scratch, begin=one_ref.shape[0])
 
@@ -434,7 +434,7 @@
         padded, scalars, keep, received, taps, one,
     )
     (two,) = call(
-        second_states_kernel, [second], buffers, scalars, keep, received, taps, one, fold
+        second_states_kernel, [second], buffers, scalars, keep, received, taps, one
     )
     near_two = lax.ppermute(two, line, hops(1))
     (wrap,) = call(wrap_kernel, [((heads, HEAD + EDGE, HEAD), BF16)], [], scalars, one, two)

time: 109 us -> 115 us (1.055)
  waiting for transfers between devices: 27.6 us -> 33 us
    all_to_all x1, starting transfers between devices: 10.1 us -> 16.4 us  [per_device(): rows = lax.all_to_all(rows, ('core', 'zl', 'zh'), 0, 0, tiled=True)]
    ppermute x1, starting transfers between devices: 7.29 us -> 1.92 us  [per_device(): partner = lax.ppermute(partner, 'core', swap)]
    ppermute x2, waiting for transfers between devices: 6.93 us -> 11.9 us  [per_device(): lax.ppermute(call(hand_on_kernel, [((near.shape[0], HEAD + 2 * EDGE, HEAD...]
  transfers between devices with their start and end apart: 9 -> 9, of which waited for: 5 -> 5; matrix products, arithmetic and copies ran while one was open for 1% -> 1% of each run, Pallas kernels for 11% -> 10%
where the time goes in v8:
time: 115 us
  starting transfers between devices  42.9 us (37%)
  waiting for transfers between devices  33 us (29%)
  Pallas kernels  18.2 us (16%)
  blocking collectives  18.1 us (16%)
  local copies, waits for them, and re-layouts  1.28 us (1%)
    pallas_call x13, Pallas kernels, call(): pl.pallas_call(kernel, out_shape=[jax.ShapeDtypeStruct(s, t) for s, t in...  18.2 us
    all_to_all x1, blocking collectives, per_device(): lax.all_to_all(rows, 'yx', 0, 0, tiled=True)  18.1 us
    all_to_all x1, starting transfers between devices, per_device(): rows = lax.all_to_all(rows, ('core', 'zl', 'zh'), 0, 0, tiled=True)  16.4 us
    ppermute x1, starting transfers between devices, per_device(): received = lax.ppermute(send, 'core', swap)  16 us
    ppermute x2, waiting for transfers between devices, per_device(): lax.ppermute(call(hand_on_kernel, [((near.shape[0], HEAD + 2 * EDGE, HEAD...  11.9 us
    ppermute x1, waiting for transfers between devices, per_device(): near_one = lax.ppermute(one, line, hops(1))  9.98 us
    all_to_all x1, waiting for transfers between devices, per_device(): rows = lax.all_to_all(rows, ('core', 'zl', 'zh'), 0, 0, tiled=True)  7.7 us
    ppermute x2, starting transfers between devices, per_device(): lax.ppermute(call(hand_on_kernel, [((near.shape[0], HEAD + 2 * EDGE, HEAD...  2.58 us
  transfers between devices with their start and end apart: 9, of which 5 were waited for; matrix products, arithmetic and copies ran while one was open for 1% of the time, Pallas kernels for 10%

profile of v8, /device:TPU:1, one launch (start us, length us, event | category | flops | bytes accessed | tf_op | source)
XLA Modules:
  0.0 114.6 jit_solution(16156242466265613313)
XLA Ops:
  0.6 0.0 copy-start
  0.7 0.1 pad_add_fusion.scalars
  0.8 2.3 %shard_map.50 = (bf16[128,5120]{1,0:T(8,128)(2,1)S(1)}, bf16[144,5120]{1,0:T(8,128)(2,1)S(1)}) custom-call(s32[2]{0:T(128)S(1)} %pad_add_fusion.scalars, bf16[128,7680]{1,0:T(8,128)(2,1)} %bitcast.9, bf16[128,2560]{1,0:T(8,128)(2,1)} %bitcast.11, f32[32,1]{1,0:T(8,128)S(1)} %fusion.4.before_ref), custom_call_target="tpu_custom_call" | custom-call | tf_op jit(solution)/shard_map/pallas_call | solution.py:25
  3.1 16.0 %collective-permute-start = (bf16[144,5120]{1,0:T(8,128)(2,1)S(1)}, bf16[144,5120]{1,0:T(8,128)(2,1)S(1)}, u32[]{:S(2)}, u32[]{:S(2)}) collective-permute-start(bf16[144,5120]{1,0:T(8,128)(2,1)S(1)} %get-tuple-element.18), channel_id=1, source_target_pairs={{0,1},{1,0},{2,3},{3,2},{4,5},{5,4},{6,7},{7,6},{8,9},{9,8},{10,11... | collective-permute-start | bytes 4423688 | tf_op jit(solution)/shard_map/ppermute | solution.py:418
  19.2 0.0 copy-done
  19.2 0.6 shard_map.51.taps_ref
  19.7 2.3 %collective-permute-done.received_ref = bf16[144,5120]{1,0:T(8,128)(2,1)S(1)} collective-permute-done((bf16[144,5120]{1,0:T(8,128)(2,1)S(1)}, bf16[144,5120]{1,0:T(8,128)(2,1)S(1)}, u32[]{:S(2)}, u32[]{:S(2)}) %collective-permute-start) | collective-permute-done | bytes 1474592 | tf_op jit(solution)/shard_map/ppermute | solution.py:418
  22.0 1.4 %shard_map.52.one_ref.after_ref = bf16[6,160,128]{2,1,0:T(8,128)(2,1)S(1)} custom-call(s32[2]{0:T(128)S(1)} %pad_add_fusion.scalars, bf16[128,5120]{1,0:T(8,128)(2,1)S(1)} %get-tuple-element.17.keep_ref, bf16[144,5120]{1,0:T(8,128)(2,1)S(1)} %collective-permute-done.received_ref, f32[4,5120]{1,0:T(4,128)S(1)} %shard_map.51.taps_ref), custom_call_target="tpu_custom_call" | custom-call | tf_op jit(solution)/shard_map/pallas_call | solution.py:25
  23.4 1.3 %collective-permute-start.1 = (bf16[6,160,128]{2,1,0:T(8,128)(2,1)S(1)}, bf16[6,160,128]{2,1,0:T(8,128)(2,1)S(1)}, u32[]{:S(2)}, u32[]{:S(2)}) collective-permute-start(bf16[6,160,128]{2,1,0:T(8,128)(2,1)S(1)} %shard_map.52.one_ref.after_ref), channel_id=1, source_target_pairs={{0,2},{2,4},{4,6},{3,1},{5,3},{7,5},{8,10},{10,12},{12,14},{11,9},... | collective-permute-start | bytes 737288 | tf_op jit(solution)/shard_map/ppermute | solution.py:423
  24.7 1.2 %shard_map.53.two_ref = bf16[4,160,128]{2,1,0:T(8,128)(2,1)S(1)} custom-call(s32[2]{0:T(128)S(1)} %pad_add_fusion.scalars, bf16[128,5120]{1,0:T(8,128)(2,1)S(1)} %get-tuple-element.17.keep_ref, bf16[144,5120]{1,0:T(8,128)(2,1)S(1)} %collective-permute-done.received_ref, f32[4,5120]{1,0:T(4,128)S(1)} %shard_map.51.taps_ref, ...), custom_call_target="tpu_custom_call" | custom-call | tf_op jit(solution)/shard_map/pallas_call | solution.py:25
  25.9 0.6 shard_map.59
  26.5 1.3 %collective-permute-start.6 = (bf16[10,136,128]{2,1,0:T(8,128)(2,1)S(1)}, bf16[10,136,128]{2,1,0:T(8,128)(2,1)S(1)}, u32[]{:S(2)}, u32[]{:S(2)}) collective-permute-start(bf16[10,136,128]{2,1,0:T(8,128)(2,1)S(1)} %shard_map.59), channel_id=1, source_target_pairs={{0,6},{7,1},{8,14},{15,9},{16,22},{23,17},{24,30},{31,25},{32,38},... | collective-permute-start | bytes 1044488 | tf_op jit(solution)/shard_map/ppermute | solution.py:441
  27.8 1.3 %collective-permute-start.2 = (bf16[4,160,128]{2,1,0:T(8,128)(2,1)S(1)}, bf16[4,160,128]{2,1,0:T(8,128)(2,1)S(1)}, u32[]{:S(2)}, u32[]{:S(2)}) collective-permute-start(bf16[4,160,128]{2,1,0:T(8,128)(2,1)S(1)} %shard_map.53.two_ref), channel_id=1, source_target_pairs={{0,2},{2,4},{4,6},{3,1},{5,3},{7,5},{8,10},{10,12},{12,14},{11,9},... | collective-permute-start | bytes 491528 | tf_op jit(solution)/shard_map/ppermute | solution.py:439
  29.1 1.9 %shard_map.56 = (f32[10,4,128,128]{3,2,1,0:T(8,128)S(1)}, bf16[640,256]{1,0:T(8,128)(2,1)S(1)}, f32[32,640]{1,0:T(8,128)S(1)}) custom-call(s32[2]{0:T(128)S(1)} %pad_add_fusion.scalars, bf16[128,5120]{1,0:T(8,128)(2,1)S(1)} %get-tuple-element.17.keep_ref, bf16[144,5120]{1,0:T(8,128)(2,1)S(1)} %collective-permute-done.received_ref, ...), custom_call_target="tpu_custom_call" | custom-call | tf_op jit(solution)/shard_map/pallas_call | solution.py:25
  31.0 10.0 %collective-permute-done.1.near_one_ref.message_ref = bf16[6,160,128]{2,1,0:T(8,128)(2,1)S(1)} collective-permute-done((bf16[6,160,128]{2,1,0:T(8,128)(2,1)S(1)}, bf16[6,160,128]{2,1,0:T(8,128)(2,1)S(1)}, u32[]{:S(2)}, u32[]{:S(2)}) %collective-permute-start.1) | collective-permute-done | bytes 245792 | tf_op jit(solution)/shard_map/ppermute | solution.py:423
  41.0 0.6 shard_map.57
  41.6 1.3 %collective-permute-start.4 = (bf16[6,144,128]{2,1,0:T(8,128)(2,1)S(1)}, bf16[6,144,128]{2,1,0:T(8,128)(2,1)S(1)}, u32[]{:S(2)}, u32[]{:S(2)}) collective-permute-start(bf16[6,144,128]{2,1,0:T(8,128)(2,1)S(1)} %shard_map.57), channel_id=1, source_target_pairs={{2,4},{4,6},{3,1},{5,3},{10,12},{12,14},{11,9},{13,11},{18,20},{20... | collective-permute-start | bytes 663560 | tf_op jit(solution)/shard_map/ppermute | solution.py:444
  42.9 0.0 collective-permute-done.2.near_two_ref.message_ref
  42.9 0.6 shard_map.58
  43.5 1.3 %collective-permute-start.5 = (bf16[4,144,128]{2,1,0:T(8,128)(2,1)S(1)}, bf16[4,144,128]{2,1,0:T(8,128)(2,1)S(1)}, u32[]{:S(2)}, u32[]{:S(2)}) collective-permute-start(bf16[4,144,128]{2,1,0:T(8,128)(2,1)S(1)} %shard_map.58), channel_id=1, source_target_pairs={{2,4},{4,6},{3,1},{5,3},{10,12},{12,14},{11,9},{13,11},{18,20},{20... | collective-permute-start | bytes 442376 | tf_op jit(solution)/shard_map/ppermute | solution.py:444
  44.8 0.6 shard_map.54
  45.3 1.9 %collective-permute-start.3 = (bf16[4,3840]{1,0:T(4,128)(2,1)S(1)}, bf16[4,3840]{1,0:T(4,128)(2,1)S(1)}, u32[]{:S(2)}, u32[]{:S(2)}) collective-permute-start(bf16[4,3840]{1,0:T(4,128)(2,1)S(1)} %shard_map.54), channel_id=1, source_target_pairs={{0,1},{1,0},{2,3},{3,2},{4,5},{5,4},{6,7},{7,6},{8,9},{9,8},{10,11... | collective-permute-start | bytes 92168 | tf_op jit(solution)/shard_map/ppermute | solution.py:452
  47.2 1.2 %collective-permute-done.3.other_ref = bf16[4,3840]{1,0:T(4,128)(2,1)S(1)} collective-permute-done((bf16[4,3840]{1,0:T(4,128)(2,1)S(1)}, bf16[4,3840]{1,0:T(4,128)(2,1)S(1)}, u32[]{:S(2)}, u32[]{:S(2)}) %collective-permute-start.3) | collective-permute-done | bytes 30752 | tf_op jit(solution)/shard_map/ppermute | solution.py:452
  48.4 3.9 %shard_map.55 = (f32[272,1280]{1,0:T(8,128)S(1)}, bf16[272,1280]{1,0:T(8,128)(2,1)S(1)}, bf16[16,1280]{1,0:T(8,128)(2,1)S(1)}, bf16[16,1280]{1,0:T(8,128)(2,1)S(...) custom-call(s32[2]{0:T(128)S(1)} %pad_add_fusion.scalars, bf16[128,5120]{1,0:T(8,128)(2,1)S(1)} %get-tuple-element.17.keep_ref, ...), custom_call_target="tpu_custom_call" | custom-call | tf_op jit(solution)/shard_map/pallas_call | solution.py:25
  52.3 11.9 %collective-permute-done.5.far_two_ref = bf16[4,144,128]{2,1,0:T(8,128)(2,1)S(1)} collective-permute-done((bf16[4,144,128]{2,1,0:T(8,128)(2,1)S(1)}, bf16[4,144,128]{2,1,0:T(8,128)(2,1)S(1)}, u32[]{:S(2)}, u32[]{:S(2)}) %collective-permute-start.5) | collective-permute-done | bytes 147488 | tf_op jit(solution)/shard_map/ppermute | solution.py:444
  64.1 0.0 collective-permute-done.6.wrap_ref
  64.1 0.0 collective-permute-done.4.far_one_ref
  64.2 1.5 %shard_map.60 = (bf16[10,128,128]{2,1,0:T(8,128)(2,1)S(1)}, f32[32,1,256]{2,1,0:T(1,128)S(1)}) custom-call(s32[2]{0:T(128)S(1)} %pad_add_fusion.scalars, f32[4,1280]{1,0:T(4,128)S(1)} %get-tuple-element.21.terms_ref, f32[10,4,128,128]{3,2,1,0:T(8,128)S(1)} %get-tuple-element.22.products_ref, bf16[272,1280]{1,0:T(8,128)(2,1)S(1)} %get-tuple-element.20.a_ref, ...), custom_call_target="tpu_custom_call" | custom-call | tf_op jit(solution)/shard_map/pallas_call | solution.py:25
  65.7 18.1 %all_to_all.17 = f32[32,1,256]{2,1,0:T(1,128)S(1)} all-to-all(f32[32,1,256]{2,1,0:T(1,128)S(1)} %get-tuple-element.29), channel_id=1, replica_groups=mesh['zl'=4,'yx'=32,'zh'=4,'core'=2] {'yx'}, dimensions={0} | all-to-all | bytes 65536 | tf_op jit(solution)/shard_map/all_to_all | solution.py:471
  83.8 0.1 reduce_sum.18
  83.8 0.6 broadcast_in_dim.12
  84.4 16.4 %all-to-all-start.1 = ((f32[32,1,128]{2,1,0:T(1,128)}), f32[32,1,128]{2,1,0:T(1,128)S(1)}, u32[]{:S(2)}, u32[]{:S(2)}) async-start(f32[32,1,128]{2,1,0:T(1,128)} %bitcast.7), calls=%async_computation.1 | async-start | bytes 32768 | tf_op jit(solution)/shard_map/all_to_all | solution.py:478
  100.8 1.8 %shard_map.61 = (bf16[128,1280]{1,0:T(8,128)(2,1)S(1)}, bf16[128,1280]{1,0:T(8,128)(2,1)S(1)}) custom-call(s32[2]{0:T(128)S(1)} %pad_add_fusion.scalars, f32[272,1280]{1,0:T(8,128)S(1)} %get-tuple-element.19.inside_ref, bf16[272,1280]{1,0:T(8,128)(2,1)S(1)} %get-tuple-element.20.a_ref, bf16[10,128,128]{2,1,0:T(8,128)(2,1)S(1)} %get-tuple-element.28.states_ref, ...), custom_call_target="tpu_custom_call" | custom-call | tf_op jit(solution)/shard_map/pallas_call | solution.py:25
  102.6 2.1 %collective-permute-start.7 = (bf16[128,1280]{1,0:T(8,128)(2,1)S(1)}, bf16[128,1280]{1,0:T(8,128)(2,1)S(1)}, u32[]{:S(2)}, u32[]{:S(2)}) collective-permute-start(bf16[128,1280]{1,0:T(8,128)(2,1)S(1)} %get-tuple-element.31), channel_id=1, source_target_pairs={{0,1},{1,0},{2,3},{3,2},{4,5},{5,4},{6,7},{7,6},{8,9},{9,8},{10,11... | collective-permute-start | bytes 983048 | tf_op jit(solution)/shard_map/ppermute | solution.py:479
  104.7 7.7 %all-to-all-done.1 = f32[32,1,128]{2,1,0:T(1,128)S(1)} async-done(((f32[32,1,128]{2,1,0:T(1,128)}), f32[32,1,128]{2,1,0:T(1,128)S(1)}, u32[]{:S(2)}, u32[]{:S(2)}) %all-to-all-start.1) | async-done | bytes 16416 | tf_op jit(solution)/shard_map/all_to_all | solution.py:478
  112.4 0.1 multiply_reduce_fusion
  112.5 0.7 mul.21
  113.2 0.0 collective-permute-done.7.other_ref
  113.2 1.4 %shard_map.62 = bf16[128,2560]{1,0:T(8,128)(2,1)} custom-call(s32[2]{0:T(128)S(1)} %pad_add_fusion.scalars, bf16[128,1280]{1,0:T(8,128)(2,1)S(1)} %get-tuple-element.30.own_ref, bf16[128,1280]{1,0:T(8,128)(2,1)S(1)} %collective-permute-done.7.other_ref), custom_call_target="tpu_custom_call" | custom-call | tf_op jit(solution)/shard_map/pallas_call | solution.py:25
  (3 shorter events, 0.0 us)
Async XLA Ops:
  0.6 18.5 %copy-start = (f32[4,7680]{1,0:T(4,128)S(1)}, f32[4,7680]{1,0:T(4,128)}, u32[]{:S(2)}) copy-start(f32[4,7680]{1,0:T(4,128)} %w_ref.1) | copy-start | bytes 368644
  3.1 18.9 %collective-permute-start = (bf16[144,5120]{1,0:T(8,128)(2,1)S(1)}, bf16[144,5120]{1,0:T(8,128)(2,1)S(1)}, u32[]{:S(2)}, u32[]{:S(2)}) collective-permute-start(bf16[144,5120]{1,0:T(8,128)(2,1)S(1)} %get-tuple-element.18), channel_id=1, source_target_pairs={{0,1},{1,0},{2,3},{3,2},{4,5},{5,4},{6,7},{7,6},{8,9},{9,8},{10,11... | collective-permute-start | bytes 4423688 | tf_op jit(solution)/shard_map/ppermute | solution.py:418
  23.4 17.6 %collective-permute-start.1 = (bf16[6,160,128]{2,1,0:T(8,128)(2,1)S(1)}, bf16[6,160,128]{2,1,0:T(8,128)(2,1)S(1)}, u32[]{:S(2)}, u32[]{:S(2)}) collective-permute-start(bf16[6,160,128]{2,1,0:T(8,128)(2,1)S(1)} %shard_map.52.one_ref.after_ref), channel_id=1, source_target_pairs={{0,2},{2,4},{4,6},{3,1},{5,3},{7,5},{8,10},{10,12},{12,14},{11,9},... | collective-permute-start | bytes 737288 | tf_op jit(solution)/shard_map/ppermute | solution.py:423
  26.5 37.7 %collective-permute-start.6 = (bf16[10,136,128]{2,1,0:T(8,128)(2,1)S(1)}, bf16[10,136,128]{2,1,0:T(8,128)(2,1)S(1)}, u32[]{:S(2)}, u32[]{:S(2)}) collective-permute-start(bf16[10,136,128]{2,1,0:T(8,128)(2,1)S(1)} %shard_map.59), channel_id=1, source_target_pairs={{0,6},{7,1},{8,14},{15,9},{16,22},{23,17},{24,30},{31,25},{32,38},... | collective-permute-start | bytes 1044488 | tf_op jit(solution)/shard_map/ppermute | solution.py:441
  27.8 15.1 %collective-permute-start.2 = (bf16[4,160,128]{2,1,0:T(8,128)(2,1)S(1)}, bf16[4,160,128]{2,1,0:T(8,128)(2,1)S(1)}, u32[]{:S(2)}, u32[]{:S(2)}) collective-permute-start(bf16[4,160,128]{2,1,0:T(8,128)(2,1)S(1)} %shard_map.53.two_ref), channel_id=1, source_target_pairs={{0,2},{2,4},{4,6},{3,1},{5,3},{7,5},{8,10},{10,12},{12,14},{11,9},... | collective-permute-start | bytes 491528 | tf_op jit(solution)/shard_map/ppermute | solution.py:439
  41.6 22.6 %collective-permute-start.4 = (bf16[6,144,128]{2,1,0:T(8,128)(2,1)S(1)}, bf16[6,144,128]{2,1,0:T(8,128)(2,1)S(1)}, u32[]{:S(2)}, u32[]{:S(2)}) collective-permute-start(bf16[6,144,128]{2,1,0:T(8,128)(2,1)S(1)} %shard_map.57), channel_id=1, source_target_pairs={{2,4},{4,6},{3,1},{5,3},{10,12},{12,14},{11,9},{13,11},{18,20},{20... | collective-permute-start | bytes 663560 | tf_op jit(solution)/shard_map/ppermute | solution.py:444
  43.5 20.7 %collective-permute-start.5 = (bf16[4,144,128]{2,1,0:T(8,128)(2,1)S(1)}, bf16[4,144,128]{2,1,0:T(8,128)(2,1)S(1)}, u32[]{:S(2)}, u32[]{:S(2)}) collective-permute-start(bf16[4,144,128]{2,1,0:T(8,128)(2,1)S(1)} %shard_map.58), channel_id=1, source_target_pairs={{2,4},{4,6},{3,1},{5,3},{10,12},{12,14},{11,9},{13,11},{18,20},{20... | collective-permute-start | bytes 442376 | tf_op jit(solution)/shard_map/ppermute | solution.py:444
  45.3 3.1 %collective-permute-start.3 = (bf16[4,3840]{1,0:T(4,128)(2,1)S(1)}, bf16[4,3840]{1,0:T(4,128)(2,1)S(1)}, u32[]{:S(2)}, u32[]{:S(2)}) collective-permute-start(bf16[4,3840]{1,0:T(4,128)(2,1)S(1)} %shard_map.54), channel_id=1, source_target_pairs={{0,1},{1,0},{2,3},{3,2},{4,5},{5,4},{6,7},{7,6},{8,9},{9,8},{10,11... | collective-permute-start | bytes 92168 | tf_op jit(solution)/shard_map/ppermute | solution.py:452
  84.4 28.0 %all-to-all-start.1 = ((f32[32,1,128]{2,1,0:T(1,128)}), f32[32,1,128]{2,1,0:T(1,128)S(1)}, u32[]{:S(2)}, u32[]{:S(2)}) async-start(f32[32,1,128]{2,1,0:T(1,128)} %bitcast.7), calls=%async_computation.1 | async-start | bytes 32768 | tf_op jit(solution)/shard_map/all_to_all | solution.py:478
  102.6 10.6 %collective-permute-start.7 = (bf16[128,1280]{1,0:T(8,128)(2,1)S(1)}, bf16[128,1280]{1,0:T(8,128)(2,1)S(1)}, u32[]{:S(2)}, u32[]{:S(2)}) collective-permute-start(bf16[128,1280]{1,0:T(8,128)(2,1)S(1)} %get-tuple-element.31), channel_id=1, source_target_pairs={{0,1},{1,0},{2,3},{3,2},{4,5},{5,4},{6,7},{7,6},{8,9},{9,8},{10,11... | collective-permute-start | bytes 983048 | tf_op jit(solution)/shard_map/ppermute | solution.py:479
